TPU v7x, 32 devices: a whole 2x2x4 slice. The times are simulated.
32 devices in a mesh: section: 16 (over z, x, core), dp: 2 (over y).
Axes of the slice: x: 2, y: 2, z: 4, core: 2. Of those that a mesh axis runs over, the one named last changes fastest.
Arguments:
- token_ids: int32 [2, 16, 2, 128], P('dp', 'section'), may hold values from 0 to 32127
- targets: int32 [2, 16, 128], P('dp', 'section'), may hold values from 0 to 32127
- objective: int32 [2, 16], P('dp', 'section'), may hold values from 0 to 1
- buckets: int32 [2, 255], replicated, may hold values from 0 to 31, as said below
- table: float32 [32128, 768], P('section')
- table_first: float32 [32128, 768], P('section'), may hold values from -0.00024414062 to 0.00024414062
- table_second: float32 [32128, 768], P('section'), may hold values from 1.2867396e-09 to 5.098402e-09
- inner_weight: float32 [2, 768, 3072], P(None, None, 'section'), may hold values from -0.21875 to 0.21875
- inner_first: float32 [2, 768, 3072], P(None, None, 'section'), may hold values from -0.00024414062 to 0.00024414062
- inner_second: float32 [2, 768, 3072], P(None, None, 'section'), may hold values from 1.2867396e-09 to 5.098402e-09
- outer_weight: float32 [2, 3072, 768], P(None, 'section'), may hold values from -0.109375 to 0.109375
- outer_first: float32 [2, 3072, 768], P(None, 'section'), may hold values from -0.00024414062 to 0.00024414062
- outer_second: float32 [2, 3072, 768], P(None, 'section'), may hold values from 1.2867396e-09 to 5.098402e-09
- gain_rows: float32 [7, 768], replicated, may hold values from 0.5 to 1.5
- gain_first: float32 [7, 768], replicated, may hold values from -0.0024414062 to 0.0024414062
- gain_second: float32 [7, 768], replicated, may hold values from 1.2867396e-07 to 5.098402e-07
- position_bias: float32 [2, 32, 12], replicated, may hold values from -4 to 4
- bias_first: float32 [2, 32, 12], replicated, may hold values from -0.0024414062 to 0.0024414062
- bias_second: float32 [2, 32, 12], replicated, may hold values from 1.2867396e-07 to 5.098402e-07
- attention: float32 [12, 768, 768], P(None, 'section'), may hold values from -0.21875 to 0.21875
- left_stats: float32 [12, 768, 768], P(None, 'section'), as said below
- right_stats: float32 [12, 768, 768], P(None, 'section'), as said below
- left_roots: bfloat16 [12, 768, 768], P(None, 'section'), as said below
- right_inverse_roots: bfloat16 [12, 768, 768], P(None, 'section'), as said below
Outputs:
- loss_sum: float32 [], replicated
- loss_count: float32 [], replicated
- grad_norm: float32 [], replicated
- table_moment: float32 [32128, 768], P('section')
- table_square: float32 [32128, 768], P('section')
- table_new: float32 [32128, 768], P('section')
- inner_moment: float32 [2, 768, 3072], P(None, None, 'section')
- inner_second_moment: float32 [2, 768, 3072], P(None, None, 'section')
- inner_new: float32 [2, 768, 3072], P(None, None, 'section')
- outer_moment: float32 [2, 3072, 768], P(None, 'section')
- outer_second_moment: float32 [2, 3072, 768], P(None, 'section')
- outer_new: float32 [2, 3072, 768], P(None, 'section')
- gain_moment: float32 [7, 768], replicated
- gain_square: float32 [7, 768], replicated
- gain_new: float32 [7, 768], replicated
- bias_moment: float32 [2, 32, 12], replicated
- bias_square: float32 [2, 32, 12], replicated
- updated_position_bias: float32 [2, 32, 12], replicated
- attention_grad: float32 [12, 768, 768], P(None, 'section')
- left_new: float32 [12, 768, 768], P(None, 'section')
- right_new: float32 [12, 768, 768], P(None, 'section')
- attention_new: float32 [12, 768, 768], P(None, 'section')
Inputs may be any that keep to these rules, and one draw needn't show every extreme that they name: `buckets`: on each side of offset 0 the bucket does not fall as the offset's magnitude grows; offsets before the query use 0 to 15, offsets after it the upper half. `left_stats`: Symmetric, dominated by a positive diagonal. `right_stats`: Symmetric, dominated by a positive diagonal. `left_roots`: Symmetric. `right_inverse_roots`: Symmetric.
All inputs are finite; a program needn't handle non-finite values.
Results may differ from a plain program's by a relative error of at most 0.0078.
Values may be sent and summed in bfloat16 or wider, within the bound.
No kernel may reach another device: no remote copies, remote signals or barrier semaphores. Data moves between devices by JAX's collectives and lax.ppermute only.
A program may use at most 640 MiB of HBM per device.

v0:
```python
import math

import jax
import jax.numpy as jnp
from jax import lax
from jax.sharding import PartitionSpec as P

D = 768
HEADS = 12
DK = 64
MICRO = 2
STEP = 5
SPAN = 28


EPS = 1e-06
CLIP = 1.0
BETA_ONE = 0.9
BETA_TWO = 0.95
BETA_STATS = 0.95
ADAM_EPS = 1e-08
DECAY = 0.01
RATE_TABLE = 0.5
RATE_INNER = 0.01
RATE_GAIN = 0.2
RATE_BIAS = 0.3
RATE_ATTENTION = 0.01
NEGATIVE = -1000000000.0
HIGH = lax.Precision.HIGHEST


def swapped(value, axis, bit):
    mask = 2**bit
    pairs = [(source, source ^ mask) for source in range(lax.axis_size(axis))]
    return lax.ppermute(value, axis, pairs)


def merged(part, axis, combine):
    gathered = jax.tree.map(lambda a: lax.all_gather(a, axis), part)

    def take(source):
        return jax.tree.map(lambda a: lax.dynamic_index_in_dim(a, source, 0, False), gathered)

    return lax.fori_loop(
        1, lax.axis_size(axis), lambda source, state: combine(state, take(source)), take(0)
    )


def to_low(values):
    return values.astype(jnp.bfloat16)


def forward_mul(left, right):
    return jnp.dot(left, right, preferred_element_type=jnp.float32)


def weight_grad(inputs, upstream):
    return jnp.einsum("nd,ne->de", inputs, upstream, preferred_element_type=jnp.float32)


def input_grad(upstream, weight):
    return jnp.einsum("ne,de->nd", upstream, weight, preferred_element_type=jnp.float32)


def rms_rows(values, gain_row):
    return values * lax.rsqrt(jnp.mean(values * values, -1, keepdims=True) + EPS) * gain_row


def final_rows(values, gain_row):
    return rms_rows(values, gain_row) * D ** (-0.5)


def norm_back(norm_rule, values, gain_row, upstream):
    result, pull = jax.vjp(norm_rule, values, gain_row)
    return pull(upstream)


def branch(condition, compute):
    return lax.cond(condition, compute, lambda: jax.tree.map(jnp.zeros_like, compute()))


def partner(values):
    bit_index = lax.axis_size("section").bit_length() - 2
    return swapped(values, "section", bit_index)


def split_heads(values):
    return values.reshape(MICRO, -1, HEADS, DK)


def position_table(onehot, bias_layer):
    return jnp.einsum("qkb,bh->hqk", onehot.astype(jnp.float32), bias_layer, precision=HIGH)


def score_block(query_heads, key_heads, bias_term, causal):
    scores = jnp.einsum(
        "sqhd,skhd->shqk", query_heads, key_heads, preferred_element_type=jnp.float32
    ) * DK ** (-0.5)
    if bias_term is not None:
        scores = scores + bias_term[None]
    if causal:
        length = scores.shape[-1]
        lower_mask = jnp.arange(length)[:, None] >= jnp.arange(length)[None, :]
        scores = jnp.where(lower_mask, scores, NEGATIVE)
    return scores


def attend_forward(query_heads, key_heads, value_heads, bias_term, causal):
    scores = score_block(query_heads, key_heads, bias_term, causal)
    row_peak = jnp.max(scores, -1, keepdims=True)
    log_total = row_peak + jnp.log(jnp.sum(jnp.exp(scores - row_peak), -1, keepdims=True))
    probs_low = to_low(jnp.exp(scores - log_total))
    mixed = jnp.einsum(
        "shqk,skhd->sqhd", probs_low, value_heads, preferred_element_type=jnp.float32
    )
    return (mixed, log_total)


def attend_backward(query_heads, key_heads, value_heads, bias_term, causal, log_total, grad_mixed):
    scores = score_block(query_heads, key_heads, bias_term, causal)
    probs = jnp.exp(scores - log_total)
    grad_probs = jnp.einsum(
        "sqhd,skhd->shqk", grad_mixed, value_heads, preferred_element_type=jnp.float32
    )
    grad_scores = to_low(probs * (grad_probs - jnp.sum(probs * grad_probs, -1, keepdims=True)))
    grad_value = jnp.einsum(
        "shqk,sqhd->skhd", to_low(probs), grad_mixed, preferred_element_type=jnp.float32
    )
    grad_query = jnp.einsum(
        "shqk,skhd->sqhd", grad_scores, key_heads, preferred_element_type=jnp.float32
    ) * DK ** (-0.5)
    grad_key = jnp.einsum(
        "shqk,sqhd->skhd", grad_scores, query_heads, preferred_element_type=jnp.float32
    ) * DK ** (-0.5)
    return (grad_query, grad_key, grad_value, grad_scores)


def attention_forward(resid, gain_row, weight_set, source, bias_term, causal):
    normed = to_low(rms_rows(resid, gain_row))
    kv_input = normed if source is None else source
    query_rows = to_low(forward_mul(normed, weight_set[0]))
    key_rows = to_low(forward_mul(kv_input, weight_set[1]))
    value_rows = to_low(forward_mul(kv_input, weight_set[2]))
    mixed, log_total = attend_forward(
        split_heads(query_rows), split_heads(key_rows), split_heads(value_rows), bias_term, causal
    )
    mixed_low = to_low(mixed.reshape(resid.shape))
    kept = (resid, normed, query_rows, key_rows, value_rows, mixed_low, log_total)
    return (resid + forward_mul(mixed_low, weight_set[3]), kept)


def attention_backward(grad_resid, kept, gain_row, weight_set, source, bias_term, causal, onehot):
    resid, normed, query_rows, key_rows, value_rows, mixed_low, log_total = kept
    kv_input = normed if source is None else source
    grad_out = to_low(grad_resid)
    grad_mixed = to_low(input_grad(grad_out, weight_set[3]))
    grad_query, grad_key, grad_value, grad_scores = attend_backward(
        split_heads(query_rows),
        split_heads(key_rows),
        split_heads(value_rows),
        bias_term,
        causal,
        log_total,
        split_heads(grad_mixed),
    )
    grad_query = to_low(grad_query.reshape(resid.shape))
    grad_key = to_low(grad_key.reshape(key_rows.shape))
    grad_value = to_low(grad_value.reshape(value_rows.shape))
    weight_grads = jnp.stack(
        [
            weight_grad(normed, grad_query),
            weight_grad(kv_input, grad_key),
            weight_grad(kv_input, grad_value),
            weight_grad(mixed_low, grad_out),
        ]
    )
    grad_normed = input_grad(grad_query, weight_set[0])
    source_grad = input_grad(grad_key, weight_set[1]) + input_grad(grad_value, weight_set[2])
    if source is None:
        grad_normed = grad_normed + source_grad
    grad_in, grad_gain = norm_back(rms_rows, resid, gain_row, grad_normed)
    bias_grad = None
    if bias_term is not None:
        bias_grad = jnp.einsum(
            "shqk,qkb->bh", grad_scores, onehot, preferred_element_type=jnp.float32
        )
    return (grad_resid + grad_in, grad_gain, weight_grads, source_grad, bias_grad)


def feed_forward(resid, gain_row, inner, outer):
    normed = to_low(rms_rows(resid, gain_row))
    before = forward_mul(normed, inner)
    active = to_low(jax.nn.gelu(before))
    return (resid + forward_mul(active, outer), (resid, normed, before, active))


def feed_backward(grad_resid, kept, gain_row, inner, outer):
    resid, normed, before, active = kept
    grad_out = to_low(grad_resid)
    grad_active = input_grad(grad_out, outer)
    result, pull = jax.vjp(jax.nn.gelu, before)
    grad_before = to_low(pull(grad_active)[0])
    grad_normed = input_grad(grad_before, inner)
    grad_in, grad_gain = norm_back(rms_rows, resid, gain_row, grad_normed)
    return (
        grad_resid + grad_in,
        grad_gain,
        weight_grad(normed, grad_before),
        weight_grad(active, grad_out),
    )


def encoder_forward(
    token_rows, table_low, inner_low, outer_low, gain_rows, attention_low, bias_enc
):
    resid = table_low[token_rows].astype(jnp.float32)
    resid, kept_attn = attention_forward(
        resid, gain_rows[0], attention_low[0:4], None, bias_enc, False
    )
    resid, kept_feed = feed_forward(resid, gain_rows[1], inner_low[0], outer_low[0])
    return (to_low(rms_rows(resid, gain_rows[2])), (kept_attn, kept_feed, resid))


def encoder_backward(
    grad_encoded, kept, inner_low, outer_low, gain_rows, attention_low, bias_enc, onehot_enc
):
    kept_attn, kept_feed, resid = kept
    grad_resid, gain_last = norm_back(
        rms_rows, resid, gain_rows[2], grad_encoded.astype(jnp.float32)
    )
    grad_resid, gain_feed, inner_grad, outer_grad = feed_backward(
        grad_resid, kept_feed, gain_rows[1], inner_low[0], outer_low[0]
    )
    grad_resid, gain_attn, weight_grads, unused, bias_grad = attention_backward(
        grad_resid, kept_attn, gain_rows[0], attention_low[0:4], None, bias_enc, False, onehot_enc
    )
    return (
        weight_grads,
        jnp.stack([gain_attn, gain_feed, gain_last]),
        bias_grad,
        inner_grad,
        outer_grad,
        to_low(grad_resid),
    )


def decoder_forward(
    token_rows, encoded, table_low, inner_low, outer_low, gain_rows, attention_low, bias_dec
):
    resid = table_low[token_rows].astype(jnp.float32)
    resid, kept_self = attention_forward(
        resid, gain_rows[3], attention_low[4:8], None, bias_dec, True
    )
    resid, kept_cross = attention_forward(
        resid, gain_rows[4], attention_low[8:12], encoded, None, False
    )
    resid, kept_feed = feed_forward(resid, gain_rows[5], inner_low[1], outer_low[1])
    return (to_low(final_rows(resid, gain_rows[6])), (kept_self, kept_cross, kept_feed, resid))


def decoder_backward(
    grad_final, kept, encoded, inner_low, outer_low, gain_rows, attention_low, bias_dec, onehot_dec
):
    kept_self, kept_cross, kept_feed, resid = kept
    grad_resid, gain_last = norm_back(
        final_rows, resid, gain_rows[6], grad_final.astype(jnp.float32)
    )
    grad_resid, gain_feed, inner_grad, outer_grad = feed_backward(
        grad_resid, kept_feed, gain_rows[5], inner_low[1], outer_low[1]
    )
    grad_resid, gain_cross, cross_weights, grad_encoded, unused = attention_backward(
        grad_resid, kept_cross, gain_rows[4], attention_low[8:12], encoded, None, False, onehot_dec
    )
    grad_resid, gain_self, self_weights, unused_source, bias_grad = attention_backward(
        grad_resid, kept_self, gain_rows[3], attention_low[4:8], None, bias_dec, True, onehot_dec
    )
    return (
        jnp.concatenate([self_weights, cross_weights]),
        jnp.stack([gain_self, gain_cross, gain_feed, gain_last]),
        bias_grad,
        inner_grad,
        outer_grad,
        to_low(grad_resid),
        to_low(grad_encoded),
    )


def vocab_stats(head_rows, table_part, parts):

    def visit(running, block_index):
        row_peak, row_total = running
        logits = jnp.einsum("nd,vd->nv", head_rows, table_part, preferred_element_type=jnp.float32)
        new_peak = jnp.maximum(row_peak, jnp.max(logits, -1))
        row_total = row_total * jnp.exp(row_peak - new_peak) + jnp.sum(
            jnp.exp(logits - new_peak[:, None]), -1
        )
        return ((new_peak, row_total), None)

    start_value = (
        jnp.full((head_rows.shape[0],), NEGATIVE, jnp.float32),
        jnp.zeros((head_rows.shape[0],), jnp.float32),
    )
    result, unused = lax.scan(visit, start_value, jnp.arange(parts))
    return result


def merge_stats(earlier, later):
    new_peak = jnp.maximum(earlier[0], later[0])
    return (
        new_peak,
        earlier[1] * jnp.exp(earlier[0] - new_peak) + later[1] * jnp.exp(later[0] - new_peak),
    )


def vocab_rows_back(all_rows, shard_low, total_all):
    row_block = math.gcd(all_rows.shape[0], 2048)
    blocks = all_rows.shape[0] // row_block

    def visit(running, block_index):
        row_slice = lax.dynamic_slice_in_dim(all_rows, block_index * row_block, row_block, 0)
        total_slice = lax.dynamic_slice_in_dim(total_all, block_index * row_block, row_block, 0)
        logits = jnp.einsum("nd,vd->nv", row_slice, shard_low, preferred_element_type=jnp.float32)
        probs_low = to_low(jnp.exp(logits - total_slice[:, None]))
        grad_slice = jnp.einsum(
            "nv,vd->nd", probs_low, shard_low, preferred_element_type=jnp.float32
        )
        return (
            running
            + jnp.einsum("nv,nd->vd", probs_low, row_slice, preferred_element_type=jnp.float32),
            grad_slice,
        )

    head_table, grad_blocks = lax.scan(
        visit, jnp.zeros(shard_low.shape, jnp.float32), jnp.arange(blocks)
    )
    return (head_table, grad_blocks.reshape(all_rows.shape))


def sum_rows(row_ids, row_values, row_count):
    inside = (row_ids >= 0) & (row_ids < row_count)
    return jax.ops.segment_sum(row_values, jnp.where(inside, row_ids, row_count), row_count + 1)[
        :row_count
    ]


def adamw(weight, first, second, gradient, rate):
    first = BETA_ONE * first + (1 - BETA_ONE) * gradient
    second = BETA_TWO * second + (1 - BETA_TWO) * gradient * gradient
    stepped = first / (1 - BETA_ONE**STEP) / (jnp.sqrt(second / (1 - BETA_TWO**STEP)) + ADAM_EPS)
    return (first, second, weight - rate * (stepped + DECAY * weight))


def shampoo_direction(left_roots, attention_full, complete_inverse_roots):
    blended_left_factor = to_low(
        jnp.einsum("mrd,mde->mre", left_roots.astype(jnp.float32), attention_full, precision=HIGH)
    )
    return jnp.einsum(
        "cqt,ctx->cqx",
        blended_left_factor,
        complete_inverse_roots,
        preferred_element_type=jnp.float32,
    )


def local(
    token_ids,
    targets,
    objective,
    buckets,
    table,
    table_first,
    table_second,
    inner_weight,
    inner_first,
    inner_second,
    outer_weight,
    outer_first,
    outer_second,
    gain_rows,
    gain_first,
    gain_second,
    position_bias,
    bias_first,
    bias_second,
    attention,
    left_stats,
    right_stats,
    left_roots,
    right_inverse_roots,
):
    sections = lax.axis_size("section")
    section_index = lax.axis_index("section")
    is_encoder = section_index < sections // 2
    is_decoder = jnp.logical_not(is_encoder)
    table_low, inner_low, outer_low, attention_low, complete_inverse_roots = (
        lax.all_gather(to_low(table), "section", axis=0, tiled=True),
        lax.all_gather(to_low(inner_weight), "section", axis=2, tiled=True),
        lax.all_gather(to_low(outer_weight), "section", axis=1, tiled=True),
        lax.all_gather(to_low(attention), "section", axis=1, tiled=True),
        lax.all_gather(right_inverse_roots, "section", axis=1, tiled=True),
    )
    shard_low = to_low(table)
    length = token_ids.shape[-1]
    token_rows = token_ids.reshape(-1)
    goal_rows = targets.reshape(-1)
    offsets = jnp.arange(length)[None, :] - jnp.arange(length)[:, None] + length - 1
    bucket_range = jnp.arange(position_bias.shape[1])
    onehot_enc = (buckets[0][offsets][:, :, None] == bucket_range).astype(jnp.bfloat16)
    onehot_dec = (buckets[1][offsets][:, :, None] == bucket_range).astype(jnp.bfloat16)
    bias_enc = position_table(onehot_enc, position_bias[0])
    bias_dec = position_table(onehot_dec, position_bias[1])
    encoded, enc_kept = branch(
        is_encoder,
        lambda: encoder_forward(
            token_rows, table_low, inner_low, outer_low, gain_rows, attention_low, bias_enc
        ),
    )
    arrived = partner(encoded)
    final_low, dec_kept = branch(
        is_decoder,
        lambda: decoder_forward(
            token_rows, arrived, table_low, inner_low, outer_low, gain_rows, attention_low, bias_dec
        ),
    )
    final_split = final_low.reshape(MICRO, length, -1)
    handed = partner(final_split[1])
    own_rows = jnp.where(is_encoder, handed, final_split[0])
    live_rows = (jnp.arange(length) < jnp.where(objective.reshape(()) == 1, length, SPAN)).astype(
        jnp.float32
    )
    head_low = own_rows * live_rows[:, None].astype(jnp.bfloat16)
    target_rows = table_low[goal_rows]
    target_logit = jnp.einsum("nd,nd->n", head_low, target_rows, preferred_element_type=jnp.float32)
    all_rows = lax.all_gather(head_low, "section", axis=0, tiled=True)
    row_peak, row_total = vocab_stats(all_rows, shard_low, 1)
    row_peak, row_total = merged((row_peak, row_total), "section", merge_stats)
    total_all = row_peak + jnp.log(row_total)
    log_total = lax.dynamic_slice_in_dim(total_all, section_index * length, length, 0)
    head_table, grad_all = vocab_rows_back(all_rows, shard_low, total_all)
    grad_head = lax.psum_scatter(grad_all, "section", scatter_dimension=0, tiled=True)
    head_gradient_reduced = to_low(
        (grad_head - target_rows.astype(jnp.float32)) * live_rows[:, None]
    )
    loss_part = jnp.sum(live_rows * (log_total - target_logit))
    count_part = jnp.sum(live_rows)
    returned = partner(head_gradient_reduced)
    grad_final = jnp.concatenate([head_gradient_reduced, returned])
    dec_grads = branch(
        is_decoder,
        lambda: decoder_backward(
            grad_final,
            dec_kept,
            arrived,
            inner_low,
            outer_low,
            gain_rows,
            attention_low,
            bias_dec,
            onehot_dec,
        ),
    )
    back_encoded = partner(dec_grads[6])
    enc_grads = branch(
        is_encoder,
        lambda: encoder_backward(
            back_encoded,
            enc_kept,
            inner_low,
            outer_low,
            gain_rows,
            attention_low,
            bias_enc,
            onehot_enc,
        ),
    )
    embed_grad = enc_grads[5].astype(jnp.float32) + dec_grads[5].astype(jnp.float32)
    scatter_ids = jnp.concatenate([token_rows, goal_rows])
    scatter_values = jnp.concatenate([embed_grad, -head_low.astype(jnp.float32)])
    owned_rows = table.shape[0]
    row_terms = sum_rows(scatter_ids, scatter_values, owned_rows * lax.axis_size("section"))
    table_grad = (
        lax.psum_scatter(row_terms, "section", scatter_dimension=0, tiled=True) + head_table
    )
    attention_grad = jnp.concatenate([enc_grads[0], dec_grads[0]])
    gain_grad = jnp.concatenate([enc_grads[1], dec_grads[1]])
    bias_grad = jnp.stack([enc_grads[2], dec_grads[2]])
    inner_grad = jnp.stack([enc_grads[3], dec_grads[3]])
    outer_grad = jnp.stack([enc_grads[4], dec_grads[4]])
    inner_part, outer_part = (
        lax.psum_scatter(inner_grad, "section", scatter_dimension=2, tiled=True),
        lax.psum_scatter(outer_grad, "section", scatter_dimension=1, tiled=True),
    )
    attention_full, gain_full, bias_full = lax.psum(
        (attention_grad, gain_grad, bias_grad), ("section", "dp")
    )
    table_grad, inner_part, outer_part, loss_part, count_part = lax.psum(
        (table_grad, inner_part, outer_part, loss_part, count_part), "dp"
    )
    rows_here = attention.shape[1]
    own_grad = lax.dynamic_slice_in_dim(attention_full, section_index * rows_here, rows_here, 1)
    small_square = jnp.sum(gain_full * gain_full) + jnp.sum(bias_full * bias_full)
    square_sum = (
        jnp.sum(table_grad * table_grad)
        + jnp.sum(inner_part * inner_part)
        + jnp.sum(outer_part * outer_part)
        + jnp.sum(own_grad * own_grad)
        + jnp.where(section_index == 0, small_square, 0.0)
    )
    square_total, summed_loss_value, count_total = lax.psum(
        (square_sum, loss_part, count_part), "section"
    )
    direction = shampoo_direction(left_roots, attention_full, complete_inverse_roots)
    direction_total = lax.psum(jnp.sum(direction * direction, (1, 2)), "section")
    grad_norm = jnp.sqrt(square_total)
    clip_factor = CLIP / jnp.maximum(grad_norm, CLIP)
    table_out = adamw(table, table_first, table_second, table_grad * clip_factor, RATE_TABLE)
    inner_out = adamw(inner_weight, inner_first, inner_second, inner_part * clip_factor, RATE_INNER)
    outer_out = adamw(outer_weight, outer_first, outer_second, outer_part * clip_factor, RATE_INNER)
    gain_out = adamw(gain_rows, gain_first, gain_second, gain_full * clip_factor, RATE_GAIN)
    bias_out = adamw(position_bias, bias_first, bias_second, bias_full * clip_factor, RATE_BIAS)
    clipped = attention_full * clip_factor
    own_clipped = own_grad * clip_factor
    column_part = lax.dynamic_slice_in_dim(clipped, section_index * rows_here, rows_here, 2)
    left_new = BETA_STATS * left_stats + (1 - BETA_STATS) * jnp.einsum(
        "mrd,med->mre", own_clipped, clipped, precision=HIGH
    )
    right_new = BETA_STATS * right_stats + (1 - BETA_STATS) * jnp.einsum(
        "mdr,mde->mre", column_part, clipped, precision=HIGH
    )
    spread = jnp.sqrt(direction_total / (D * D) + EPS)[:, None, None]
    attention_new = attention - RATE_ATTENTION * (direction / spread + DECAY * attention)
    return (
        summed_loss_value,
        count_total,
        grad_norm,
        table_out[0],
        table_out[1],
        table_out[2],
        inner_out[0],
        inner_out[1],
        inner_out[2],
        outer_out[0],
        outer_out[1],
        outer_out[2],
        gain_out[0],
        gain_out[1],
        gain_out[2],
        bias_out[0],
        bias_out[1],
        bias_out[2],
        own_clipped,
        left_new,
        right_new,
        attention_new,
    )


def solution(mesh):
    in_specs = (
        P("dp", "section", None, None),
        P("dp", "section", None),
        P("dp", "section"),
        P(),
        P("section", None),
        P("section", None),
        P("section", None),
        P(None, None, "section"),
        P(None, None, "section"),
        P(None, None, "section"),
        P(None, "section", None),
        P(None, "section", None),
        P(None, "section", None),
        P(),
        P(),
        P(),
        P(),
        P(),
        P(),
        P(None, "section", None),
        P(None, "section", None),
        P(None, "section", None),
        P(None, "section", None),
        P(None, "section", None),
    )
    out_specs = (
        P(),
        P(),
        P(),
        P("section", None),
        P("section", None),
        P("section", None),
        P(None, None, "section"),
        P(None, None, "section"),
        P(None, None, "section"),
        P(None, "section", None),
        P(None, "section", None),
        P(None, "section", None),
        P(),
        P(),
        P(),
        P(),
        P(),
        P(),
        P(None, "section", None),
        P(None, "section", None),
        P(None, "section", None),
        P(None, "section", None),
    )
    return jax.shard_map(local, mesh=mesh, in_specs=in_specs, out_specs=out_specs, check_vma=False)
```

profile of v0, /device:TPU:0, one launch (start us, length us, event | category | flops | bytes accessed | tf_op | source)
XLA Modules:
  0.0 3596.0 jit_solution(12380204106856123351)
XLA Ops:
  7.3 3.1 copy.501
  13.8 4.7 convert_element_type.348
  18.6 101.4 %gather_fusion.3 = s32[16384]{0:T(1024)S(1)} fusion(s32[255]{0:T(256)S(1)} %bitcast.481, s32[16384]{0:T(1024)S(1)} %fusion.255), kind=kCustom, calls=%fused_computation.3 | custom fusion | bytes 196608 | tf_op jit(solution)/shard_map/gather | solution.py:408
  124.0 101.4 %gather_fusion.2 = s32[16384]{0:T(1024)S(1)} fusion(s32[255]{0:T(256)S(1)} %bitcast.480, s32[16384]{0:T(1024)S(1)} %fusion.255), kind=kCustom, calls=%fused_computation.2 | custom fusion | bytes 196608 | tf_op jit(solution)/shard_map/gather | solution.py:409
  226.8 62.5 %all-gather.11.cloned.1.call-done = bf16[12,768,768]{2,1,0:T(8,128)(2,1)} async-done(((bf16[12,48,768]{2,1,0:T(8,128)(2,1)}), bf16[12,768,768]{2,1,0:T(8,128)(2,1)}) %all-gather.11.cloned.1.call-update) | async-done | bytes 14155792 | tf_op jit(solution)/shard_map/all_gather | solution.py:399
  289.3 242.7 %all-gather.9.cloned.1.call-done = bf16[32128,768]{1,0:T(8,128)(2,1)} async-done(((bf16[2008,768]{1,0:T(8,128)(2,1)}), bf16[32128,768]{1,0:T(8,128)(2,1)}) %all-gather.9.cloned.1.call-update) | async-done | bytes 49348624 | tf_op jit(solution)/shard_map/all_gather | solution.py:396
  532.0 70.1 %conditional.4 = (bf16[256,768]{1,0:T(8,128)(2,1)}, f32[256,768]{1,0:T(8,128)S(1)}, bf16[256,768]{1,0:T(8,128)(2,1)}, bf16[256,768]{1,0:T(8,128)(2,1)}, bf16[256...) conditional(s32[]{:T(128)} %convert_element_type.350, () %tuple.83, ...), branch_computations={%region_0.0_spmd, %region_1.0_spmd} | conditional | flops 3738697216 | bytes 77253920 | solution.py:79
  532.3 2.9 gather_fusion
  558.9 2.8 multiply_reduce_fusion.22
  563.8 23.8 copy.282
  587.5 6.6 fusion.185
  594.1 5.3 multiply_reduce_fusion.21
  608.5 14.5 collective-permute-done
  623.8 21.8 conditional.5
  645.6 67.2 %collective-permute-start.1 = (bf16[128,768]{1,0:T(8,128)(2,1)S(1)}, bf16[128,768]{1,0:T(8,128)(2,1)S(1)}, u32[]{:S(2)}, u32[]{:S(2)}) collective-permute-start(bf16[128,768]{1,0:T(8,128)(2,1)S(1)} %slice.197), channel_id=1, source_target_pairs={{0,16},{2,18},{4,20},{6,22},{8,24},{10,26},{12,28},{14,30},{16,0},... | collective-permute-start | bytes 589832 | tf_op jit(solution)/shard_map/ppermute | solution.py:35
  713.5 8.4 collective-permute-done.1
  722.8 45.6 %all-gather.17.cloned.1.call-done = bf16[2048,768]{1,0:T(8,128)(2,1)} async-done(((bf16[128,768]{1,0:T(8,128)(2,1)}), bf16[2048,768]{1,0:T(8,128)(2,1)}) %all-gather.17.cloned.1.call-update) | async-done | bytes 3145744 | tf_op jit(solution)/shard_map/all_gather | solution.py:434
  768.4 12.4 fusion.276
  780.8 7.9 exponential_reduce_fusion.3
  788.8 19.6 all-gather.1
  808.4 17.8 all-gather
  827.3 13.1 fusion.246
  843.5 80.7 %reduce-scatter.7.cloned.1.call-done = f32[128,768]{1,0:T(8,128)} async-done(((f32[2048,768]{1,0:T(8,128)}), f32[128,768]{1,0:T(8,128)}) %reduce-scatter.7.cloned.1.call-update) | async-done | bytes 393232 | tf_op jit(solution)/shard_map/reduce_scatter | solution.py:440
  927.5 9.4 collective-permute-done.2
  937.0 22.9 conditional.6
  937.4 8.1 broadcast.556.clone
  945.5 4.1 stack.74
  949.6 4.1 stack.75.clone
  961.1 147.0 %collective-permute-start.3 = (bf16[256,768]{1,0:T(8,128)(2,1)}, bf16[256,768]{1,0:T(8,128)(2,1)S(1)}, u32[]{:S(2)}, u32[]{:S(2)}) collective-permute-start(bf16[256,768]{1,0:T(8,128)(2,1)} %get-tuple-element.451), channel_id=1, source_target_pairs={{0,16},{2,18},{4,20},{6,22},{8,24},{10,26},{12,28},{14,30},{16,0},... | collective-permute-start | bytes 1179656 | tf_op jit(solution)/shard_map/ppermute | solution.py:35
  1109.3 15.9 collective-permute-done.3
  1125.3 115.7 %conditional.7 = (f32[3,768]{1,0:T(4,128)S(1)}, f32[1,768,3072]{1,2,0:T(8,128)}, f32[256,768]{1,0:T(8,128)}, f32[1,3072,768]{2,1,0:T(8,128)}, f32[4,768,768]{2,1,0:T(8,128)}, /*index=5*/f32[1,32,12]{1,0,2:T(1,128)}) conditional(s32[]{:T(128)} %convert_element_type.350, () %tuple.87, (bf16[256,768]{1,0:T(8,128)(2,1)}, bf16[256,768]{1,0:T(8,128)(2,1)}, ...), branch_computations={%region_45.46_spmd, %region_46.58_spmd} | conditional | flops 7552503296 | bytes 218593328 | solution.py:79
  1128.2 7.4 fusion.118
  1136.9 24.1 copy.298
  1161.0 5.1 multiply_reduce_fusion.18
  1174.6 2.7 fusion.153
  1196.2 3.9 pad_maximum_fusion.1
  1200.1 10.1 copy.338
  1218.3 6.1 convolution_bitcast_fusion.4
  1224.4 6.8 convolution_bitcast_fusion.3
  1231.2 9.6 copy.336
  1243.6 30.6 broadcast_in_dim.70
  1274.1 49.8 %scatter_fusion = f32[32129,768]{1,0:T(8,128)} fusion(f32[32129,768]{1,0:T(8,128)} %broadcast_in_dim.70, s32[384]{0:T(512)S(1)} %copy-done.129, f32[384,768]{1,0:T(8,128)S(1)} %pad_maximum_fusion.6), kind=kCustom, calls=%fused_computation.5 | custom fusion | flops 294912 | bytes 3540480 | tf_op jit(solution)/shard_map/scatter-add | solution.py:341
  1323.9 65.7 %slice.218 = f32[32128,768]{1,0:T(8,128)} slice(f32[32129,768]{1,0:T(8,128)} %scatter_fusion), slice={[0:32128], [0:768]} | slice | bytes 197394432 | tf_op jit(solution)/shard_map/slice | solution.py:341
  1389.7 16.5 pad_maximum_fusion.5
  1406.3 18.5 pad_maximum_fusion.4
  1424.8 26.0 pad_maximum_fusion.3
  1451.6 828.7 %reduce-scatter.13.cloned.1.call-done = f32[2008,768]{1,0:T(8,128)} async-done(((f32[32128,768]{1,0:T(8,128)}), f32[2008,768]{1,0:T(8,128)}) %reduce-scatter.13.cloned.1.call-update) | async-done | bytes 6168592
  2280.3 13.7 convolution_add_fusion.6
  2294.0 184.5 %reduce-scatter.11.cloned.1.call-done = f32[2,192,768]{2,1,0:T(8,128)} async-done(((f32[2,3072,768]{2,1,0:T(8,128)}), f32[2,192,768]{2,1,0:T(8,128)}) %reduce-scatter.11.cloned.1.call-update) | async-done | bytes 1179664 | tf_op jit(solution)/shard_map/reduce_scatter | solution.py:491
  2478.5 198.2 %reduce-scatter.9.cloned.1.call-done = f32[2,768,192]{1,2,0:T(8,128)} async-done(((f32[2,768,3072]{1,2,0:T(8,128)}), f32[2,768,192]{1,2,0:T(8,128)}) %reduce-scatter.9.cloned.1.call-update) | async-done | bytes 1179664 | tf_op jit(solution)/shard_map/reduce_scatter | solution.py:490
  2678.0 5.6 all-reduce.3
  2684.3 42.2 %all-reduce.1 = (f32[7,768]{1,0:T(8,128)S(1)}, f32[2,32,12]{1,0,2:T(2,128)S(1)}) all-reduce(f32[7,768]{1,0:T(8,128)S(1)} %pad_maximum_fusion.8, f32[2,32,12]{1,0,2:T(2,128)S(1)} %pad_maximum_fusion.9), channel_id=1, replica_groups=mesh['section'=16,'dp'=2] {'section','dp'}, use_global_device_ids=true, to_apply=%region_70.71 | all-reduce | flops 6144 | bytes 49152 | tf_op jit(solution)/shard_map/psum | solution.py:493
  2729.0 383.1 %all-reduce.8.cloned.1.call-done = f32[12,768,768]{2,1,0:T(8,128)} async-done(((f32[12,768,768]{2,1,0:T(8,128)}), f32[12,768,768]{2,1,0:T(8,128)}) %all-reduce.8.cloned.1.call-update) | async-done | bytes 28311568 | tf_op jit(solution)/shard_map/psum | solution.py:493
  3114.7 15.4 convolution_convert_fusion.18
  3130.1 95.2 %all-gather.19.cloned.1.call-done = bf16[12,768,768]{2,1,0:T(8,128)(2,1)} async-done(((bf16[12,48,768]{2,1,0:T(8,128)(2,1)}), bf16[12,768,768]{2,1,0:T(8,128)(2,1)}) %all-gather.19.cloned.1.call-update) | async-done | bytes 14155792 | tf_op jit(solution)/shard_map/all_gather | solution.py:400
  3225.4 7.7 multiply_reduce_fusion.29
  3233.0 195.8 %all-reduce.10.cloned.1.call-done = (f32[2008,768]{1,0:T(8,128)}, f32[2,768,192]{1,2,0:T(8,128)}, f32[2,192,768]{2,1,0:T(8,128)}) async-done(((f32[2008,768]{1,0:T(8,128)}, f32[2,768,192]{1,2,0:T(8,128)}, f32[2,192,768]{2,1,0:T(8,128)}), (f32[2008,768]{1,0:T(8,128)}, f32[2,768,192]{1,2,0:T(8,128)}, f32[2,192,768]{2,1,0:T(8,128)})) %all-reduce.10.cloned.1.call-update) | async-done | bytes 8527888 | tf_op jit(solution)/shard_map/psum | solution.py:496
  3428.9 5.1 multiply_reduce_fusion.28
  3438.3 34.0 all-reduce.2
  3473.1 20.9 broadcast_multiply_fusion
  3494.0 36.1 %multiply_add_fusion.10 = f32[12,48,768]{2,1,0:T(8,128)} fusion(f32[12,48,768]{2,1,0:T(8,128)} %param.55, f32[12,768,768]{2,1,0:T(8,128)} %broadcast_multiply_fusion, s32[]{:T(128)S(6)} %select_n.98), kind=kOutput, calls=%fused_computation.433 | convolution fusion | flops 4078190592 | bytes 36569092 | tf_op jit(solution)/shard_map/mdr,mde->mre/dot_general | solution.py:527
  3530.1 3.8 multiply_subtract_fusion.1
  3534.0 32.9 multiply_add_fusion.11
  3574.4 13.5 multiply_subtract_fusion
  (333 shorter events, 128.5 us)
Async XLA Ops:
  7.2 3107.5 %copy-start = (bf16[12,48,768]{2,1,0:T(8,128)(2,1)S(1)}, bf16[12,48,768]{2,1,0:T(8,128)(2,1)}, u32[]{:S(2)}) copy-start(bf16[12,48,768]{2,1,0:T(8,128)(2,1)} %param.56) | copy-start | bytes 2654212
  7.2 5.5 copy-start.24
  7.2 219.6 %all-gather.13.cloned.1.call-start = ((), (), s32[]{:S(2)}) async-start(), calls=%async_computation.6 | async-start | bytes 10027008 | tf_op jit(solution)/shard_map/all_gather | solution.py:397
  10.4 216.4 %all-gather.15.cloned.1.call-start = ((), (), s32[]{:S(2)}) async-start(), calls=%async_computation.7 | async-start | bytes 10027008 | tf_op jit(solution)/shard_map/all_gather | solution.py:398
  12.7 276.6 %all-gather.11.cloned.1.call-start = ((), (), s32[]{:S(2)}) async-start(), calls=%async_computation.5 | async-start | bytes 15040512 | tf_op jit(solution)/shard_map/all_gather | solution.py:399
  13.7 4.8 copy-start.134
  13.8 518.2 %all-gather.9.cloned.1.call-start = ((), (), s32[]{:S(2)}) async-start(), calls=%async_computation.4 | async-start | bytes 52432896 | tf_op jit(solution)/shard_map/all_gather | solution.py:396
  18.5 749.9 %all-gather.17.cloned.1.call-start = ((), (), s32[]{:S(2)}) async-start(), calls=%async_computation.8 | async-start | bytes 3342336 | tf_op jit(solution)/shard_map/all_gather | solution.py:434
  123.9 102.2 %copy-start.111 = (f32[2,32,12]{1,0,2:T(2,128)S(1)}, f32[2,32,12]{1,0,2:T(2,128)}, u32[]{:S(2)}) copy-start(f32[2,32,12]{1,0,2:T(2,128)} %param.50) | copy-start | bytes 9220
  123.9 408.0 %copy-start.96 = (f32[7,768]{1,0:T(8,128)S(1)}, f32[7,768]{1,0:T(8,128)}, u32[]{:S(2)}) copy-start(f32[7,768]{1,0:T(8,128)} %param.47) | copy-start | bytes 64516
  124.0 408.0 %copy-start.128 = (s32[1,1,2,128]{3,2,1,0:T(2,128)S(1)}, s32[1,1,2,128]{3,2,1,0:T(2,128)}, u32[]{:S(2)}) copy-start(s32[1,1,2,128]{3,2,1,0:T(2,128)} %param.34) | copy-start | bytes 3076
  226.7 305.2 %copy-start.20 = (f32[12,128,128]{2,0,1:T(8,128)}, f32[12,128,128]{2,0,1:T(8,128)S(1)}, u32[]{:S(2)}) copy-start(f32[12,128,128]{2,0,1:T(8,128)S(1)} %convolution_bitcast_fusion.10) | copy-start | bytes 2359300
  535.4 23.5 copy-start.3
  535.6 7.3 copy-start.33
  537.6 9.1 copy-start.61
  550.1 7.6 copy-start.102
  594.1 7.4 copy-start.4
  602.1 21.0 copy-start.5
  602.1 21.0 collective-permute-start
  645.6 76.2 %collective-permute-start.1 = (bf16[128,768]{1,0:T(8,128)(2,1)S(1)}, bf16[128,768]{1,0:T(8,128)(2,1)S(1)}, u32[]{:S(2)}, u32[]{:S(2)}) collective-permute-start(bf16[128,768]{1,0:T(8,128)(2,1)S(1)} %slice.197), channel_id=1, source_target_pairs={{0,16},{2,18},{4,20},{6,22},{8,24},{10,26},{12,28},{14,30},{16,0},... | collective-permute-start | bytes 589832 | tf_op jit(solution)/shard_map/ppermute | solution.py:35
  722.8 201.4 %reduce-scatter.7.cloned.1.call-start = ((), (), s32[]{:S(2)}) async-start(), calls=%async_computation.9 | async-start | bytes 6684672 | tf_op jit(solution)/shard_map/reduce_scatter | solution.py:440
  827.3 13.1 copy-start.125
  840.4 83.8 %copy-start.73 = (bf16[128,768]{1,0:T(8,128)(2,1)S(1)}, bf16[128,768]{1,0:T(8,128)(2,1)}, u32[]{:S(2)}) copy-start(bf16[128,768]{1,0:T(8,128)(2,1)} %get-tuple-element.803) | copy-start | bytes 589828
  840.5 1439.9 %reduce-scatter.13.cloned.1.call-start = ((), (), s32[]{:S(2)}) async-start(), calls=%async_computation.14 | async-start | bytes 104865792
  925.9 11.1 collective-permute-start.2
  937.0 188.3 %copy-start.6 = (f32[256,768]{1,0:T(8,128)S(1)}, f32[256,768]{1,0:T(8,128)}, u32[]{:S(2)}) copy-start(f32[256,768]{1,0:T(8,128)} %copy-done.5) | copy-start | bytes 2359300
  961.1 164.2 %collective-permute-start.3 = (bf16[256,768]{1,0:T(8,128)(2,1)}, bf16[256,768]{1,0:T(8,128)(2,1)S(1)}, u32[]{:S(2)}, u32[]{:S(2)}) collective-permute-start(bf16[256,768]{1,0:T(8,128)(2,1)} %get-tuple-element.451), channel_id=1, source_target_pairs={{0,16},{2,18},{4,20},{6,22},{8,24},{10,26},{12,28},{14,30},{16,0},... | collective-permute-start | bytes 1179656 | tf_op jit(solution)/shard_map/ppermute | solution.py:35
  1125.3 40.9 %copy-start.45 = (bf16[256,768]{1,0:T(8,128)(2,1)}, bf16[256,768]{1,0:T(8,128)(2,1)S(1)}, u32[]{:S(2)}) copy-start(bf16[256,768]{1,0:T(8,128)(2,1)S(1)} %get-tuple-element.340) | copy-start | bytes 1179652 | tf_op jit(solution)/shard_map/cond
  1172.7 12.1 copy-start.21
  1174.6 11.4 copy-start.103
  1186.0 3.7 copy-start.35
  1200.1 12.0 copy-start.91
  1210.2 3.7 copy-start.50
  1213.9 3.3 copy-start.43
  1218.3 6.1 copy-start.46
  1241.0 33.1 copy-start.109
  1243.5 30.6 copy-start.129
  1389.6 1088.9 %reduce-scatter.11.cloned.1.call-start = ((), (), s32[]{:S(2)}) async-start(), calls=%async_computation.11 | async-start | bytes 20054016 | tf_op jit(solution)/shard_map/reduce_scatter | solution.py:491
  1406.2 1270.5 %reduce-scatter.9.cloned.1.call-start = ((), (), s32[]{:S(2)}) async-start(), calls=%async_computation.10 | async-start | bytes 20054016 | tf_op jit(solution)/shard_map/reduce_scatter | solution.py:490
  1424.8 1687.4 %all-reduce.8.cloned.1.call-start = ((), (), s32[]{:S(2)}) async-start(), calls=%async_computation.12 | async-start | bytes 56623104 | tf_op jit(solution)/shard_map/psum | solution.py:493
  1450.8 829.5 %copy-start.126 = (f32[2048]{0:T(1024)S(1)}, f32[2048]{0:T(1024)}, u32[]{:S(2)}) copy-start(f32[2048]{0:T(1024)} %copy-done.125) | copy-start | bytes 24580
  1450.8 1774.5 %all-gather.19.cloned.1.call-start = ((), (), s32[]{:S(2)}) async-start(), calls=%async_computation.13 | async-start | bytes 15040512 | tf_op jit(solution)/shard_map/all_gather | solution.py:400
  1451.6 1977.3 %all-reduce.10.cloned.1.call-start = ((), (), s32[]{:S(2)}) async-start(), calls=%async_computation.15 | async-start | bytes 17055744 | tf_op jit(solution)/shard_map/psum | solution.py:496
  2676.7 6.9 copy-start.116
  2676.7 7.6 copy-start.108
  2676.7 7.6 copy-start.110
  2726.5 403.6 %copy-start.104 = (f32[7,768]{1,0:T(8,128)}, f32[7,768]{1,0:T(8,128)S(1)}, u32[]{:S(2)}) copy-start(f32[7,768]{1,0:T(8,128)S(1)} %get-tuple-element.766) | copy-start | bytes 64516
  3428.9 5.1 copy-start.39
  3428.9 6.0 copy-start.41
  3530.1 3.8 copy-start.36
  3533.9 33.0 copy-start.9
  3533.9 33.0 copy-start.112
  3533.9 33.0 copy-start.123
  3533.9 33.0 copy-start.124
  3533.9 33.6 copy-start.97
  3533.9 33.6 copy-start.105
  3533.9 33.6 copy-start.117
  3533.9 33.6 copy-start.118
  3533.9 34.3 copy-start.37
  3533.9 34.2 copy-start.42
  3534.0 34.2 copy-start.92
  3534.0 34.2 copy-start.93
  3534.0 36.7 %copy-start.95 = (f32[2,768,192]{1,2,0:T(8,128)S(1)}, f32[2,768,192]{1,2,0:T(8,128)}, u32[]{:S(2)}) copy-start(f32[2,768,192]{1,2,0:T(8,128)} %param.42) | copy-start | bytes 3538948
  3568.2 5.7 slice-start
  (19 other events, 34.7 us)
Sparse Core Ops, SparseCore 0:
  10.9 84.1 all-gather.12
  97.9 79.6 all-gather.14
  180.5 108.7 all-gather.10
  291.3 240.6 all-gather.8
  722.9 45.5 all-gather.16
  840.6 83.5 reduce-scatter.6
  1389.7 890.5 reduce-scatter.12
  2284.4 194.0 reduce-scatter.10
  2482.6 194.0 reduce-scatter.8
  2683.0 429.1 all-reduce.7
  3114.7 110.5 all-gather.18
  3228.6 200.2 all-reduce.9
where the time goes:
time: 3610 us; the launch traced here: 3600 us
  waiting for transfers between devices  2370 us (66%)
  local copies, waits for them, and re-layouts  446 us (12%)
  starting transfers between devices  216 us (6%)
  other arithmetic  211 us (6%)
  matrix products  202 us (6%)
  blocking collectives  119 us (3%)
    unnamed x13, waiting for transfers between devices  830 us
    psum x1, waiting for transfers between devices, local(): lax.psum((attention_grad, gain_grad, bias_grad), ('section', 'dp'))  383 us
    all_gather x1, waiting for transfers between devices, local(): lax.all_gather(to_low(table), 'section', axis=0, tiled=True)  243 us
    ppermute x4, starting transfers between devices, swapped(): return lax.ppermute(value, axis, pairs)  216 us
    reduce_scatter x1, waiting for transfers between devices, local(): lax.psum_scatter(inner_grad, 'section', scatter_dimension=2, tiled=True)  198 us
    psum x1, waiting for transfers between devices, local(): lax.psum((table_grad, inner_part, outer_part, loss_part, count_part), 'dp')  196 us
    reduce_scatter x1, waiting for transfers between devices, local(): lax.psum_scatter(outer_grad, 'section', scatter_dimension=1, tiled=True)  184 us
    gather x2, local copies, waits for them, and re-layouts, local(): buckets[1][offsets][:, :, None] == bucket_range  102 us
  transfers between devices with their start and end apart: 16, of which 14 were waited for; matrix products, arithmetic and copies ran while one was open for 9% of the time, Pallas kernels for 0%

commit v1 on v0

v1 whole, which is shorter than its diff:
```python
import jax
import jax.numpy as jnp
from jax import lax
from jax.sharding import PartitionSpec as P

D = 768
HEADS = 12
DK = 64
MICRO = 2
STEP = 5
SPAN = 28
MATRICES = 4


EPS = 1e-06
CLIP = 1.0
BETA_ONE = 0.9
BETA_TWO = 0.95
BETA_STATS = 0.95
ADAM_EPS = 1e-08
DECAY = 0.01
RATE_TABLE = 0.5
RATE_INNER = 0.01
RATE_GAIN = 0.2
RATE_BIAS = 0.3
RATE_ATTENTION = 0.01
NEGATIVE = -1000000000.0
HIGH = lax.Precision.HIGHEST


def to_low(values):
    return values.astype(jnp.bfloat16)


def to_full(values):
    return values.astype(jnp.float32)


def pick(values, index, axis):
    return lax.dynamic_index_in_dim(values, index, axis, False)


def swap_bit(value, bit):
    pairs = [(source, source ^ (1 << bit)) for source in range(lax.axis_size("section"))]
    return lax.ppermute(value, "section", pairs)


def section_bit(bit):
    return (lax.axis_index("section") >> bit) & 1


def swap_half(value):
    return lax.ppermute(value, "dp", [(0, 1), (1, 0)])


def to_decoder(value):
    return lax.ppermute(value, "dp", [(0, 1)])


def to_encoder(value):
    return lax.ppermute(value, "dp", [(1, 0)])


def sum_to_owner(values, axes):
    axes = list(axes)
    while axes:
        bit, axis = axes.pop(0)
        mine = section_bit(bit)
        arrived = swap_bit(to_low(pick(values, 1 - mine, axis)), bit)
        values = to_full(pick(values, mine, axis)) + to_full(arrived)
        axes = [(b, a - 1 if a > axis else a) for b, a in axes]
    return values


def forward_mul(left, right):
    return jnp.dot(left, right, preferred_element_type=jnp.float32)


def weight_grad(inputs, upstream):
    return jnp.einsum("nd,ne->de", inputs, upstream, preferred_element_type=jnp.float32)


def input_grad(upstream, weight):
    return jnp.einsum("ne,de->nd", upstream, weight, preferred_element_type=jnp.float32)


def rms_rows(values, gain_row):
    return values * lax.rsqrt(jnp.mean(values * values, -1, keepdims=True) + EPS) * gain_row


def final_rows(values, gain_row):
    return rms_rows(values, gain_row) * D ** (-0.5)


def norm_back(norm_rule, values, gain_row, upstream):
    result, pull = jax.vjp(norm_rule, values, gain_row)
    return pull(upstream)


def split_heads(values):
    return values.reshape(MICRO, -1, HEADS, DK)


def offset_square(row, length):
    width = 2 * length
    padded = jnp.pad(row, (0, width - row.shape[0]))
    flat = jnp.tile(padded, length)[length - 1 : length - 1 + length * (width - 1)]
    return flat.reshape(length, width - 1)[:, :length]


def position_table(onehot, bias_layer):
    return jnp.einsum("qkb,bh->hqk", onehot.astype(jnp.float32), bias_layer, precision=HIGH)


def score_block(query_heads, key_heads, bias_term, allowed):
    scores = jnp.einsum(
        "sqhd,skhd->shqk", query_heads, key_heads, preferred_element_type=jnp.float32
    ) * DK ** (-0.5)
    if bias_term is not None:
        scores = jnp.where(allowed, scores + bias_term[None], NEGATIVE)
    return scores


def attend_forward(query_heads, key_heads, value_heads, bias_term, allowed):
    scores = score_block(query_heads, key_heads, bias_term, allowed)
    row_peak = jnp.max(scores, -1, keepdims=True)
    log_total = row_peak + jnp.log(jnp.sum(jnp.exp(scores - row_peak), -1, keepdims=True))
    probs_low = to_low(jnp.exp(scores - log_total))
    mixed = jnp.einsum(
        "shqk,skhd->sqhd", probs_low, value_heads, preferred_element_type=jnp.float32
    )
    return (mixed, log_total)


def attend_backward(query_heads, key_heads, value_heads, bias_term, allowed, log_total, grad_mixed):
    scores = score_block(query_heads, key_heads, bias_term, allowed)
    probs = jnp.exp(scores - log_total)
    grad_probs = jnp.einsum(
        "sqhd,skhd->shqk", grad_mixed, value_heads, preferred_element_type=jnp.float32
    )
    grad_scores = to_low(probs * (grad_probs - jnp.sum(probs * grad_probs, -1, keepdims=True)))
    grad_value = jnp.einsum(
        "shqk,sqhd->skhd", to_low(probs), grad_mixed, preferred_element_type=jnp.float32
    )
    grad_query = jnp.einsum(
        "shqk,skhd->sqhd", grad_scores, key_heads, preferred_element_type=jnp.float32
    ) * DK ** (-0.5)
    grad_key = jnp.einsum(
        "shqk,sqhd->skhd", grad_scores, query_heads, preferred_element_type=jnp.float32
    ) * DK ** (-0.5)
    return (grad_query, grad_key, grad_value, grad_scores)


def attention_forward(resid, gain_row, weight_set, source, bias_term, allowed):
    normed = to_low(rms_rows(resid, gain_row))
    kv_input = normed if source is None else source
    query_rows = to_low(forward_mul(normed, weight_set[0]))
    key_rows = to_low(forward_mul(kv_input, weight_set[1]))
    value_rows = to_low(forward_mul(kv_input, weight_set[2]))
    mixed, log_total = attend_forward(
        split_heads(query_rows), split_heads(key_rows), split_heads(value_rows), bias_term, allowed
    )
    mixed_low = to_low(mixed.reshape(resid.shape))
    kept = (resid, normed, query_rows, key_rows, value_rows, mixed_low, log_total)
    return (resid + forward_mul(mixed_low, weight_set[3]), kept)


def attention_backward(grad_resid, kept, gain_row, weight_set, source, bias_term, allowed, onehot):
    resid, normed, query_rows, key_rows, value_rows, mixed_low, log_total = kept
    kv_input = normed if source is None else source
    grad_out = to_low(grad_resid)
    grad_mixed = to_low(input_grad(grad_out, weight_set[3]))
    grad_query, grad_key, grad_value, grad_scores = attend_backward(
        split_heads(query_rows),
        split_heads(key_rows),
        split_heads(value_rows),
        bias_term,
        allowed,
        log_total,
        split_heads(grad_mixed),
    )
    grad_query = to_low(grad_query.reshape(resid.shape))
    grad_key = to_low(grad_key.reshape(key_rows.shape))
    grad_value = to_low(grad_value.reshape(value_rows.shape))
    weight_grads = jnp.stack(
        [
            weight_grad(normed, grad_query),
            weight_grad(kv_input, grad_key),
            weight_grad(kv_input, grad_value),
            weight_grad(mixed_low, grad_out),
        ]
    )
    grad_normed = input_grad(grad_query, weight_set[0])
    source_grad = input_grad(grad_key, weight_set[1]) + input_grad(grad_value, weight_set[2])
    if source is None:
        grad_normed = grad_normed + source_grad
    grad_in, grad_gain = norm_back(rms_rows, resid, gain_row, grad_normed)
    bias_grad = None
    if bias_term is not None:
        bias_grad = jnp.einsum(
            "shqk,qkb->bh", grad_scores, onehot, preferred_element_type=jnp.float32
        )
    return (grad_resid + grad_in, grad_gain, weight_grads, source_grad, bias_grad)


def feed_forward(resid, gain_row, feed):
    normed = to_low(rms_rows(resid, gain_row))
    before = input_grad(normed, feed[0])
    active = to_low(jax.nn.gelu(before))
    return (resid + forward_mul(active, feed[1]), (resid, normed, before, active))


def feed_backward(grad_resid, kept, gain_row, feed):
    resid, normed, before, active = kept
    grad_out = to_low(grad_resid)
    grad_active = input_grad(grad_out, feed[1])
    result, pull = jax.vjp(jax.nn.gelu, before)
    grad_before = to_low(pull(grad_active)[0])
    grad_normed = forward_mul(grad_before, feed[0])
    grad_in, grad_gain = norm_back(rms_rows, resid, gain_row, grad_normed)
    feed_grads = jnp.stack([weight_grad(grad_before, normed), weight_grad(active, grad_out)])
    return (grad_resid + grad_in, grad_gain, feed_grads)


def adamw(weight, first, second, gradient, rate):
    first = BETA_ONE * first + (1 - BETA_ONE) * gradient
    second = BETA_TWO * second + (1 - BETA_TWO) * gradient * gradient
    stepped = first / (1 - BETA_ONE**STEP) / (jnp.sqrt(second / (1 - BETA_TWO**STEP)) + ADAM_EPS)
    return (first, second, weight - rate * (stepped + DECAY * weight))


def ordered(own, other, mine, axis):
    return jnp.where(
        mine == 0, jnp.stack([own, other], axis), jnp.stack([other, own], axis)
    )


def rows_to_matrix(rows):
    first, second = section_bit(0), section_bit(1)
    split = rows.reshape(2, 2, -1, D)
    arrived = swap_bit(pick(split, 1 - second, 1), 1)
    split = ordered(pick(split, second, 1), arrived, second, 1)
    arrived = swap_bit(pick(split, 1 - first, 0), 0)
    return ordered(pick(split, first, 0), arrived, first, 1).reshape(-1, D)


def matrix_to_rows(block):
    first, second = section_bit(0), section_bit(1)
    kinds, rows = block.shape[0], block.shape[1] // 4
    split = block.reshape(kinds, 2, 2, rows, D)
    arrived = swap_bit(pick(split, 1 - first, 2), 0)
    split = ordered(pick(split, first, 2), arrived, first, 1)
    arrived = swap_bit(pick(split, 1 - second, 2), 1)
    split = ordered(pick(split, second, 2), arrived, second, 2)
    return split.reshape(kinds, MATRICES, rows, D)


def gather_group(block):
    sections = lax.axis_size("section")
    groups = [list(range(low, sections, MATRICES)) for low in range(MATRICES)]
    return lax.all_gather(block, "section", axis=0, tiled=True, axis_index_groups=groups)


def sum_matrices(grads):
    bits = lax.axis_size("section").bit_length() - 1
    split = grads.reshape((2,) * bits + (-1, D))
    axes = [(0, 0), (1, 1)] + [(bit, 1 + bits - bit) for bit in range(2, bits)]
    return sum_to_owner(split, axes)


def sum_feed(grads):
    bits = lax.axis_size("section").bit_length() - 1
    split = grads.reshape((2,) + (2,) * bits + (-1, D))
    return sum_to_owner(split, [(bit, bits - bit) for bit in range(bits)])


def shampoo_terms(block, left_block, right_full):
    low = to_low(block)
    full = gather_group(low)
    rows = block.shape[0]
    start = (lax.axis_index("section") // MATRICES) * rows
    columns = lax.dynamic_slice_in_dim(full, start, rows, 1)
    blended = to_low(forward_mul(left_block, full))
    direction = forward_mul(blended, right_full)
    left_term = jnp.einsum("rd,ed->re", low, full, preferred_element_type=jnp.float32)
    right_term = jnp.einsum("dr,de->re", columns, full, preferred_element_type=jnp.float32)
    return matrix_to_rows(
        jnp.stack([low, to_low(direction), to_low(left_term), to_low(right_term)])
    )


def lookup_rows(ids, shard_low):
    sections = lax.axis_size("section")
    bits = sections.bit_length() - 1
    count = ids.shape[1]
    start = lax.axis_index("section") * shard_low.shape[0]
    split = (ids - start).reshape((2,) * bits + (count,))

    def owned(some_ids):
        hit = some_ids.reshape(-1, 1) == jnp.arange(shard_low.shape[0])[None, :]
        return to_low(forward_mul(hit.astype(jnp.bfloat16), shard_low))

    mine = section_bit(0)
    arrived = swap_bit(owned(pick(split, 1 - mine, bits - 1)), 0)
    rows = owned(pick(split, mine, bits - 1)) + arrived
    rows = rows.reshape((2,) * (bits - 1) + (count, D))
    for bit in range(1, bits):
        axis = bits - 1 - bit
        mine = section_bit(bit)
        arrived = swap_bit(pick(rows, 1 - mine, axis), bit)
        rows = pick(rows, mine, axis) + arrived
    return rows


def local(
    token_ids,
    targets,
    objective,
    buckets,
    table,
    table_first,
    table_second,
    inner_weight,
    inner_first,
    inner_second,
    outer_weight,
    outer_first,
    outer_second,
    gain_rows,
    gain_first,
    gain_second,
    position_bias,
    bias_first,
    bias_second,
    attention,
    left_stats,
    right_stats,
    left_roots,
    right_inverse_roots,
):
    sections = lax.axis_size("section")
    section_index = lax.axis_index("section")
    half = lax.axis_index("dp")
    is_encoder = half == 0
    is_decoder = half == 1
    length = token_ids.shape[-1]
    vocab_rows = table.shape[0]
    bits = sections.bit_length() - 1

    packed = jnp.concatenate(
        [token_ids.reshape(-1), targets.reshape(-1), objective.reshape(-1)]
    )
    every = lax.all_gather(packed, ("section", "dp")).reshape(sections, 2, -1).swapaxes(0, 1)
    every_tokens = every[:, :, : MICRO * length]
    every_targets = every[:, :, MICRO * length : (MICRO + 1) * length]
    every_objective = every[:, :, (MICRO + 1) * length]
    halves = sections // 2
    encoder_ids = every_tokens[:, :halves].reshape(sections, MICRO * length)
    decoder_ids = every_tokens[:, halves:].reshape(sections, MICRO * length)
    own_ids = jnp.where(is_encoder, encoder_ids, decoder_ids)

    def of_micro(values):
        return jnp.where(is_encoder, values[:, halves:], values[:, :halves])

    goal_ids = of_micro(every_targets).reshape(-1)
    goal_objective = of_micro(every_objective).reshape(sections)
    live_all = (
        jnp.arange(length)[None, :] < jnp.where(goal_objective == 1, length, SPAN)[:, None]
    ).astype(jnp.float32)
    live_rows = pick(live_all, section_index, 0)

    shard_low = to_low(table)
    attention_low = to_low(attention)
    self_shard = lax.dynamic_slice_in_dim(attention_low, half * MATRICES, MATRICES, 0)
    feed_shard = jnp.stack(
        [to_low(pick(inner_weight, half, 0).T), to_low(pick(outer_weight, half, 0))]
    )
    self_weights = lax.all_gather(self_shard, "section", axis=1, tiled=True)
    feed_weights = lax.all_gather(feed_shard, "section", axis=1, tiled=True)
    cross_weights = lax.all_gather(attention_low[8:12], "section", axis=1, tiled=True)

    bucket_square = offset_square(pick(buckets, half, 0), length)
    bucket_range = jnp.arange(position_bias.shape[1])
    onehot = (bucket_square[:, :, None] == bucket_range).astype(jnp.bfloat16)
    bias_term = position_table(onehot, pick(position_bias, half, 0))
    allowed = is_encoder | (jnp.arange(length)[:, None] >= jnp.arange(length)[None, :])

    resid = to_full(lookup_rows(own_ids, shard_low))
    gain_self = gain_rows[jnp.where(is_encoder, 0, 3)]
    gain_feed = gain_rows[jnp.where(is_encoder, 1, 5)]
    resid, kept_self = attention_forward(
        resid, gain_self, self_weights, None, bias_term, allowed
    )

    def encoder_rest():
        after, kept_feed = feed_forward(resid, gain_feed, feed_weights)
        return (to_low(rms_rows(after, gain_rows[2])), after, kept_feed)

    encoded, resid_enc, kept_feed = lax.cond(
        is_encoder, encoder_rest, lambda: jax.tree.map(jnp.zeros_like, encoder_rest())
    )
    arrived = to_decoder(encoded)

    def decoder_rest(kept_feed, resid_enc):
        after, kept_cross = attention_forward(
            resid, gain_rows[4], cross_weights, arrived, None, None
        )
        after, kept_feed = feed_forward(after, gain_feed, feed_weights)
        return (to_low(final_rows(after, gain_rows[6])), after, kept_feed, kept_cross)

    def decoder_skip(kept_feed, resid_enc):
        shapes = jax.eval_shape(decoder_rest, kept_feed, resid_enc)
        empty = jax.tree.map(lambda a: jnp.zeros(a.shape, a.dtype), shapes)
        return (empty[0], resid_enc, kept_feed, empty[3])

    final_low, resid_last, kept_feed, kept_cross = lax.cond(
        is_decoder, decoder_rest, decoder_skip, kept_feed, resid_enc
    )

    final_split = final_low.reshape(MICRO, length, D)
    handed = to_encoder(final_split[0])
    own_rows = jnp.where(is_encoder, handed, final_split[1])
    head_low = own_rows * live_rows[:, None].astype(jnp.bfloat16)
    all_rows = lax.all_gather(head_low, "section", axis=0, tiled=True)
    logits = jnp.einsum("nd,vd->nv", all_rows, shard_low, preferred_element_type=jnp.float32)
    goal_hit = (goal_ids - section_index * vocab_rows)[:, None] == jnp.arange(vocab_rows)[None, :]
    row_peak = jnp.max(logits, -1)
    row_total = jnp.sum(jnp.exp(logits - row_peak[:, None]), -1)
    goal_logit = jnp.sum(jnp.where(goal_hit, logits, 0.0), -1)
    every_stat = lax.all_gather(jnp.stack([row_peak, row_total]), "section")
    top_peak = jnp.max(every_stat[:, 0], 0)
    log_total = top_peak + jnp.log(
        jnp.sum(every_stat[:, 1] * jnp.exp(every_stat[:, 0] - top_peak), 0)
    )
    grad_logits = to_low(jnp.exp(logits - log_total[:, None]) - goal_hit.astype(jnp.float32))
    grad_all = forward_mul(grad_logits, shard_low)
    split_grad = grad_all.reshape((2,) * bits + (length, D))
    grad_head = sum_to_owner(split_grad, [(bit, bits - 1 - bit) for bit in range(bits)])
    grad_head = to_low(grad_head * live_rows[:, None])
    own_live = lax.dynamic_slice_in_dim(log_total, section_index * length, length, 0)
    loss_part = jnp.sum(live_rows * own_live) - jnp.sum(live_all.reshape(-1) * goal_logit)
    count_part = jnp.sum(live_rows)
    head_table = to_low(
        jnp.einsum("nv,nd->vd", grad_logits, all_rows, preferred_element_type=jnp.float32)
    )
    grad_final = jnp.stack([to_decoder(grad_head), grad_head]).reshape(MICRO * length, D)

    def decoder_back():
        grad_resid, gain_last = norm_back(
            final_rows, resid_last, gain_rows[6], to_full(grad_final)
        )
        grad_resid, gain_fed, feed_grads = feed_backward(
            grad_resid, kept_feed, gain_feed, feed_weights
        )
        grad_resid, gain_crossed, cross_grads, grad_source, unused = attention_backward(
            grad_resid, kept_cross, gain_rows[4], cross_weights, arrived, None, None, None
        )
        return (
            grad_resid,
            feed_grads,
            cross_grads,
            to_low(grad_source),
            gain_fed,
            gain_last,
            gain_crossed,
        )

    grad_resid, feed_grads, cross_grads, grad_source, gain_fed, gain_last, gain_crossed = lax.cond(
        is_decoder, decoder_back, lambda: jax.tree.map(jnp.zeros_like, decoder_back())
    )
    back_source = to_encoder(grad_source)

    def encoder_back(grad_resid, feed_grads, gain_fed, gain_last):
        grad_resid, gain_last = norm_back(
            rms_rows, resid_last, gain_rows[2], to_full(back_source)
        )
        grad_resid, gain_fed, feed_grads = feed_backward(
            grad_resid, kept_feed, gain_feed, feed_weights
        )
        return (grad_resid, feed_grads, gain_fed, gain_last)

    grad_resid, feed_grads, gain_fed, gain_last = lax.cond(
        is_encoder,
        encoder_back,
        lambda *same: same,
        grad_resid,
        feed_grads,
        gain_fed,
        gain_last,
    )
    grad_resid, gain_selfed, self_grads, unused, bias_grad = attention_backward(
        grad_resid, kept_self, gain_self, self_weights, None, bias_term, allowed, onehot
    )

    embed_low = to_low(grad_resid)
    both_rows = ordered(embed_low, swap_half(embed_low), half, 0)
    every_rows = lax.all_gather(both_rows, "section").reshape(-1, D)
    every_ids = jnp.stack([encoder_ids, decoder_ids], 1).reshape(-1)
    table_hit = (every_ids - section_index * vocab_rows)[None, :] == jnp.arange(vocab_rows)[:, None]
    head_both = to_full(head_table) + to_full(swap_half(head_table))
    table_grad = forward_mul(table_hit.astype(jnp.bfloat16), every_rows) + head_both

    feed_own = to_low(sum_feed(feed_grads))
    feed_both = to_full(ordered(feed_own, swap_half(feed_own), half, 1))
    inner_part = jnp.swapaxes(feed_both[0], 1, 2)
    outer_part = feed_both[1]

    left_self = lax.dynamic_slice_in_dim(left_roots, half * MATRICES, MATRICES, 0)
    right_self = lax.dynamic_slice_in_dim(right_inverse_roots, half * MATRICES, MATRICES, 0)
    cross_terms = shampoo_terms(
        sum_matrices(cross_grads),
        rows_to_matrix(left_roots[8:12]),
        gather_group(rows_to_matrix(right_inverse_roots[8:12])),
    )
    self_terms = shampoo_terms(
        sum_matrices(self_grads),
        rows_to_matrix(left_self),
        gather_group(rows_to_matrix(right_self)),
    )
    other_terms = swap_half(self_terms)
    cross_terms = jnp.where(is_encoder, to_encoder(cross_terms), cross_terms)
    terms = jnp.concatenate(
        [ordered(self_terms, other_terms, half, 1).reshape(4, 2 * MATRICES, -1, D), cross_terms], 1
    )
    attention_grad, direction, left_term, right_term = to_full(terms)

    gain_none = jnp.zeros_like(gain_selfed)
    gain_part = jnp.where(
        is_encoder,
        jnp.stack([gain_selfed, gain_fed, gain_last] + [gain_none] * 4),
        jnp.stack([gain_none] * 3 + [gain_selfed, gain_crossed, gain_fed, gain_last]),
    )
    bias_part = jnp.stack([jnp.where(half == layer, bias_grad, 0.0) for layer in range(2)])
    gain_full, bias_full = lax.psum((gain_part, bias_part), ("section", "dp"))

    square_sum = (
        jnp.sum(table_grad * table_grad)
        + jnp.sum(inner_part * inner_part)
        + jnp.sum(outer_part * outer_part)
        + jnp.sum(attention_grad * attention_grad)
    )
    small_square = jnp.sum(gain_full * gain_full) + jnp.sum(bias_full * bias_full)
    sums = jnp.concatenate(
        [
            jnp.stack([loss_part, count_part, 0.5 * square_sum]),
            0.5 * jnp.sum(direction * direction, (1, 2)),
        ]
    )
    sums = lax.psum(sums, ("section", "dp"))
    grad_norm = jnp.sqrt(sums[2] + small_square)
    clip_factor = CLIP / jnp.maximum(grad_norm, CLIP)
    table_out = adamw(table, table_first, table_second, table_grad * clip_factor, RATE_TABLE)
    inner_out = adamw(inner_weight, inner_first, inner_second, inner_part * clip_factor, RATE_INNER)
    outer_out = adamw(outer_weight, outer_first, outer_second, outer_part * clip_factor, RATE_INNER)
    gain_out = adamw(gain_rows, gain_first, gain_second, gain_full * clip_factor, RATE_GAIN)
    bias_out = adamw(position_bias, bias_first, bias_second, bias_full * clip_factor, RATE_BIAS)
    clip_square = clip_factor * clip_factor
    left_new = BETA_STATS * left_stats + (1 - BETA_STATS) * clip_square * left_term
    right_new = BETA_STATS * right_stats + (1 - BETA_STATS) * clip_square * right_term
    spread = jnp.sqrt(sums[3:] / (D * D) + EPS)[:, None, None]
    attention_new = attention - RATE_ATTENTION * (direction / spread + DECAY * attention)
    return (
        sums[0],
        sums[1],
        grad_norm,
        *table_out,
        *inner_out,
        *outer_out,
        *gain_out,
        *bias_out,
        attention_grad * clip_factor,
        left_new,
        right_new,
        attention_new,
    )


def solution(mesh):
    in_specs = (
        P("dp", "section", None, None),
        P("dp", "section", None),
        P("dp", "section"),
        P(),
        P("section", None),
        P("section", None),
        P("section", None),
        P(None, None, "section"),
        P(None, None, "section"),
        P(None, None, "section"),
        P(None, "section", None),
        P(None, "section", None),
        P(None, "section", None),
        P(),
        P(),
        P(),
        P(),
        P(),
        P(),
        P(None, "section", None),
        P(None, "section", None),
        P(None, "section", None),
        P(None, "section", None),
        P(None, "section", None),
    )
    out_specs = (
        P(),
        P(),
        P(),
        P("section", None),
        P("section", None),
        P("section", None),
        P(None, None, "section"),
        P(None, None, "section"),
        P(None, None, "section"),
        P(None, "section", None),
        P(None, "section", None),
        P(None, "section", None),
        P(),
        P(),
        P(),
        P(),
        P(),
        P(),
        P(None, "section", None),
        P(None, "section", None),
        P(None, "section", None),
        P(None, "section", None),
    )
    return jax.shard_map(local, mesh=mesh, in_specs=in_specs, out_specs=out_specs, check_vma=False)
```

time: 3610 us -> 1110 us (0.31)
  waiting for transfers between devices: 2370 us -> 596 us
  local copies, waits for them, and re-layouts: 446 us -> 80.5 us
  starting transfers between devices: 216 us -> 23.8 us
  other arithmetic: 211 us -> 111 us
  matrix products: 202 us -> 152 us
    unnamed x13 -> x9, waiting for transfers between devices: 830 us -> 0.15 us
    psum x2 -> x0, waiting for transfers between devices: 579 us -> none  [the longest x1 383 us: local(): lax.psum((attention_grad, gain_grad, bias_grad), ('section', 'dp'))]
    ppermute x4 -> x41, waiting for transfers between devices: 48.2 us -> 548 us  [the longest x32 364 us: swap_bit(): return lax.ppermute(value, 'section', pairs)]
    reduce_scatter x3 -> x0, waiting for transfers between devices: 463 us -> none  [the longest x1 198 us: local(): lax.psum_scatter(inner_grad, 'section', scatter_dimension=2, tiled=True)]
    all_gather x5 -> x8, waiting for transfers between devices: 400 us -> 1.29 us  [the longest x1 1.2 us: local(): lax.all_gather(attention_low[8:12], 'section', axis=1, tiled=True)]
    gather x6 -> x0, local copies, waits for them, and re-layouts: 209 us -> none  [the longest x2 102 us: local(): buckets[1][offsets][:, :, None] == bucket_range]
    ppermute x4 -> x41, starting transfers between devices: 216 us -> 23 us  [the longest x32 14.3 us: swap_bit(): return lax.ppermute(value, 'section', pairs)]
    dot_general x7 -> x6, matrix products: 131 us -> 30 us  [the longest x1 13.3 us: local(): jnp.einsum('nv,nd->vd', grad_logits, all_rows, preferred_element_type=jnp...]
  transfers between devices with their start and end apart: 16 -> 50, of which waited for: 14 -> 33; matrix products, arithmetic and copies ran while one was open for 9% -> 18% of each run, Pallas kernels for 0% -> 0%
where the time goes in v1:
time: 1110 us; the launch traced here: 1100 us
  waiting for transfers between devices  596 us (54%)
  matrix products  152 us (14%)
  other arithmetic  111 us (10%)
  blocking collectives  104 us (9%)
  local copies, waits for them, and re-layouts  80.5 us (7%)
  between operations  24 us (2%)
  starting transfers between devices  23.8 us (2%)
    ppermute x32, waiting for transfers between devices, swap_bit(): return lax.ppermute(value, 'section', pairs)  364 us
    ppermute x3, waiting for transfers between devices, to_encoder(): return lax.ppermute(value, 'dp', [(1, 0)])  136 us
    dot_general x12, matrix products, forward_mul(): return jnp.dot(left, right, preferred_element_type=jnp.float32)  84.3 us
    all_gather x1, waiting for transfers between devices, local(): all_rows = lax.all_gather(head_low, 'section', axis=0, tiled=True)  47.2 us
    unnamed x1, blocking collectives  43.5 us
    psum x1, blocking collectives, local(): sums = lax.psum(sums, ('section', 'dp'))  39.8 us
    ppermute x4, waiting for transfers between devices, swap_half(): return lax.ppermute(value, 'dp', [(0, 1), (1, 0)])  39.3 us
    sub x5, other arithmetic, adamw(): return (first, second, weight - rate * (stepped + DECAY * weight))  26.6 us
  transfers between devices with their start and end apart: 50, of which 33 were waited for; matrix products, arithmetic and copies ran while one was open for 18% of the time, Pallas kernels for 0%

profile of v1, /device:TPU:0, one launch (start us, length us, event | category | flops | bytes accessed | tf_op | source)
XLA Modules:
  0.0 1098.5 jit_solution(10356424308054654280)
XLA Ops:
  13.8 43.5 %all-reduce.1 = s32[12320]{0:T(1024)S(1)} all-reduce(s32[12320]{0:T(1024)S(1)} %add_dynamic-update-slice_fusion), channel_id=2, replica_groups=mesh['section'=16,'dp'=2] {'section','dp'}, use_global_device_ids=true, to_apply=%add.1 | all-reduce | flops 12320 | bytes 98560
  58.7 3.1 convert_element_type.446
  61.8 8.7 fusion.145
  70.6 5.9 collective-permute-done
  76.5 9.3 fusion.150
  89.8 53.3 %collective-permute-done.1 = bf16[2,2,256,768]{3,2,1,0:T(8,128)(2,1)S(1)} collective-permute-done((bf16[2,2,256,768]{3,2,1,0:T(8,128)(2,1)S(1)}, bf16[2,2,256,768]{3,2,1,0:T(8,128)(2,1)S(1)}, u32[]{:S(2)}, u32[]{:S(2)}) %collective-permute-start.1) | collective-permute-done | bytes 1572896 | tf_op jit(solution)/shard_map/ppermute | solution.py:45
  147.8 30.2 %collective-permute-done.2 = bf16[2,256,768]{2,1,0:T(8,128)(2,1)S(1)} collective-permute-done((bf16[2,256,768]{2,1,0:T(8,128)(2,1)S(1)}, bf16[2,256,768]{2,1,0:T(8,128)(2,1)S(1)}, u32[]{:S(2)}, u32[]{:S(2)}) %collective-permute-start.2) | collective-permute-done | bytes 786464 | tf_op jit(solution)/shard_map/ppermute | solution.py:45
  185.6 22.1 %collective-permute-done.3 = bf16[256,768]{1,0:T(8,128)(2,1)S(1)} collective-permute-done((bf16[256,768]{1,0:T(8,128)(2,1)}, bf16[256,768]{1,0:T(8,128)(2,1)S(1)}, u32[]{:S(2)}, u32[]{:S(2)}) %collective-permute-start.3) | collective-permute-done | bytes 393248 | tf_op jit(solution)/shard_map/ppermute | solution.py:45
  219.3 14.3 %conditional.4 = (bf16[256,768]{1,0:T(8,128)(2,1)S(1)}, f32[256,768]{1,0:T(8,128)}, f32[256,768]{1,0:T(8,128)}, bf16[256,768]{1,0:T(8,128)(2,1)}, f32[256,3072]{1,0:T(8,128)}, /*index=5*/bf16[256,3072]{1,0:T(8,128)(2,1)}) conditional(s32[]{:T(128)} %convert_element_type.445, () %tuple.55, (f32[256,768]{1,0:T(8,128)S(1)}, f32[1,768]{1,0:T(1,128)S(1)}, ...), branch_computations={%region_3.4_spmd, %region_4.7_spmd} | conditional | flops 2425160192 | bytes 52324504 | solution.py:399
  221.3 7.1 fusion.13
  228.4 3.7 multiply_reduce_fusion
  237.1 3.6 collective-permute-done.4
  240.7 3.8 conditional.5
  245.9 28.7 %collective-permute-done.5 = bf16[128,768]{1,0:T(8,128)(2,1)S(1)} collective-permute-done((bf16[128,768]{1,0:T(8,128)(2,1)S(1)}, bf16[128,768]{1,0:T(8,128)(2,1)S(1)}, u32[]{:S(2)}, u32[]{:S(2)}) %collective-permute-start.5) | collective-permute-done | bytes 196640 | tf_op jit(solution)/shard_map/ppermute | solution.py:61
  276.5 47.2 %all-gather.19.cloned.1.call-done = bf16[2048,768]{1,0:T(8,128)(2,1)} async-done(((bf16[128,768]{1,0:T(8,128)(2,1)}), bf16[2048,768]{1,0:T(8,128)(2,1)}) %all-gather.19.cloned.1.call-update) | async-done | bytes 3145744 | tf_op jit(solution)/shard_map/all_gather | solution.py:424
  323.7 9.6 fusion.269
  333.3 6.0 select_reduce_fusion
  339.3 20.4 %all-gather.2 = f32[16,2,2048]{2,1,0:T(2,128)S(1)} all-gather(f32[1,2,2048]{2,1,0:T(2,128)S(1)} %maximum_bitcast_fusion), channel_id=3, replica_groups=mesh['section'=16,'dp'=2] {'section'}, dimensions={0}, use_global_device_ids=true | all-gather | bytes 278528 | tf_op jit(solution)/shard_map/all_gather | solution.py:430
  360.1 9.8 fusion.223
  372.4 3.1 collective-permute-done.6
  378.0 19.8 %collective-permute-done.7 = bf16[2,2,128,768]{3,2,0,1:T(8,128)(2,1)S(1)} collective-permute-done((bf16[2,2,128,768]{3,2,0,1:T(8,128)(2,1)S(1)}, bf16[2,2,128,768]{3,2,0,1:T(8,128)(2,1)S(1)}, u32[]{:S(2)}, u32[]{:S(2)}) %collective-permute-start.7) | collective-permute-done | bytes 786464 | tf_op jit(solution)/shard_map/ppermute | solution.py:45
  398.2 10.6 collective-permute-done.8
  408.9 10.5 collective-permute-done.9
  419.6 3.1 collective-permute-start.10
  422.7 4.3 collective-permute-done.10
  427.0 16.5 %conditional.6 = (f32[256,768]{1,0:T(8,128)S(1)}, f32[2,3072,768]{2,1,0:T(8,128)}, bf16[256,768]{1,0:T(8,128)(2,1)S(1)}, f32[768]{0:T(1024)S(1)}, f32[768]{0:T(1...) conditional(s32[]{:T(128)} %convert_element_type.444, () %tuple.59, ...), branch_computations={%region_22.23_spmd, %region_23.34_spmd} | conditional | flops 7541096448 | bytes 231739104 | solution.py:468
  429.2 7.6 broadcast.455
  448.8 45.7 %collective-permute-done.11 = bf16[256,768]{1,0:T(8,128)(2,1)S(1)} collective-permute-done((bf16[256,768]{1,0:T(8,128)(2,1)S(1)}, bf16[256,768]{1,0:T(8,128)(2,1)S(1)}, u32[]{:S(2)}, u32[]{:S(2)}) %collective-permute-start.11) | collective-permute-done | bytes 393248 | tf_op jit(solution)/shard_map/ppermute | solution.py:61
  494.5 43.9 %conditional.7 = (f32[256,768]{1,0:T(8,128)S(1)}, f32[2,2,2,2,2,192,768]{6,5,4,3,2,1,0:T(8,128)}, f32[768]{0:T(1024)S(1)}, f32[768]{0:T(1024)}) conditional(s32[]{:T(128)} %convert_element_type.445, (f32[2,3072,768]{2,1,0:T(8,128)}, f32[256,768]{1,0:T(8,128)S(1)}, f32[768]{0:T(1024)S(1)}, f32[768]{0:T(1024)}) %tuple.153, ...), branch_computations={%region_34.35_spmd, %region_35.42_spmd} | conditional | flops 4860741120 | bytes 183706848 | solution.py:482
  499.1 6.4 fusion.125
  505.6 3.8 multiply_reduce_fusion.14
  511.1 6.9 convolution_bitcast_fusion.6
  517.9 9.7 copy.336
  531.3 6.7 pad_maximum_fusion.2
  548.0 3.6 bitcast_add_fusion.1
  556.9 21.2 %collective-permute-done.31 = bf16[2,2,192,768]{3,2,1,0:T(8,128)(2,1)S(1)} collective-permute-done((bf16[2,2,192,768]{3,2,1,0:T(8,128)(2,1)S(1)}, bf16[2,2,192,768]{3,2,1,0:T(8,128)(2,1)S(1)}, u32[]{:S(2)}, u32[]{:S(2)}) %collective-permute-start.31) | collective-permute-done | bytes 1179680 | tf_op jit(solution)/shard_map/ppermute | solution.py:45
  578.6 12.8 %collective-permute-done.32 = bf16[2,192,768]{2,1,0:T(8,128)(2,1)S(1)} collective-permute-done((bf16[2,192,768]{2,1,0:T(8,128)(2,1)S(1)}, bf16[2,192,768]{2,1,0:T(8,128)(2,1)S(1)}, u32[]{:S(2)}, u32[]{:S(2)}) %collective-permute-start.32) | collective-permute-done | bytes 589856 | tf_op jit(solution)/shard_map/ppermute | solution.py:45
  591.6 12.8 %collective-permute-done.33 = bf16[192,768]{1,0:T(8,128)(2,1)S(1)} collective-permute-done((bf16[192,768]{1,0:T(8,128)(2,1)S(1)}, bf16[192,768]{1,0:T(8,128)(2,1)S(1)}, u32[]{:S(2)}, u32[]{:S(2)}) %collective-permute-start.33) | collective-permute-done | bytes 294944 | tf_op jit(solution)/shard_map/ppermute | solution.py:45
  605.3 3.7 bitcast_add_fusion.2
  613.4 26.8 %collective-permute-done.36 = bf16[2,48,768]{2,1,0:T(8,128)(2,1)S(1)} collective-permute-done((bf16[2,48,768]{2,1,0:T(8,128)(2,1)}, bf16[2,48,768]{2,1,0:T(8,128)(2,1)S(1)}, u32[]{:S(2)}, u32[]{:S(2)}) %collective-permute-start.36) | collective-permute-done | bytes 147488 | tf_op jit(solution)/shard_map/ppermute | solution.py:45
  648.6 33.4 %collective-permute-done.21 = bf16[2,192,768]{2,1,0:T(8,128)(2,1)S(1)} collective-permute-done((bf16[2,192,768]{2,1,0:T(8,128)(2,1)S(1)}, bf16[2,192,768]{2,1,0:T(8,128)(2,1)S(1)}, u32[]{:S(2)}, u32[]{:S(2)}) %collective-permute-start.21) | collective-permute-done | bytes 589856 | tf_op jit(solution)/shard_map/ppermute | solution.py:45
  682.3 12.3 %collective-permute-done.22 = bf16[192,768]{1,0:T(8,128)(2,1)S(1)} collective-permute-done((bf16[192,768]{1,0:T(8,128)(2,1)S(1)}, bf16[192,768]{1,0:T(8,128)(2,1)S(1)}, u32[]{:S(2)}, u32[]{:S(2)}) %collective-permute-start.22) | collective-permute-done | bytes 294944 | tf_op jit(solution)/shard_map/ppermute | solution.py:45
  695.6 5.1 collective-permute-done.25
  709.2 11.1 %collective-permute-done.12 = bf16[256,768]{1,0:T(8,128)(2,1)S(1)} collective-permute-done((bf16[256,768]{1,0:T(8,128)(2,1)S(1)}, bf16[256,768]{1,0:T(8,128)(2,1)S(1)}, u32[]{:S(2)}, u32[]{:S(2)}) %collective-permute-start.12) | collective-permute-done | bytes 393248 | tf_op jit(solution)/shard_map/ppermute | solution.py:53
  721.4 6.5 fusion.144
  730.0 4.5 collective-permute-done.34
  739.6 6.2 bitcast_add_fusion
  745.8 3.7 copy-done.6
  757.5 2.9 convolution_convert_fusion.17
  772.0 50.3 %collective-permute-done.15 = bf16[2,2,2,192,768]{4,3,0,1,2:T(8,128)(2,1)} collective-permute-done((bf16[2,2,2,192,768]{4,3,0,1,2:T(8,128)(2,1)}, bf16[2,2,2,192,768]{4,3,0,1,2:T(8,128)(2,1)}, u32[]{:S(2)}, u32[]{:S(2)}) %collective-permute-start.15) | collective-permute-done | bytes 2359328 | tf_op jit(solution)/shard_map/ppermute | solution.py:45
  822.3 3.9 bitcast_add_fusion.3
  829.1 13.3 %convolution_convert_fusion.6 = bf16[2008,768]{1,0:T(8,128)(2,1)} fusion(bf16[2048,768]{1,0:T(8,128)(2,1)S(1)} %copy-done.105, f32[2048,2008]{0,1:T(8,128)} %copy-done.9, f32[2048]{0:T(1024)S(1)} %copy-done.92, s32[2048]{0:T(1024)S(1)} %copy-done.80), kind=kOutput, calls=%fused_computation.246 | convolution fusion | flops 6338725888 | bytes 22695936 | tf_op jit(solution)/shard_map/nv,nd->vd/dot_general | solution.py:444
  843.2 4.3 collective-permute-done.39
  852.8 19.1 %collective-permute-done.28 = bf16[4,2,48,768]{3,2,1,0:T(8,128)(2,1)S(1)} collective-permute-done((bf16[4,2,48,768]{3,2,1,0:T(8,128)(2,1)}, bf16[4,2,48,768]{3,2,1,0:T(8,128)(2,1)S(1)}, u32[]{:S(2)}, u32[]{:S(2)}) %collective-permute-start.28) | collective-permute-done | bytes 589856 | tf_op jit(solution)/shard_map/ppermute | solution.py:45
  875.9 61.8 %collective-permute-done.40 = bf16[4,4,48,768]{3,2,1,0:T(8,128)(2,1)} collective-permute-done((bf16[4,4,48,768]{3,2,1,0:T(8,128)(2,1)S(1)}, bf16[4,4,48,768]{3,2,1,0:T(8,128)(2,1)}, u32[]{:S(2)}, u32[]{:S(2)}) %collective-permute-start.40) | collective-permute-done | bytes 1179680 | tf_op jit(solution)/shard_map/ppermute | solution.py:61
  939.2 19.9 %collective-permute-done.29 = bf16[4,4,48,768]{3,2,1,0:T(8,128)(2,1)S(1)} collective-permute-done((bf16[4,4,48,768]{3,2,1,0:T(8,128)(2,1)S(1)}, bf16[4,4,48,768]{3,2,1,0:T(8,128)(2,1)S(1)}, u32[]{:S(2)}, u32[]{:S(2)}) %collective-permute-start.29) | collective-permute-done | bytes 1179680 | tf_op jit(solution)/shard_map/ppermute | solution.py:53
  963.0 8.3 collective-permute-done.18
  972.5 36.6 %multiply_reduce_fusion.18 = (f32[]{:T(128)}, f32[2008,768]{1,0:T(8,128)}) fusion(bf16[2008,768]{1,0:T(8,128)(2,1)} %collective-permute-done.13, bf16[2008,768]{1,0:T(8,128)(2,1)} %convolution_convert_fusion.6, bf16[8192,768]{1,0:T(8,128)(2,1)} %bitcast.651, s32[8192]{0:T(1024)S(1)} %bitcast.643), kind=kOutput, calls=%fused_computation.234 | convolution fusion | flops 25292189696 | bytes 24952836 | tf_op jit(solution)/shard_map/dot_general | solution.py:76
  1012.5 39.8 %all-reduce.2 = (f32[15]{0:T(128)S(1)}, f32[7,768]{1,0:T(8,128)S(1)}, f32[2,32,12]{1,2,0:T(8,128)S(1)}) all-reduce(f32[15]{0:T(128)S(1)} %pad_maximum_fusion.9, f32[7,768]{1,0:T(8,128)S(1)} %maximum_select_fusion.15, f32[2,32,12]{1,2,0:T(8,128)S(1)} %pad_maximum_fusion.8), channel_id=1, replica_groups=mesh['section'=16,'dp'=2] {'section','dp'}, use_global_device_ids=true, to_apply=%region_49.50 | all-reduce | flops 6159 | bytes 49272 | tf_op jit(solution)/shard_map/psum | solution.py:549
  1056.3 2.8 multiply_bitcast_fusion
  1061.7 4.6 multiply_subtract_fusion.3
  1066.2 4.9 multiply_subtract_fusion.2
  1071.1 2.7 multiply_subtract_fusion.1
  1073.8 16.5 %multiply_subtract_fusion = (f32[2008,768]{1,0:T(8,128)}, f32[2008,768]{1,0:T(8,128)}, f32[2008,768]{1,0:T(8,128)}) fusion(f32[2008,768]{1,0:T(8,128)S(1)} %bitcast.571, f32[]{:T(128)S(6)} %div.192, f32[2008,768]{1,0:T(8,128)} %get-tuple-element.589, bf16[2008,768]{1,0:T(8,128)(2,1)} %collective-permute-done.13, ...), kind=kLoop, calls=%fused_computation.232 | loop fusion | flops 30842880 | bytes 49348612 | tf_op jit(solution)/shard_map/sub | solution.py:229
  (481 shorter events, 161.5 us)
Async XLA Ops:
  7.2 139.4 %copy-start = (s32[2,255]{1,0:T(2,128)S(1)}, s32[2,255]{1,0:T(2,128)}, u32[]{:S(2)}) copy-start(s32[2,255]{1,0:T(2,128)} %param.35) | copy-start | bytes 6124
  7.2 200.8 %all-gather.13.cloned.1.call-start = ((), (), s32[]{:S(2)}) async-start(), calls=%async_computation | async-start | bytes 5013504 | tf_op jit(solution)/shard_map/all_gather | solution.py:378
  9.7 209.5 %all-gather.15.cloned.1.call-start = ((), (), s32[]{:S(2)}) async-start(), calls=%async_computation.1 | async-start | bytes 10027008 | tf_op jit(solution)/shard_map/all_gather | solution.py:379
  12.9 224.2 %all-gather.17.cloned.1.call-start = ((), (), s32[]{:S(2)}) async-start(), calls=%async_computation.2 | async-start | bytes 5013504 | tf_op jit(solution)/shard_map/all_gather | solution.py:380
  70.5 6.0 collective-permute-start
  70.5 253.2 %all-gather.19.cloned.1.call-start = ((), (), s32[]{:S(2)}) async-start(), calls=%async_computation.3 | async-start | bytes 3342336 | tf_op jit(solution)/shard_map/all_gather | solution.py:424
  87.6 55.5 %collective-permute-start.1 = (bf16[2,2,256,768]{3,2,1,0:T(8,128)(2,1)S(1)}, bf16[2,2,256,768]{3,2,1,0:T(8,128)(2,1)S(1)}, u32[]{:S(2)}, u32[]{:S(2)}) collective-permute-start(bf16[2,2,256,768]{3,2,1,0:T(8,128)(2,1)S(1)} %dynamic-slice_bitcast_fusion), channel_id=1, source_target_pairs={{0,4},{2,6},{4,0},{6,2},{8,12},{10,14},{12,8},{14,10},{16,20},{18,... | collective-permute-start | bytes 4718600 | tf_op jit(solution)/shard_map/ppermute | solution.py:45
  144.9 33.2 %collective-permute-start.2 = (bf16[2,256,768]{2,1,0:T(8,128)(2,1)S(1)}, bf16[2,256,768]{2,1,0:T(8,128)(2,1)S(1)}, u32[]{:S(2)}, u32[]{:S(2)}) collective-permute-start(bf16[2,256,768]{2,1,0:T(8,128)(2,1)S(1)} %dynamic-slice_bitcast_fusion.1), channel_id=1, source_target_pairs={{0,8},{2,10},{4,12},{6,14},{8,0},{10,2},{12,4},{14,6},{16,24},{18,... | collective-permute-start | bytes 2359304 | tf_op jit(solution)/shard_map/ppermute | solution.py:45
  146.6 34.0 %copy-start.75 = (f32[2,32,12]{1,0,2:T(2,128)S(1)}, f32[2,32,12]{1,0,2:T(2,128)}, u32[]{:S(2)}) copy-start(f32[2,32,12]{1,0,2:T(2,128)} %param.48) | copy-start | bytes 9220
  147.8 32.5 %copy-start.64 = (s32[128,128]{0,1:T(8,128)S(1)}, s32[128,128]{0,1:T(8,128)}, u32[]{:S(2)}) copy-start(s32[128,128]{0,1:T(8,128)} %copy.347) | copy-start | bytes 196612
  178.9 28.8 %collective-permute-start.3 = (bf16[256,768]{1,0:T(8,128)(2,1)}, bf16[256,768]{1,0:T(8,128)(2,1)S(1)}, u32[]{:S(2)}, u32[]{:S(2)}) collective-permute-start(bf16[256,768]{1,0:T(8,128)(2,1)} %dynamic-slice_bitcast_fusion.8), channel_id=1, source_target_pairs={{0,16},{2,18},{4,20},{6,22},{8,24},{10,26},{12,28},{14,30},{16,0},... | collective-permute-start | bytes 1179656 | tf_op jit(solution)/shard_map/ppermute | solution.py:45
  233.5 7.1 collective-permute-start.4
  244.5 30.1 %collective-permute-start.5 = (bf16[128,768]{1,0:T(8,128)(2,1)S(1)}, bf16[128,768]{1,0:T(8,128)(2,1)S(1)}, u32[]{:S(2)}, u32[]{:S(2)}) collective-permute-start(bf16[128,768]{1,0:T(8,128)(2,1)S(1)} %slice.169), channel_id=1, source_target_pairs={{1,0},{3,2},{5,4},{7,6},{9,8},{11,10},{13,12},{15,14},{17,16},{19,... | collective-permute-start | bytes 589832 | tf_op jit(solution)/shard_map/ppermute | solution.py:61
  245.9 87.4 %copy-start.100 = (pred[16,128]{1,0:T(8,128)(4,1)}, pred[16,128]{1,0:T(8,128)(4,1)S(1)}, u32[]{:S(2)}) copy-start(pred[16,128]{1,0:T(8,128)(4,1)S(1)} %iota_compare_fusion.15) | copy-start | bytes 6148
  245.9 173.5 %copy-start.97 = (f32[128]{0:T(128)}, f32[128]{0:T(128)S(1)}, u32[]{:S(2)}) copy-start(f32[128]{0:T(128)S(1)} %get-tuple-element.510) | copy-start | bytes 1540
  275.4 476.0 %all-gather.27.cloned.1.call-start = ((), (), s32[]{:S(2)}) async-start(), calls=%async_computation.7 | async-start | bytes 1474560 | tf_op jit(solution)/shard_map/all_gather | solution.py:261
  276.5 83.6 %copy-start.79 = (s32[2048]{0:T(1024)}, s32[2048]{0:T(1024)S(1)}, u32[]{:S(2)}) copy-start(s32[2048]{0:T(1024)S(1)} %fusion.242) | copy-start | bytes 24580
  372.0 3.5 collective-permute-start.6
  378.0 19.9 %collective-permute-start.7 = (bf16[2,2,128,768]{3,2,0,1:T(8,128)(2,1)S(1)}, bf16[2,2,128,768]{3,2,0,1:T(8,128)(2,1)S(1)}, u32[]{:S(2)}, u32[]{:S(2)}) collective-permute-start(bf16[2,2,128,768]{3,2,0,1:T(8,128)(2,1)S(1)} %fusion.184), channel_id=1, source_target_pairs={{0,4},{2,6},{4,0},{6,2},{8,12},{10,14},{12,8},{14,10},{16,20},{18,... | collective-permute-start | bytes 2359304 | tf_op jit(solution)/shard_map/ppermute | solution.py:45
  398.1 10.6 collective-permute-start.8
  408.9 10.6 collective-permute-start.9
  419.6 7.4 collective-permute-start.10
  443.6 50.9 %collective-permute-start.11 = (bf16[256,768]{1,0:T(8,128)(2,1)S(1)}, bf16[256,768]{1,0:T(8,128)(2,1)S(1)}, u32[]{:S(2)}, u32[]{:S(2)}) collective-permute-start(bf16[256,768]{1,0:T(8,128)(2,1)S(1)} %get-tuple-element.227), channel_id=1, source_target_pairs={{1,0},{3,2},{5,4},{7,6},{9,8},{11,10},{13,12},{15,14},{17,16},{19,... | collective-permute-start | bytes 1179656 | tf_op jit(solution)/shard_map/ppermute | solution.py:61
  447.2 47.3 %copy-start.21 = (bf16[256,768]{1,0:T(8,128)(2,1)S(1)}, bf16[256,768]{1,0:T(8,128)(2,1)}, u32[]{:S(2)}) copy-start(bf16[256,768]{1,0:T(8,128)(2,1)} %get-tuple-element.219) | copy-start | bytes 1179652
  448.8 99.2 %collective-permute-start.30 = (bf16[2,2,2,192,768]{4,3,2,1,0:T(8,128)(2,1)}, bf16[2,2,2,192,768]{4,3,2,1,0:T(8,128)(2,1)}, u32[]{:S(2)}, u32[]{:S(2)}) collective-permute-start(bf16[2,2,2,192,768]{4,3,2,1,0:T(8,128)(2,1)} %fusion.149), channel_id=1, source_target_pairs={{0,2},{2,0},{4,6},{6,4},{8,10},{10,8},{12,14},{14,12},{16,18},{18,... | collective-permute-start | bytes 7077896 | tf_op jit(solution)/shard_map/ppermute | solution.py:45
  551.8 26.4 %collective-permute-start.31 = (bf16[2,2,192,768]{3,2,1,0:T(8,128)(2,1)S(1)}, bf16[2,2,192,768]{3,2,1,0:T(8,128)(2,1)S(1)}, u32[]{:S(2)}, u32[]{:S(2)}) collective-permute-start(bf16[2,2,192,768]{3,2,1,0:T(8,128)(2,1)S(1)} %fusion.168), channel_id=1, source_target_pairs={{0,4},{2,6},{4,0},{6,2},{8,12},{10,14},{12,8},{14,10},{16,20},{18,... | collective-permute-start | bytes 3538952 | tf_op jit(solution)/shard_map/ppermute | solution.py:45
  555.0 36.5 %copy-start.7 = (f32[4,768,768]{2,1,0:T(8,128)}, f32[4,768,768]{2,1,0:T(8,128)S(1)}, u32[]{:S(2)}) copy-start(f32[4,768,768]{2,1,0:T(8,128)S(1)} %pad_maximum_fusion.3) | copy-start | bytes 28311556
  556.9 48.3 %collective-permute-start.19 = (bf16[2,2,2,192,768]{4,3,2,1,0:T(8,128)(2,1)}, bf16[2,2,2,192,768]{4,3,2,1,0:T(8,128)(2,1)}, u32[]{:S(2)}, u32[]{:S(2)}) collective-permute-start(bf16[2,2,2,192,768]{4,3,2,1,0:T(8,128)(2,1)} %fusion.148), channel_id=1, source_target_pairs={{0,2},{2,0},{4,6},{6,4},{8,10},{10,8},{12,14},{14,12},{16,18},{18,... | collective-permute-start | bytes 7077896 | tf_op jit(solution)/shard_map/ppermute | solution.py:45
  578.5 12.9 %collective-permute-start.32 = (bf16[2,192,768]{2,1,0:T(8,128)(2,1)S(1)}, bf16[2,192,768]{2,1,0:T(8,128)(2,1)S(1)}, u32[]{:S(2)}, u32[]{:S(2)}) collective-permute-start(bf16[2,192,768]{2,1,0:T(8,128)(2,1)S(1)} %fusion.187), channel_id=1, source_target_pairs={{0,8},{2,10},{4,12},{6,14},{8,0},{10,2},{12,4},{14,6},{16,24},{18,... | collective-permute-start | bytes 1769480 | tf_op jit(solution)/shard_map/ppermute | solution.py:45
  591.6 12.8 %collective-permute-start.33 = (bf16[192,768]{1,0:T(8,128)(2,1)S(1)}, bf16[192,768]{1,0:T(8,128)(2,1)S(1)}, u32[]{:S(2)}, u32[]{:S(2)}) collective-permute-start(bf16[192,768]{1,0:T(8,128)(2,1)S(1)} %fusion.222), channel_id=1, source_target_pairs={{0,16},{2,18},{4,20},{6,22},{8,24},{10,26},{12,28},{14,30},{16,0},... | collective-permute-start | bytes 884744 | tf_op jit(solution)/shard_map/ppermute | solution.py:45
  605.2 148.2 %all-gather.29.cloned.1.call-start = ((), (), s32[]{:S(2)}) async-start(), calls=%async_computation.8 | async-start | bytes 1474560 | tf_op jit(solution)/shard_map/all_gather | solution.py:261
  610.1 36.1 %collective-permute-start.20 = (bf16[2,2,192,768]{3,2,1,0:T(8,128)(2,1)}, bf16[2,2,192,768]{3,2,1,0:T(8,128)(2,1)}, u32[]{:S(2)}, u32[]{:S(2)}) collective-permute-start(bf16[2,2,192,768]{3,2,1,0:T(8,128)(2,1)} %fusion.167), channel_id=1, source_target_pairs={{0,4},{2,6},{4,0},{6,2},{8,12},{10,14},{12,8},{14,10},{16,20},{18,... | collective-permute-start | bytes 3538952 | tf_op jit(solution)/shard_map/ppermute | solution.py:45
  612.5 27.7 %collective-permute-start.36 = (bf16[2,48,768]{2,1,0:T(8,128)(2,1)}, bf16[2,48,768]{2,1,0:T(8,128)(2,1)S(1)}, u32[]{:S(2)}, u32[]{:S(2)}) collective-permute-start(bf16[2,48,768]{2,1,0:T(8,128)(2,1)} %get-tuple-element.565), channel_id=1, source_target_pairs={{0,4},{2,6},{4,0},{6,2},{8,12},{10,14},{12,8},{14,10},{16,20},{18,... | collective-permute-start | bytes 442376 | tf_op jit(solution)/shard_map/ppermute | solution.py:45
  642.8 1.6 collective-permute-start.37
  646.2 111.4 %all-gather.23.cloned.1.call-start = ((), (), s32[]{:S(2)}) async-start(), calls=%async_computation.5 | async-start | bytes 1474560 | tf_op jit(solution)/shard_map/all_gather | solution.py:261
  648.6 33.5 %collective-permute-start.21 = (bf16[2,192,768]{2,1,0:T(8,128)(2,1)S(1)}, bf16[2,192,768]{2,1,0:T(8,128)(2,1)S(1)}, u32[]{:S(2)}, u32[]{:S(2)}) collective-permute-start(bf16[2,192,768]{2,1,0:T(8,128)(2,1)S(1)} %fusion.186), channel_id=1, source_target_pairs={{0,8},{2,10},{4,12},{6,14},{8,0},{10,2},{12,4},{14,6},{16,24},{18,... | collective-permute-start | bytes 1769480 | tf_op jit(solution)/shard_map/ppermute | solution.py:45
  682.2 12.3 %collective-permute-start.22 = (bf16[192,768]{1,0:T(8,128)(2,1)S(1)}, bf16[192,768]{1,0:T(8,128)(2,1)S(1)}, u32[]{:S(2)}, u32[]{:S(2)}) collective-permute-start(bf16[192,768]{1,0:T(8,128)(2,1)S(1)} %fusion.221), channel_id=1, source_target_pairs={{0,16},{2,18},{4,20},{6,22},{8,24},{10,26},{12,28},{14,30},{16,0},... | collective-permute-start | bytes 884744 | tf_op jit(solution)/shard_map/ppermute | solution.py:45
  695.4 66.8 %all-gather.25.cloned.1.call-start = ((), (), s32[]{:S(2)}) async-start(), calls=%async_computation.6 | async-start | bytes 1474560 | tf_op jit(solution)/shard_map/all_gather | solution.py:261
  695.5 5.2 collective-permute-start.25
  700.8 1.4 collective-permute-start.26
  703.0 269.5 %all-gather.21.cloned.1.call-start = ((), (), s32[]{:S(2)}) async-start(), calls=%async_computation.4 | async-start | bytes 13369344 | tf_op jit(solution)/shard_map/all_gather | solution.py:497
  709.1 11.2 %collective-permute-start.12 = (bf16[256,768]{1,0:T(8,128)(2,1)S(1)}, bf16[256,768]{1,0:T(8,128)(2,1)S(1)}, u32[]{:S(2)}, u32[]{:S(2)}) collective-permute-start(bf16[256,768]{1,0:T(8,128)(2,1)S(1)} %fusion.181), channel_id=1, source_target_pairs={{0,1},{1,0},{2,3},{3,2},{4,5},{5,4},{6,7},{7,6},{8,9},{9,8},{10,11... | collective-permute-start | bytes 1179656 | tf_op jit(solution)/shard_map/ppermute | solution.py:53
  727.8 11.8 %collective-permute-start.14 = (bf16[2,2,2,2,192,768]{5,4,0,1,2,3:T(8,128)(2,1)}, bf16[2,2,2,2,192,768]{5,4,0,1,2,3:T(8,128)(2,1)}, u32[]{:S(2)}, u32[]{:S(2)}) collective-permute-start(bf16[2,2,2,2,192,768]{5,4,0,1,2,3:T(8,128)(2,1)} %fusion.144), channel_id=1, source_target_pairs={{0,2},{2,0},{4,6},{6,4},{8,10},{10,8},{12,14},{14,12},{16,18},{18,... | collective-permute-start | bytes 14155784 | tf_op jit(solution)/shard_map/ppermute | solution.py:45
  727.8 6.7 collective-permute-start.34
  728.1 9.2 collective-permute-start.23
  734.6 2.9 collective-permute-start.35
  737.4 1.4 collective-permute-start.24
  751.1 71.1 %collective-permute-start.15 = (bf16[2,2,2,192,768]{4,3,0,1,2:T(8,128)(2,1)}, bf16[2,2,2,192,768]{4,3,0,1,2:T(8,128)(2,1)}, u32[]{:S(2)}, u32[]{:S(2)}) collective-permute-start(bf16[2,2,2,192,768]{4,3,0,1,2:T(8,128)(2,1)} %fusion.147), channel_id=1, source_target_pairs={{0,4},{2,6},{4,0},{6,2},{8,12},{10,14},{12,8},{14,10},{16,20},{18,... | collective-permute-start | bytes 7077896 | tf_op jit(solution)/shard_map/ppermute | solution.py:45
  757.5 11.2 %collective-permute-start.38 = (bf16[4,2,48,768]{3,2,1,0:T(8,128)(2,1)}, bf16[4,2,48,768]{3,2,1,0:T(8,128)(2,1)S(1)}, u32[]{:S(2)}, u32[]{:S(2)}) collective-permute-start(bf16[4,2,48,768]{3,2,1,0:T(8,128)(2,1)} %get-tuple-element.543), channel_id=1, source_target_pairs={{0,2},{2,0},{4,6},{6,4},{8,10},{10,8},{12,14},{14,12},{16,18},{18,... | collective-permute-start | bytes 1769480 | tf_op jit(solution)/shard_map/ppermute | solution.py:45
  765.6 5.1 collective-permute-start.27
  768.9 78.6 %collective-permute-start.39 = (bf16[4,2,48,768]{3,2,1,0:T(8,128)(2,1)S(1)}, bf16[4,2,48,768]{3,2,1,0:T(8,128)(2,1)S(1)}, u32[]{:S(2)}, u32[]{:S(2)}) collective-permute-start(bf16[4,2,48,768]{3,2,1,0:T(8,128)(2,1)S(1)} %get-tuple-element.541), channel_id=1, source_target_pairs={{0,4},{2,6},{4,0},{6,2},{8,12},{10,14},{12,8},{14,10},{16,20},{18,... | collective-permute-start | bytes 1769480 | tf_op jit(solution)/shard_map/ppermute | solution.py:45
  771.7 100.2 %collective-permute-start.28 = (bf16[4,2,48,768]{3,2,1,0:T(8,128)(2,1)}, bf16[4,2,48,768]{3,2,1,0:T(8,128)(2,1)S(1)}, u32[]{:S(2)}, u32[]{:S(2)}) collective-permute-start(bf16[4,2,48,768]{3,2,1,0:T(8,128)(2,1)} %get-tuple-element.537), channel_id=1, source_target_pairs={{0,4},{2,6},{4,0},{6,2},{8,12},{10,14},{12,8},{14,10},{16,20},{18,... | collective-permute-start | bytes 1769480 | tf_op jit(solution)/shard_map/ppermute | solution.py:45
  828.5 44.9 %collective-permute-start.16 = (bf16[2,2,192,768]{3,2,0,1:T(8,128)(2,1)S(1)}, bf16[2,2,192,768]{3,2,0,1:T(8,128)(2,1)}, u32[]{:S(2)}, u32[]{:S(2)}) collective-permute-start(bf16[2,2,192,768]{3,2,0,1:T(8,128)(2,1)S(1)} %fusion.166), channel_id=1, source_target_pairs={{0,8},{2,10},{4,12},{6,14},{8,0},{10,2},{12,4},{14,6},{16,24},{18,... | collective-permute-start | bytes 3538952 | tf_op jit(solution)/shard_map/ppermute | solution.py:45
  842.4 130.1 %collective-permute-start.13 = (bf16[2008,768]{1,0:T(8,128)(2,1)}, bf16[2008,768]{1,0:T(8,128)(2,1)}, u32[]{:S(2)}, u32[]{:S(2)}) collective-permute-start(bf16[2008,768]{1,0:T(8,128)(2,1)} %convolution_convert_fusion.6), channel_id=1, source_target_pairs={{0,1},{1,0},{2,3},{3,2},{4,5},{5,4},{6,7},{7,6},{8,9},{9,8},{10,11... | collective-permute-start | bytes 9252872 | tf_op jit(solution)/shard_map/ppermute | solution.py:53
  847.5 90.2 %collective-permute-start.40 = (bf16[4,4,48,768]{3,2,1,0:T(8,128)(2,1)S(1)}, bf16[4,4,48,768]{3,2,1,0:T(8,128)(2,1)}, u32[]{:S(2)}, u32[]{:S(2)}) collective-permute-start(bf16[4,4,48,768]{3,2,1,0:T(8,128)(2,1)S(1)} %bitcast.577), channel_id=1, source_target_pairs={{1,0},{3,2},{5,4},{7,6},{9,8},{11,10},{13,12},{15,14},{17,16},{19,... | collective-permute-start | bytes 3538952 | tf_op jit(solution)/shard_map/ppermute | solution.py:61
  872.0 87.1 %collective-permute-start.29 = (bf16[4,4,48,768]{3,2,1,0:T(8,128)(2,1)S(1)}, bf16[4,4,48,768]{3,2,1,0:T(8,128)(2,1)S(1)}, u32[]{:S(2)}, u32[]{:S(2)}) collective-permute-start(bf16[4,4,48,768]{3,2,1,0:T(8,128)(2,1)S(1)} %bitcast.573), channel_id=1, source_target_pairs={{0,1},{1,0},{2,3},{3,2},{4,5},{5,4},{6,7},{7,6},{8,9},{9,8},{10,11... | collective-permute-start | bytes 3538952 | tf_op jit(solution)/shard_map/ppermute | solution.py:53
  875.8 84.1 %collective-permute-start.17 = (bf16[2,192,768]{2,1,0:T(8,128)(2,1)S(1)}, bf16[2,192,768]{2,1,0:T(8,128)(2,1)S(1)}, u32[]{:S(2)}, u32[]{:S(2)}) collective-permute-start(bf16[2,192,768]{2,1,0:T(8,128)(2,1)S(1)} %fusion.185), channel_id=1, source_target_pairs={{0,16},{2,18},{4,20},{6,22},{8,24},{10,26},{12,28},{14,30},{16,0},... | collective-permute-start | bytes 1769480 | tf_op jit(solution)/shard_map/ppermute | solution.py:45
  960.1 11.2 %collective-permute-start.18 = (bf16[2,192,768]{2,1,0:T(8,128)(2,1)S(1)}, bf16[2,192,768]{2,1,0:T(8,128)(2,1)S(1)}, u32[]{:S(2)}, u32[]{:S(2)}) collective-permute-start(bf16[2,192,768]{2,1,0:T(8,128)(2,1)S(1)} %fusion.172), channel_id=1, source_target_pairs={{0,1},{1,0},{2,3},{3,2},{4,5},{5,4},{6,7},{7,6},{8,9},{9,8},{10,11... | collective-permute-start | bytes 1769480 | tf_op jit(solution)/shard_map/ppermute | solution.py:53
  1009.1 50.0 %copy-start.76 = (f32[2,32,12]{1,0,2:T(2,128)S(1)}, f32[2,32,12]{1,0,2:T(2,128)}, u32[]{:S(2)}) copy-start(f32[2,32,12]{1,0,2:T(2,128)} %param.48) | copy-start | bytes 9220
  1009.1 50.0 %copy-start.89 = (f32[2,32,12]{1,0,2:T(2,128)S(1)}, f32[2,32,12]{1,0,2:T(2,128)}, u32[]{:S(2)}) copy-start(f32[2,32,12]{1,0,2:T(2,128)} %param.50) | copy-start | bytes 9220
  1009.1 50.0 %copy-start.90 = (f32[2,32,12]{1,0,2:T(2,128)S(1)}, f32[2,32,12]{1,0,2:T(2,128)}, u32[]{:S(2)}) copy-start(f32[2,32,12]{1,0,2:T(2,128)} %param.49) | copy-start | bytes 9220
  1009.1 51.9 %copy-start.71 = (f32[7,768]{1,0:T(8,128)S(1)}, f32[7,768]{1,0:T(8,128)}, u32[]{:S(2)}) copy-start(f32[7,768]{1,0:T(8,128)} %param.45) | copy-start | bytes 64516
  1009.1 51.9 %copy-start.83 = (f32[7,768]{1,0:T(8,128)S(1)}, f32[7,768]{1,0:T(8,128)}, u32[]{:S(2)}) copy-start(f32[7,768]{1,0:T(8,128)} %param.47) | copy-start | bytes 64516
  1009.1 51.9 %copy-start.84 = (f32[7,768]{1,0:T(8,128)S(1)}, f32[7,768]{1,0:T(8,128)}, u32[]{:S(2)}) copy-start(f32[7,768]{1,0:T(8,128)} %param.46) | copy-start | bytes 64516
  (78 other events, 493.1 us)
Sparse Core Ops, SparseCore 0:
  10.9 56.9 all-gather.12
  70.8 105.3 all-gather.14
  179.1 57.9 all-gather.16
  275.6 48.0 all-gather.18
  605.3 27.0 all-gather.26
  646.3 37.0 all-gather.28
  695.5 28.0 all-gather.22
  725.7 29.5 all-gather.24
  758.2 153.8 all-gather.20

commit v2 on v1

v2 whole, which is shorter than its diff:
```python
import functools
import heapq
import math

import jax
import jax.numpy as jnp
from jax import lax
from jax.experimental import pallas as pl
from jax.experimental.pallas import tpu as pltpu
from jax.sharding import PartitionSpec as P

D = 768
HEADS = 12
DK = 64
MICRO = 2
STEP = 5
SPAN = 28
MATRICES = 4


EPS = 1e-06
CLIP = 1.0
BETA_ONE = 0.9
BETA_TWO = 0.95
BETA_STATS = 0.95
ADAM_EPS = 1e-08
DECAY = 0.01
RATE_TABLE = 0.5
RATE_INNER = 0.01
RATE_GAIN = 0.2
RATE_BIAS = 0.3
RATE_ATTENTION = 0.01
NEGATIVE = -1000000000.0
HIGH = lax.Precision.HIGHEST
VMEM_BYTES = 52 * 1024 * 1024
LOW = jnp.bfloat16
FULL = jnp.float32


def to_low(values):
    return values.astype(jnp.bfloat16)


def to_full(values):
    return values.astype(jnp.float32)


def pick(values, index, axis):
    return lax.dynamic_index_in_dim(values, index, axis, False)


def bit_count():
    return lax.axis_size("section").bit_length() - 1


def section_bit(bit):
    return (lax.axis_index("section") >> bit) & 1


def swap_bit(value, bit, planes=(0, 1)):
    pairs = [
        (2 * source + plane, 2 * (source ^ (1 << bit)) + plane)
        for source in range(lax.axis_size("section"))
        for plane in planes
    ]
    return lax.ppermute(value, ("section", "dp"), pairs)


def swap_half(value):
    return lax.ppermute(value, "dp", [(0, 1), (1, 0)])


def to_decoder(value):
    return lax.ppermute(value, "dp", [(0, 1)])


def to_encoder(value):
    return lax.ppermute(value, "dp", [(1, 0)])


def over(bit, planes=(0, 1)):
    return lambda value: swap_bit(value, bit, planes)


def link_cost(bit, value):
    return 4 + value.size * (6e-6 if bit == 0 else 5.5e-5 if bit < 3 else 1.1e-4)


def interleave(tasks, after):
    results, free, pending, now, count = [None] * len(tasks), {}, [], 0.0, 0
    last = after

    def advance(index, arrived):
        nonlocal last, now, count
        try:
            link, cost, move, value = tasks[index].send(arrived)
        except StopIteration as stop:
            results[index] = stop.value
            return
        count += 1
        if move is None:
            heapq.heappush(pending, (now + cost, count, index, None))
            return
        value, last = lax.optimization_barrier((value, last))
        if link == "core":
            now += cost
            free[link] = now
        else:
            now += 1.0
            free[link] = max(now, free.get(link, 0.0)) + cost
        heapq.heappush(pending, (free[link], count, index, move(value)))

    for index in range(len(tasks)):
        advance(index, None)
    while pending:
        ended, unused, index, arrived = heapq.heappop(pending)
        now = max(now, ended)
        if arrived is not None:
            now += 1.0 + 4e-6 * arrived.size
            arrived, last = lax.optimization_barrier((arrived, last))
            last = arrived
        advance(index, arrived)
    return results


def halved(rows, layout, order, planes=(0, 1)):
    layout = list(layout)
    if isinstance(rows, tuple):
        part, kept = rows
        arrived = yield (0, link_cost(0, part), over(0, planes), part)
        rows = to_low(to_full(kept) + to_full(arrived))
    for bit in order:
        place = layout.index(bit)
        layout.remove(bit)
        split = rows.reshape(2**place, 2, -1, D)
        mine = section_bit(bit)
        part = to_low(pick(split, 1 - mine, 1)).reshape(-1, D)
        arrived = yield (bit, link_cost(bit, part), over(bit, planes), part)
        rows = to_low(to_full(pick(split, mine, 1).reshape(-1, D)) + to_full(arrived))
    return rows


def doubled(block, planes=(0, 1)):
    for stage, bit in enumerate(range(bit_count() - 1, 1, -1)):
        arrived = yield (bit, link_cost(bit, block), over(bit, planes), block)
        block = ordered(block, arrived, section_bit(bit), stage)
    return block.reshape(-1, D)


def to_rows(terms, planes=(0, 1)):
    first, second = section_bit(0), section_bit(1)
    part = pick(terms, 1 - first, 2)
    arrived = yield (0, link_cost(0, part), over(0, planes), part)
    terms = ordered(pick(terms, first, 2), arrived, first, 1)
    part = pick(terms, 1 - second, 2)
    arrived = yield (1, link_cost(1, part), over(1, planes), part)
    terms = ordered(pick(terms, second, 2), arrived, second, 2)
    return terms.reshape(terms.shape[0], MATRICES, -1, D)


def summed(values):
    arrived = yield ("dp", 5, swap_half, values)
    values = values + arrived
    for bit in range(bit_count()):
        arrived = yield (bit, 5, over(bit), values)
        values = values + arrived
    return values


def until(found, names):
    while not all(name in found for name in names):
        yield (None, 2, None, None)


def forward_mul(left, right):
    return jnp.dot(left, right, preferred_element_type=jnp.float32)


def offset_square(row, length):
    width = 2 * length
    padded = jnp.pad(row, (0, width - row.shape[0]))
    flat = jnp.tile(padded, length)[length - 1 : length - 1 + length * (width - 1)]
    return flat.reshape(length, width - 1)[:, :length]


def position_table(onehot, bias_layer):
    return jnp.einsum("qkb,bh->hqk", onehot.astype(jnp.float32), bias_layer, precision=HIGH)


def mul(left, right):
    return lax.dot_general(left, right, (((1,), (0,)), ((), ())), preferred_element_type=FULL)


def mul_right(left, right):
    return lax.dot_general(left, right, (((1,), (1,)), ((), ())), preferred_element_type=FULL)


def mul_left(left, right):
    return lax.dot_general(left, right, (((0,), (0,)), ((), ())), preferred_element_type=FULL)


def rms_scale(values):
    return lax.rsqrt(jnp.mean(values * values, -1, keepdims=True) + EPS)


def rms_back(values, gain_row, upstream):
    scale = rms_scale(values)
    normal = values * scale
    grad_gain = jnp.sum(upstream * normal, 0, keepdims=True)
    weighted = upstream * gain_row
    inner = jnp.mean(weighted * normal, -1, keepdims=True)
    return scale * (weighted - normal * inner), grad_gain


def gelu_parts(values):
    inner = math.sqrt(2.0 / math.pi) * (values + 0.044715 * values * values * values)
    bent = jnp.tanh(inner)
    slope = math.sqrt(2.0 / math.pi) * (1.0 + 3 * 0.044715 * values * values)
    value = 0.5 * values * (1.0 + bent)
    grad = 0.5 * (1.0 + bent) + 0.5 * values * (1.0 - bent * bent) * slope
    return value, grad


def params():
    return pltpu.CompilerParams(vmem_limit_bytes=VMEM_BYTES)


def whole():
    return pl.BlockSpec(memory_space=pltpu.VMEM)


def feed_forward_kernel(
    last_scale, rows_ref, gain_ref, last_ref, in_ref, out_ref, after_ref, head_ref, before_ref, norm_ref, total_ref
):
    step = pl.program_id(0)

    @pl.when(step == 0)
    def start():
        rows = rows_ref[...]
        norm_ref[...] = (rows * rms_scale(rows) * gain_ref[...]).astype(LOW)
        total_ref[...] = rows

    before = mul_right(norm_ref[...], in_ref[0])
    before_ref[...] = before
    active, unused = gelu_parts(before)
    total_ref[...] += mul(active.astype(LOW), out_ref[0])

    @pl.when(step == pl.num_programs(0) - 1)
    def finish():
        after = total_ref[...]
        after_ref[...] = after
        head_ref[...] = (after * rms_scale(after) * last_ref[...] * last_scale).astype(LOW)


def feed_forward(rows, gain_row, last_gain, weights, last_scale):
    count, hidden = rows.shape[0], weights.shape[1]
    chunk = D
    fixed = pl.BlockSpec((count, D), lambda j: (0, 0))
    row = pl.BlockSpec((1, D), lambda j: (0, 0))
    return pl.pallas_call(
        functools.partial(feed_forward_kernel, last_scale),
        grid=(hidden // chunk,),
        in_specs=[
            fixed,
            row,
            row,
            pl.BlockSpec((1, chunk, D), lambda j: (1, j, 0)),
            pl.BlockSpec((1, chunk, D), lambda j: (2, j, 0)),
        ],
        out_specs=[fixed, fixed, pl.BlockSpec((count, chunk), lambda j: (0, j))],
        out_shape=[
            jax.ShapeDtypeStruct((count, D), FULL),
            jax.ShapeDtypeStruct((count, D), LOW),
            jax.ShapeDtypeStruct((count, hidden), FULL),
        ],
        scratch_shapes=[pltpu.VMEM((count, D), LOW), pltpu.VMEM((count, D), FULL)],
        compiler_params=params(),
        name="feed_forward",
    )(rows, gain_row[None], last_gain[None], weights, weights)


def feed_backward_kernel(
    last_scale,
    mine_ref,
    upstream_ref,
    after_ref,
    last_ref,
    rows_ref,
    gain_ref,
    before_ref,
    in_ref,
    out_ref,
    grad_ref,
    in_sent_ref,
    in_kept_ref,
    out_sent_ref,
    out_kept_ref,
    gains_ref,
    resid_ref,
    low_ref,
    norm_ref,
    total_ref,
):
    step = pl.program_id(0)

    @pl.when(step == 0)
    def start():
        upstream = upstream_ref[...].astype(FULL) * last_scale
        resid, grad_last = rms_back(after_ref[...], last_ref[...], upstream)
        resid_ref[...] = resid
        low_ref[...] = resid.astype(LOW)
        rows = rows_ref[...]
        norm_ref[...] = (rows * rms_scale(rows) * gain_ref[...]).astype(LOW)
        total_ref[...] = jnp.zeros_like(total_ref)
        gains_ref[1:2] = grad_last

    grad_out = low_ref[...]
    active, slope = gelu_parts(before_ref[...])
    grad_before = (mul_right(grad_out, out_ref[0]) * slope).astype(LOW)
    total_ref[...] += mul(grad_before, in_ref[0])
    in_grad = mul_left(grad_before, norm_ref[...]).astype(LOW)
    out_grad = mul_left(active.astype(LOW), grad_out).astype(LOW)

    @pl.when(step < 2)
    def send():
        in_sent_ref[...] = in_grad
        out_sent_ref[...] = out_grad

    @pl.when(step >= 2)
    def keep():
        in_kept_ref[...] = in_grad
        out_kept_ref[...] = out_grad

    @pl.when(step == pl.num_programs(0) - 1)
    def finish():
        grad_rows, grad_gain = rms_back(rows_ref[...], gain_ref[...], total_ref[...])
        grad_ref[...] = resid_ref[...] + grad_rows
        gains_ref[0:1] = grad_gain


def feed_backward(upstream, after, last_gain, rows, gain_row, before, weights, last_scale):
    count, hidden = before.shape
    chunk = hidden // 4

    def place(step, mine):
        return 2 * ((step >= 2) == (mine[0] == 1)) + step % 2

    fixed = pl.BlockSpec((count, D), lambda j, mine: (0, 0))
    row = pl.BlockSpec((1, D), lambda j, mine: (0, 0))
    sent = pl.BlockSpec((chunk, D), lambda j, mine: (jnp.minimum(j, 1), 0))
    kept = pl.BlockSpec((chunk, D), lambda j, mine: (jnp.maximum(j - 2, 0), 0))
    half = jax.ShapeDtypeStruct((hidden // 2, D), LOW)
    return pl.pallas_call(
        functools.partial(feed_backward_kernel, last_scale),
        grid_spec=pltpu.PrefetchScalarGridSpec(
            num_scalar_prefetch=1,
            grid=(4,),
            in_specs=[
                fixed,
                fixed,
                row,
                fixed,
                row,
                pl.BlockSpec((count, chunk), lambda j, mine: (0, place(j, mine))),
                pl.BlockSpec((1, chunk, D), lambda j, mine: (1, place(j, mine), 0)),
                pl.BlockSpec((1, chunk, D), lambda j, mine: (2, place(j, mine), 0)),
            ],
            out_specs=[fixed, sent, kept, sent, kept, pl.BlockSpec((2, D), lambda j, mine: (0, 0))],
            scratch_shapes=[
                pltpu.VMEM((count, D), FULL),
                pltpu.VMEM((count, D), LOW),
                pltpu.VMEM((count, D), LOW),
                pltpu.VMEM((count, D), FULL),
            ],
        ),
        out_shape=[jax.ShapeDtypeStruct((count, D), FULL)]
        + [half] * 4
        + [jax.ShapeDtypeStruct((2, D), FULL)],
        compiler_params=params(),
        name="feed_backward",
    )(section_bit(0)[None], upstream, after, last_gain[None], rows, gain_row[None], before, weights, weights)


def weight_spec(weights):
    slot, values = weights
    if slot is None:
        return pl.BlockSpec(memory_space=pltpu.VMEM)
    return pl.BlockSpec((1,) + values.shape[1:], lambda i: (slot, 0, 0))


def matrix_reader(ref, places):
    if places is None:
        return lambda m: ref[m]
    rows = D // len(places)
    return lambda m: jnp.concatenate(
        [ref[0, pl.ds((place * MATRICES + m) * rows, rows)] for place in places]
    )


def head_pairs(length):
    for sequence in range(MICRO):
        for pair in range(HEADS // 2):
            yield slice(sequence * length, (sequence + 1) * length), slice(
                pair * 2 * DK, (pair + 1) * 2 * DK
            ), pair


def probabilities(queries, keys_in, bias):
    scores = mul_right(queries, keys_in) * DK ** (-0.5)
    if bias is not None:
        scores = scores + bias
    raised = jnp.exp(scores - jnp.max(scores, -1, keepdims=True))
    return raised * (1.0 / jnp.sum(raised, -1, keepdims=True))


def attention_forward_kernel(biased, crossed, places, *refs):
    refs = list(refs)
    rows_ref, gain_ref, weight_ref = refs[:3]
    matrix = matrix_reader(weight_ref, places)
    source_ref = refs[3] if crossed else None
    bias_ref = refs[3 + crossed] if biased else None
    after_ref, norm_ref, query_ref, key_ref, value_ref, mixed_ref = refs[3 + crossed + biased :]
    rows = rows_ref[...]
    normed = (rows * rms_scale(rows) * gain_ref[...]).astype(LOW)
    norm_ref[...] = normed
    source = source_ref[...] if crossed else normed
    query_ref[...] = mul(normed, matrix(0)).astype(LOW)
    key_ref[...] = mul(source, matrix(1)).astype(LOW)
    value_ref[...] = mul(source, matrix(2)).astype(LOW)
    length = rows.shape[0] // MICRO
    left = lax.broadcasted_iota(jnp.int32, (length, 2 * DK), 1) < DK
    for rows_at, columns, pair in head_pairs(length):
        queries = query_ref[rows_at, columns]
        keys_in, values_in = key_ref[rows_at, columns], value_ref[rows_at, columns]
        mixed = []
        for side in range(2):
            picked = jnp.where(left == (side == 0), queries, jnp.zeros_like(queries))
            bias = bias_ref[2 * pair + side] if biased else None
            probs = probabilities(picked, keys_in, bias)
            mixed.append(mul(probs.astype(LOW), values_in))
        mixed_ref[rows_at, columns] = jnp.where(left, mixed[0], mixed[1]).astype(LOW)
    after_ref[...] = rows + mul(mixed_ref[...], matrix(3))


def attention_forward(rows, gain_row, weights, source, bias):
    crossed, biased = source is not None, bias is not None
    operands = [rows, gain_row[None], weights[1]]
    operands += [source] * crossed + [bias] * biased
    places = None if weights[0] is None else slot_places()
    low = jax.ShapeDtypeStruct(rows.shape, LOW)
    after, *kept = pl.pallas_call(
        functools.partial(attention_forward_kernel, biased, crossed, places),
        grid=(1,),
        in_specs=[whole()] * 2 + [weight_spec(weights)] + [whole()] * (len(operands) - 3),
        out_specs=[whole()] * 6,
        out_shape=[jax.ShapeDtypeStruct(rows.shape, FULL)] + [low] * 5,
        compiler_params=params(),
        name="attention_forward",
    )(*operands)
    return after, kept


def attention_backward_kernel(biased, crossed, places, mine_ref, *refs):
    refs = list(refs)
    grad_ref, rows_ref, gain_ref, weight_ref = refs[:4]
    matrix = matrix_reader(weight_ref, places)
    norm_ref, query_ref, key_ref, value_ref, mixed_ref = refs[4:9]
    source_ref = refs[9] if crossed else None
    bias_ref = refs[9 + crossed] if biased else None
    refs = refs[9 + crossed + biased :]
    result_ref, sent_ref, kept_ref, gain_grad_ref, extra_ref = refs[:5]
    grad_query_ref, grad_key_ref, grad_value_ref, grad_mixed_ref = refs[5:]
    mine = mine_ref[0]

    def put(m, value):
        @pl.when(mine == m // 2)
        def keep():
            kept_ref[pl.ds(m % 2 * D, D)] = value

        @pl.when(mine != m // 2)
        def send():
            sent_ref[pl.ds(m % 2 * D, D)] = value

    grad = grad_ref[...]
    grad_out = grad.astype(LOW)
    grad_mixed_ref[...] = mul_right(grad_out, matrix(3)).astype(LOW)
    put(3, mul_left(mixed_ref[...], grad_out).astype(LOW))
    length = grad.shape[0] // MICRO
    left = lax.broadcasted_iota(jnp.int32, (length, 2 * DK), 1) < DK
    for rows_at, columns, pair in head_pairs(length):
        queries, keys_in = query_ref[rows_at, columns], key_ref[rows_at, columns]
        values_in, grad_mixed = value_ref[rows_at, columns], grad_mixed_ref[rows_at, columns]
        parts = []
        for side in range(2):
            half = left == (side == 0)
            bias = bias_ref[2 * pair + side] if biased else None
            probs = probabilities(jnp.where(half, queries, jnp.zeros_like(queries)), keys_in, bias)
            picked = jnp.where(half, grad_mixed, jnp.zeros_like(grad_mixed))
            grad_probs = mul_right(picked, values_in)
            grad_scores = probs * (grad_probs - jnp.sum(probs * grad_probs, -1, keepdims=True))
            grad_scores = grad_scores.astype(LOW)
            if biased:
                if rows_at.start == 0:
                    extra_ref[2 * pair + side] = grad_scores.astype(FULL)
                else:
                    extra_ref[2 * pair + side] += grad_scores.astype(FULL)
            parts.append(
                (
                    mul(grad_scores, keys_in),
                    mul_left(grad_scores, queries),
                    mul_left(probs.astype(LOW), grad_mixed),
                )
            )
        scale = DK ** (-0.5)
        grad_query_ref[rows_at, columns] = (
            jnp.where(left, parts[0][0], parts[1][0]) * scale
        ).astype(LOW)
        grad_key_ref[rows_at, columns] = (
            jnp.where(left, parts[0][1], parts[1][1]) * scale
        ).astype(LOW)
        grad_value_ref[rows_at, columns] = jnp.where(left, parts[0][2], parts[1][2]).astype(LOW)
    normed = norm_ref[...]
    source = source_ref[...] if crossed else normed
    put(0, mul_left(normed, grad_query_ref[...]).astype(LOW))
    put(1, mul_left(source, grad_key_ref[...]).astype(LOW))
    put(2, mul_left(source, grad_value_ref[...]).astype(LOW))
    grad_norm = mul_right(grad_query_ref[...], matrix(0))
    grad_source = mul_right(grad_key_ref[...], matrix(1))
    grad_source = grad_source + mul_right(grad_value_ref[...], matrix(2))
    if crossed:
        extra_ref[...] = grad_source.astype(LOW)
    else:
        grad_norm = grad_norm + grad_source
    grad_rows, grad_gain = rms_back(rows_ref[...], gain_ref[...], grad_norm)
    result_ref[...] = (grad + grad_rows).astype(result_ref.dtype)
    gain_grad_ref[...] = grad_gain


def attention_backward(grad, rows, gain_row, weights, kept, source, bias):
    crossed, biased = source is not None, bias is not None
    operands = [section_bit(0)[None], grad, rows, gain_row[None], weights[1], *kept]
    places = None if weights[0] is None else slot_places()
    half = jax.ShapeDtypeStruct((MATRICES // 2 * D, D), LOW)
    operands += [source] * crossed + [bias] * biased
    low = pltpu.VMEM(rows.shape, LOW)
    extra = jax.ShapeDtypeStruct(bias.shape, FULL) if biased else jax.ShapeDtypeStruct(rows.shape, LOW)
    return pl.pallas_call(
        functools.partial(attention_backward_kernel, biased, crossed, places),
        grid=(1,),
        in_specs=[pl.BlockSpec(memory_space=pltpu.SMEM)]
        + [whole()] * 3
        + [weight_spec(weights)]
        + [whole()] * (len(operands) - 5),
        out_specs=[whole()] * 5,
        out_shape=[
            jax.ShapeDtypeStruct(rows.shape, FULL if crossed else LOW),
            half,
            half,
            jax.ShapeDtypeStruct((1, D), FULL),
            extra,
        ],
        scratch_shapes=[low] * 4,
        compiler_params=params(),
        name="attention_backward",
    )(*operands)


def adamw(weight, first, second, gradient, rate):
    first = BETA_ONE * first + (1 - BETA_ONE) * gradient
    second = BETA_TWO * second + (1 - BETA_TWO) * gradient * gradient
    stepped = first / (1 - BETA_ONE**STEP) / (jnp.sqrt(second / (1 - BETA_TWO**STEP)) + ADAM_EPS)
    return (first, second, weight - rate * (stepped + DECAY * weight))


def ordered(own, other, mine, axis):
    return jnp.where(
        mine == 0, jnp.stack([own, other], axis), jnp.stack([other, own], axis)
    )


def slot_places():
    order = low_bit_order()
    return [order.index(section) for section in range(len(order))]


def low_bit_order():
    sections = lax.axis_size("section")
    return sorted(range(sections), key=lambda p: (p & 1, (p >> 1) & 1, p >> 2))


def slot_layout():
    return [1] + list(range(bit_count() - 1, 1, -1))


def shampoo_terms(low, full, left_block, right_full):
    rows = low.shape[0]
    start = (lax.axis_index("section") // MATRICES) * rows
    columns = lax.dynamic_slice_in_dim(full, start, rows, 1)
    blended = to_low(forward_mul(left_block, full))
    direction = forward_mul(blended, right_full)
    left_term = jnp.einsum("rd,ed->re", low, full, preferred_element_type=jnp.float32)
    right_term = jnp.einsum("dr,de->re", columns, full, preferred_element_type=jnp.float32)
    terms = jnp.stack([low, to_low(direction), to_low(left_term), to_low(right_term)])
    return terms.reshape(4, 2, 2, rows // 4, D)


def gather_small(values):
    values = ordered(values, swap_half(values), lax.axis_index("dp"), 0)[None]
    for bit in range(bit_count()):
        both = ordered(values, swap_bit(values, bit), section_bit(bit), 0)
        values = both.reshape((-1,) + values.shape[1:])
    return values


def lookup_rows(ids, shard_low):
    bits = bit_count()
    start = lax.axis_index("section") * shard_low.shape[0]
    mine = section_bit(0)

    def owned(some_ids):
        hit = some_ids.reshape(-1, 1) == jnp.arange(shard_low.shape[0])[None, :]
        return to_low(forward_mul(hit.astype(jnp.bfloat16), shard_low))

    split = (ids - start).reshape((2,) * bits + (MICRO, -1))
    split = jnp.moveaxis(split, bits, 0)
    sent, kept = pick(split, 1 - mine, bits), pick(split, mine, bits)
    arrived = swap_bit(owned(sent), 0)
    rows = (owned(kept) + arrived).reshape(MICRO, -1, D)
    layout = range(bits - 1, 0, -1)
    orders = [list(range(1, bits)), list(range(2, bits)) + [1]]
    chains = [halved(rows[micro], layout, orders[micro]) for micro in range(MICRO)]
    return jnp.concatenate(interleave(chains, arrived))


def local(
    token_ids,
    targets,
    objective,
    buckets,
    table,
    table_first,
    table_second,
    inner_weight,
    inner_first,
    inner_second,
    outer_weight,
    outer_first,
    outer_second,
    gain_rows,
    gain_first,
    gain_second,
    position_bias,
    bias_first,
    bias_second,
    attention,
    left_stats,
    right_stats,
    left_roots,
    right_inverse_roots,
):
    sections = lax.axis_size("section")
    section_index = lax.axis_index("section")
    half = lax.axis_index("dp")
    is_encoder = half == 0
    is_decoder = half == 1
    length = token_ids.shape[-1]
    vocab_rows = table.shape[0]
    bits = sections.bit_length() - 1

    packed = jnp.concatenate(
        [token_ids.reshape(-1), targets.reshape(-1), jnp.broadcast_to(objective.reshape(-1), (length,))]
    )
    every = gather_small(packed.reshape(-1, length)).reshape(sections, 2, -1).swapaxes(0, 1)
    every_tokens = every[:, :, : MICRO * length]
    every_targets = every[:, :, MICRO * length : (MICRO + 1) * length]
    every_objective = every[:, :, (MICRO + 1) * length]
    halves = sections // 2
    encoder_ids = every_tokens[:, :halves].reshape(sections, MICRO * length)
    decoder_ids = every_tokens[:, halves:].reshape(sections, MICRO * length)
    own_ids = jnp.where(is_encoder, encoder_ids, decoder_ids)

    def of_micro(values):
        return jnp.where(is_encoder, values[:, halves:], values[:, :halves])

    goal_ids = of_micro(every_targets).reshape(-1)
    goal_objective = of_micro(every_objective).reshape(sections)
    live_all = (
        jnp.arange(length)[None, :] < jnp.where(goal_objective == 1, length, SPAN)[:, None]
    ).astype(jnp.float32)
    live_rows = pick(live_all, section_index, 0)

    shard_low = to_low(table)
    attention_low = to_low(attention)
    shard_rows = attention.shape[1] * MATRICES
    self_shard = lax.dynamic_slice_in_dim(attention_low, half * MATRICES, MATRICES, 0)
    weight_shard = jnp.stack(
        [
            self_shard.reshape(shard_rows, D),
            to_low(pick(inner_weight, half, 0).T),
            to_low(pick(outer_weight, half, 0)),
            attention_low[8:12].reshape(shard_rows, D),
        ]
    )
    weights = lax.all_gather(
        weight_shard, "section", axis=1, tiled=True, axis_index_groups=[low_bit_order()]
    )
    def natural(slot):
        split = slot.reshape(2, 2, sections // 4, MATRICES, -1, D)
        return jnp.transpose(split, (3, 2, 1, 0, 4, 5)).reshape(MATRICES, D, D)

    if attention.shape[1] % 16 == 0:
        self_weights, cross_weights = (0, weights), (3, weights)
    else:
        self_weights, cross_weights = (None, natural(weights[0])), (None, natural(weights[3]))

    bucket_square = offset_square(pick(buckets, half, 0), length)
    bucket_range = jnp.arange(position_bias.shape[1])
    onehot = (bucket_square[:, :, None] == bucket_range).astype(jnp.bfloat16)
    bias_term = position_table(onehot, pick(position_bias, half, 0))
    allowed = is_encoder | (jnp.arange(length)[:, None] >= jnp.arange(length)[None, :])

    rows_in = to_full(lookup_rows(own_ids, shard_low))
    gain_self = gain_rows[jnp.where(is_encoder, 0, 3)]
    gain_feed = gain_rows[jnp.where(is_encoder, 1, 5)]
    bias_term = jnp.where(allowed, bias_term, NEGATIVE)
    resid, kept_self = attention_forward(rows_in, gain_self, self_weights, None, bias_term)

    def encoder_rest():
        return feed_forward(resid, gain_feed, gain_rows[2], weights, 1.0)

    first, second = section_bit(0), section_bit(1)
    root_rows = jnp.stack([left_roots, right_inverse_roots])
    own_roots = lax.dynamic_slice_in_dim(root_rows, half * MATRICES, MATRICES, 1)
    root_rows = jnp.stack([own_roots, root_rows[:, 8:12]]).reshape(4, 2, 2, -1, D)
    root_rows, unused = lax.optimization_barrier((root_rows, resid))
    root_part = swap_bit(pick(root_rows, 1 - first, 1), 0)

    after_enc, encoded, before_enc = lax.cond(
        is_encoder, encoder_rest, lambda: jax.tree.map(jnp.zeros_like, encoder_rest())
    )
    encoded, root_part = lax.optimization_barrier((encoded, root_part))
    arrived = to_decoder(encoded)
    root_rows = ordered(pick(root_rows, first, 1), root_part, first, 2)
    root_part = swap_bit(pick(root_rows, 1 - second, 1), 1)

    def decoder_rest(after, before):
        rows_feed, kept_cross = attention_forward(
            resid, gain_rows[4], cross_weights, arrived, None
        )
        after, final, before = feed_forward(
            rows_feed, gain_feed, gain_rows[6], weights, D ** (-0.5)
        )
        return (final, after, before, rows_feed, kept_cross)

    def decoder_skip(after, before):
        empty = jnp.zeros(resid.shape, jnp.bfloat16)
        return (empty, after, before, resid, [empty] * 5)

    final_low, after_feed, before_feed, rows_feed, kept_cross = lax.cond(
        is_decoder, decoder_rest, decoder_skip, after_enc, before_enc
    )

    final_low, root_part = lax.optimization_barrier((final_low, root_part))
    root_rows = ordered(pick(root_rows, second, 1), root_part, second, 1)
    root_rows = root_rows.reshape(2, 2, -1, D)
    root_lefts, root_rights = root_rows[:, 0], root_rows[:, 1]

    final_split = final_low.reshape(MICRO, length, D)
    handed = to_encoder(final_split[0])
    own_rows = jnp.where(is_encoder, handed, final_split[1])
    head_low = own_rows * live_rows[:, None].astype(jnp.bfloat16)
    all_rows = lax.all_gather(head_low, "section", axis=0, tiled=True)
    logits = jnp.einsum("nd,vd->nv", all_rows, shard_low, preferred_element_type=jnp.float32)
    goal_hit = (goal_ids - section_index * vocab_rows)[:, None] == jnp.arange(vocab_rows)[None, :]
    row_peak = jnp.max(logits, -1)
    row_total = jnp.sum(jnp.exp(logits - row_peak[:, None]), -1)
    goal_logit = jnp.sum(jnp.where(goal_hit, logits, 0.0), -1)
    every_stat = lax.all_gather(jnp.stack([row_peak, row_total]), "section")
    top_peak = jnp.max(every_stat[:, 0], 0)
    log_total = top_peak + jnp.log(
        jnp.sum(every_stat[:, 1] * jnp.exp(every_stat[:, 0] - top_peak), 0)
    )
    grad_logits = to_low(jnp.exp(logits - log_total[:, None]) - goal_hit.astype(jnp.float32))
    grad_all = forward_mul(grad_logits, shard_low)
    def head_table_task():
        yield (None, 14, None, None)
        product = lambda grads: mul_left(grads, all_rows)
        return (yield ("core", 10, product, grad_logits))

    chain = halved(grad_all, range(bits - 1, -1, -1), range(bits))
    grad_head, head_table = interleave([chain, head_table_task()], log_total)
    grad_head = to_full(grad_head)
    grad_head = to_low(grad_head * live_rows[:, None])
    own_live = lax.dynamic_slice_in_dim(log_total, section_index * length, length, 0)
    loss_part = jnp.sum(live_rows * own_live) - jnp.sum(live_all.reshape(-1) * goal_logit)
    count_part = jnp.sum(live_rows)
    grad_final = jnp.stack([to_decoder(grad_head), grad_head]).reshape(MICRO * length, D)

    def decoder_back():
        grad_rows, *feed_grads, gains = feed_backward(
            grad_final,
            after_feed,
            gain_rows[6],
            rows_feed,
            gain_feed,
            before_feed,
            weights,
            D ** (-0.5),
        )
        grad_rows, *cross_grads, gain_cross, grad_source = attention_backward(
            grad_rows, resid, gain_rows[4], cross_weights, kept_cross, arrived, None
        )
        gains = jnp.concatenate([gain_cross, gains])
        return (grad_source, grad_rows, feed_grads, cross_grads, gains)

    root_steps = list(range(bits - 1, 1, -1))

    def root_step(stage):
        return swap_bit(root_rights, root_steps[stage])

    def grown(stage, part):
        mine = section_bit(root_steps[stage])
        return ordered(root_rights, part, mine, 1 + stage)

    for stage in range(len(root_steps) - 2):
        root_rights = grown(stage, root_step(stage))
    root_part = root_step(len(root_steps) - 2)
    grad_source, grad_dec, feed_dec, cross_grads, gains_dec = lax.cond(
        is_decoder, decoder_back, lambda: jax.tree.map(jnp.zeros_like, decoder_back())
    )
    back_source = to_encoder(grad_source)

    back_source, feed_dec, cross_grads, root_part = lax.optimization_barrier(
        (back_source, feed_dec, cross_grads, root_part)
    )
    root_rights = grown(len(root_steps) - 2, root_part)
    root_part = root_step(len(root_steps) - 1)

    late = to_low(to_full(feed_dec[1]) + to_full(swap_bit(feed_dec[0], 0, (1,))))
    late_split = late.reshape(2, -1, D)
    late_arrived = swap_bit(pick(late_split, 1 - second, 0), 1, (1,))

    def self_back(grad_rows):
        return attention_backward(
            grad_rows, rows_in, gain_self, self_weights, kept_self, None, bias_term
        )

    def encoder_feed():
        grad_rows, *feed_grads, gains = feed_backward(
            back_source,
            after_feed,
            gain_rows[2],
            resid,
            gain_feed,
            before_feed,
            weights,
            1.0,
        )
        return (grad_rows, gains, jnp.zeros(bias_term.shape, jnp.float32), feed_grads)

    def decoder_self():
        embed_low, *self_grads, gain_grad, score_grad = self_back(grad_dec)
        gains = jnp.concatenate([gain_grad, gain_grad])
        return (to_full(embed_low), gains, score_grad, self_grads + cross_grads)

    grad_rows, gains_middle, score_middle, grads_middle = lax.cond(
        is_encoder, encoder_feed, decoder_self
    )
    grad_rows, grads_middle = lax.optimization_barrier((grad_rows, grads_middle))
    sent_first = swap_bit(grads_middle[0], 0)
    sent_second = swap_bit(grads_middle[2], 0)

    def encoder_self():
        embed_low, *self_grads, gain_grad, score_grad = self_back(grad_rows)
        gains = jnp.concatenate([gain_grad, gains_middle, jnp.zeros((4, D), jnp.float32)])
        return (embed_low, gains, score_grad, self_grads)

    def decoder_skip_self():
        gains = jnp.concatenate([jnp.zeros((3, D), jnp.float32), gains_middle[:1], gains_dec])
        return (to_low(grad_rows), gains, score_middle, feed_dec[2:])

    embed_low, gain_part, score_grad, third_grads = lax.cond(
        is_encoder, encoder_self, decoder_skip_self
    )
    embed_low, third_grads, sent_first, sent_second, late_arrived, root_part = (
        lax.optimization_barrier(
            (embed_low, third_grads, sent_first, sent_second, late_arrived, root_part)
        )
    )
    late = to_low(to_full(pick(late_split, second, 0)) + to_full(late_arrived))
    root_rights = grown(len(root_steps) - 1, root_part).reshape(2, D, D)
    bias_grad = jnp.einsum("hqk,qkb->bh", score_grad, onehot.astype(jnp.float32), precision=HIGH)

    found = {}
    own_local = (own_ids.reshape(-1) - section_index * vocab_rows)[None, :]

    def squares(values):
        return jnp.sum(to_full(values) * to_full(values))

    def rows_task():
        every_rows = yield ("gather", 80, lambda rows: lax.all_gather(rows, "section"), embed_low)
        found["rows"] = every_rows.reshape(-1, D)

    cuts = [vocab_rows * part // 64 * 16 for part in range(4)] + [vocab_rows]

    def table_task(part):
        start, stop = cuts[part], cuts[part + 1]
        yield from until(found, ["rows"])

        def product(rows):
            hit = own_local == jnp.arange(start, stop)[:, None]
            return to_low(mul(hit.astype(jnp.bfloat16), rows) + head_table[start:stop])

        own = yield ("core", 6, product, found["rows"])
        other = yield ("dp", 19, swap_half, own)
        both = to_full(own) + to_full(other)
        found["table", part] = squares(both)
        return both

    def first_task():
        rows = to_low(to_full(grads_middle[1]) + to_full(sent_first))
        found["first"] = yield from halved(rows, slot_layout(), range(1, bits))

    def second_task():
        yield (None, 4, None, None)
        rows = to_low(to_full(grads_middle[3]) + to_full(sent_second))
        block = yield from halved(rows, slot_layout(), range(1, bits))
        found["second"] = block
        found["cross_square"] = squares(block)
        full = yield from doubled(block, (1,))
        terms = shampoo_terms(block, full, root_lefts[1], root_rights[1])
        found["cross_direction"] = squares(terms[1])
        terms = yield from to_rows(terms, (1,))
        other = yield ("dp", 30, to_encoder, terms)
        return jnp.where(is_encoder, other, terms)

    def third_task():
        found["third"] = yield from halved(tuple(third_grads), slot_layout(), range(1, bits))

    def late_task():
        found["late"] = yield from halved(late, slot_layout()[1:], range(2, bits), (1,))

    def self_task():
        yield from until(found, ["first", "third"])
        block = jnp.where(is_encoder, found["third"], found["first"])
        found["self_square"] = squares(block)
        full = yield from doubled(block)
        terms = shampoo_terms(block, full, root_lefts[0], root_rights[0])
        found["self_direction"] = squares(terms[1])
        terms = yield from to_rows(terms)
        other = yield ("dp", 30, swap_half, terms)
        return ordered(terms, other, half, 1).reshape(4, 2 * MATRICES, -1, D)

    def feed_task():
        yield from until(found, ["first", "second", "third", "late"])
        own = jnp.where(
            is_encoder,
            jnp.stack([found["first"], found["second"]]),
            jnp.stack([found["late"], found["third"]]),
        )
        found["feed_square"] = squares(own)
        other = yield ("dp", 15, swap_half, own)
        return to_full(ordered(own, other, half, 1))

    def small_task():
        small = jnp.concatenate(
            [gain_part.reshape(-1), jnp.where(half == 0, bias_grad, 0.0).reshape(-1)]
            + [jnp.where(half == 1, bias_grad, 0.0).reshape(-1)]
        )
        small = yield from summed(small.reshape(-1, 128))
        return small.reshape(-1)

    def norm_task():
        tables = [("table", part) for part in range(4)]
        yield from until(
            found,
            tables + ["self_square", "cross_square", "feed_square"]
            + ["self_direction", "cross_direction"],
        )
        cross_live = is_decoder.astype(jnp.float32)
        square_sum = (
            0.5 * sum(found[name] for name in tables)
            + found["self_square"]
            + found["feed_square"]
            + cross_live * found["cross_square"]
        )
        matrix = 2 * section_bit(0) + section_bit(1)
        names = jnp.arange(3 * MATRICES)
        own_matrix, cross_matrix = half * MATRICES + matrix, 2 * MATRICES + matrix
        directions = jnp.where(names == own_matrix, found["self_direction"], 0.0)
        directions = directions + jnp.where(
            names == cross_matrix, cross_live * found["cross_direction"], 0.0
        )
        sums = jnp.concatenate([jnp.stack([loss_part, count_part, square_sum]), directions])
        sums = yield from summed(jnp.pad(sums, (0, 128 - sums.shape[0])).reshape(1, 128))
        return sums[0, : 3 + 3 * MATRICES]

    tasks = [rows_task(), first_task(), third_task(), second_task(), late_task(), self_task()]
    tasks += [feed_task(), small_task(), norm_task()] + [table_task(part) for part in range(4)]
    results = interleave(tasks, embed_low)
    cross_terms, self_terms = results[3], results[5]
    feed_both, small, sums = results[6:9]
    table_grad = jnp.concatenate(results[9:])
    attention_grad, direction, left_term, right_term = to_full(
        jnp.concatenate([self_terms, cross_terms], 1)
    )
    inner_part = jnp.swapaxes(feed_both[0], 1, 2)
    outer_part = feed_both[1]
    gain_full = small[: gain_rows.size].reshape(gain_rows.shape)
    bias_full = small[gain_rows.size :].reshape(position_bias.shape)
    small_square = squares(gain_full) + squares(bias_full)

    grad_norm = jnp.sqrt(sums[2] + small_square)
    clip_factor = CLIP / jnp.maximum(grad_norm, CLIP)
    table_out = adamw(table, table_first, table_second, table_grad * clip_factor, RATE_TABLE)
    inner_out = adamw(inner_weight, inner_first, inner_second, inner_part * clip_factor, RATE_INNER)
    outer_out = adamw(outer_weight, outer_first, outer_second, outer_part * clip_factor, RATE_INNER)
    gain_out = adamw(gain_rows, gain_first, gain_second, gain_full * clip_factor, RATE_GAIN)
    bias_out = adamw(position_bias, bias_first, bias_second, bias_full * clip_factor, RATE_BIAS)
    clip_square = clip_factor * clip_factor
    left_new = BETA_STATS * left_stats + (1 - BETA_STATS) * clip_square * left_term
    right_new = BETA_STATS * right_stats + (1 - BETA_STATS) * clip_square * right_term
    spread = jnp.sqrt(sums[3:] / (D * D) + EPS)[:, None, None]
    attention_new = attention - RATE_ATTENTION * (direction / spread + DECAY * attention)
    return (
        sums[0],
        sums[1],
        grad_norm,
        *table_out,
        *inner_out,
        *outer_out,
        *gain_out,
        *bias_out,
        attention_grad * clip_factor,
        left_new,
        right_new,
        attention_new,
    )


def solution(mesh):
    in_specs = (
        P("dp", "section", None, None),
        P("dp", "section", None),
        P("dp", "section"),
        P(),
        P("section", None),
        P("section", None),
        P("section", None),
        P(None, None, "section"),
        P(None, None, "section"),
        P(None, None, "section"),
        P(None, "section", None),
        P(None, "section", None),
        P(None, "section", None),
        P(),
        P(),
        P(),
        P(),
        P(),
        P(),
        P(None, "section", None),
        P(None, "section", None),
        P(None, "section", None),
        P(None, "section", None),
        P(None, "section", None),
    )
    out_specs = (
        P(),
        P(),
        P(),
        P("section", None),
        P("section", None),
        P("section", None),
        P(None, None, "section"),
        P(None, None, "section"),
        P(None, None, "section"),
        P(None, "section", None),
        P(None, "section", None),
        P(None, "section", None),
        P(),
        P(),
        P(),
        P(),
        P(),
        P(),
        P(None, "section", None),
        P(None, "section", None),
        P(None, "section", None),
        P(None, "section", None),
    )
    return jax.shard_map(local, mesh=mesh, in_specs=in_specs, out_specs=out_specs, check_vma=False)
```

time: 1110 us -> 857 us (0.77)
  waiting for transfers between devices: 596 us -> 383 us
  blocking collectives: 104 us -> 20.3 us
  matrix products: 152 us -> 76.4 us
  starting transfers between devices: 23.8 us -> 93.9 us
  Pallas kernels: 0 us -> 55 us
  other arithmetic: 111 us -> 124 us
  local copies, waits for them, and re-layouts: 80.5 us -> 67.5 us
    ppermute x32 -> x51, waiting for transfers between devices: 364 us -> 215 us  [swap_bit(): return lax.ppermute(value, ('section', 'dp'), pairs)]
    ppermute x3, waiting for transfers between devices: 136 us -> 50.6 us  [to_encoder(): return lax.ppermute(value, 'dp', [(1, 0)])]
    pallas_call x0 -> x4, Pallas kernels: none -> 55 us  [the longest x1 20.6 us: attention_backward(): pl.pallas_call(functools.partial(attention_backward_kernel, biased, cross...]
    dot_general x12 -> x5, matrix products: 84.3 us -> 31.8 us  [forward_mul(): return jnp.dot(left, right, preferred_element_type=jnp.float32)]
    unnamed x1 -> x0, blocking collectives: 43.5 us -> none
    ppermute x4 -> x9, starting transfers between devices: 0.28 us -> 41.2 us  [swap_half(): return lax.ppermute(value, 'dp', [(0, 1), (1, 0)])]
    psum x1 -> x0, blocking collectives: 39.8 us -> none  [local(): sums = lax.psum(sums, ('section', 'dp'))]
    ppermute x32 -> x51, starting transfers between devices: 14.3 us -> 43.8 us  [swap_bit(): return lax.ppermute(value, ('section', 'dp'), pairs)]
  transfers between devices with their start and end apart: 50 -> 68, of which waited for: 33 -> 42; matrix products, arithmetic and copies ran while one was open for 18% -> 21% of each run, Pallas kernels for 0% -> 5%
where the time goes in v2:
time: 857 us; the launch traced here: 847 us
  waiting for transfers between devices  383 us (45%)
  other arithmetic  124 us (14%)
  starting transfers between devices  93.9 us (11%)
  matrix products  76.4 us (9%)
  local copies, waits for them, and re-layouts  67.5 us (8%)
  Pallas kernels  55 us (6%)
  between operations  26.3 us (3%)
  blocking collectives  20.3 us (2%)
    ppermute x51, waiting for transfers between devices, swap_bit(): return lax.ppermute(value, ('section', 'dp'), pairs)  215 us
    ppermute x9, waiting for transfers between devices, swap_half(): return lax.ppermute(value, 'dp', [(0, 1), (1, 0)])  56.7 us
    ppermute x3, waiting for transfers between devices, to_encoder(): return lax.ppermute(value, 'dp', [(1, 0)])  50.6 us
    ppermute x51, starting transfers between devices, swap_bit(): return lax.ppermute(value, ('section', 'dp'), pairs)  43.8 us
    all_gather x1, waiting for transfers between devices, local(): all_rows = lax.all_gather(head_low, 'section', axis=0, tiled=True)  42.9 us
    ppermute x9, starting transfers between devices, swap_half(): return lax.ppermute(value, 'dp', [(0, 1), (1, 0)])  41.2 us
    convert_element_type x25, other arithmetic, to_low(): return values.astype(jnp.bfloat16)  32.7 us
    dot_general x5, matrix products, forward_mul(): return jnp.dot(left, right, preferred_element_type=jnp.float32)  31.8 us
  transfers between devices with their start and end apart: 68, of which 42 were waited for; matrix products, arithmetic and copies ran while one was open for 21% of the time, Pallas kernels for 5%

profile of v2, /device:TPU:0, one launch (start us, length us, event | category | flops | bytes accessed | tf_op | source)
XLA Modules:
  0.0 847.4 jit_solution(17012189216324194621)
XLA Ops:
  13.0 3.0 collective-permute-start
  26.6 3.1 collective-permute-start.4
  29.7 3.1 convert_element_type.474
  33.1 8.7 %fusion.19 = bf16[2048,768]{1,0:T(8,128)(2,1)} fusion(bf16[2008,768]{1,0:T(8,128)(2,1)S(1)} %convert_element_type.474, s32[2048]{0:T(1024)S(1)} %bitcast.520), kind=kOutput, calls=%fused_computation.39 | convolution fusion | flops 6322307072 | bytes 6238208 | tf_op jit(solution)/shard_map/dot_general | solution.py:176
  43.5 4.2 collective-permute-done.5
  47.7 9.2 %fusion.26 = bf16[2048,768]{1,0:T(8,128)(2,1)S(1)} fusion(bf16[2048,768]{1,0:T(8,128)(2,1)} %collective-permute-done.5, bf16[2008,768]{1,0:T(8,128)(2,1)S(1)} %convert_element_type.474, s32[2048]{0:T(1024)S(1)} %bitcast.519), kind=kOutput, calls=%fused_computation.54 | convolution fusion | flops 6323879936 | bytes 9383936 | tf_op jit(solution)/shard_map/dot_general | solution.py:176
  65.1 30.5 %collective-permute-done.6 = bf16[512,768]{1,0:T(8,128)(2,1)} collective-permute-done((bf16[512,768]{1,0:T(8,128)(2,1)}, bf16[512,768]{1,0:T(8,128)(2,1)}, u32[]{:S(2)}, u32[]{:S(2)}) %collective-permute-start.6) | collective-permute-done | bytes 786464 | tf_op jit(solution)/shard_map/ppermute | solution.py:66
  97.0 3.5 collective-permute-done.9
  104.5 21.0 %collective-permute-done.7 = bf16[256,768]{1,0:T(8,128)(2,1)S(1)} collective-permute-done((bf16[256,768]{1,0:T(8,128)(2,1)S(1)}, bf16[256,768]{1,0:T(8,128)(2,1)S(1)}, u32[]{:S(2)}, u32[]{:S(2)}) %collective-permute-start.7) | collective-permute-done | bytes 393248 | tf_op jit(solution)/shard_map/ppermute | solution.py:66
  128.1 5.2 collective-permute-done.10
  135.8 9.2 %collective-permute-done.11 = bf16[128,768]{1,0:T(8,128)(2,1)S(1)} collective-permute-done((bf16[128,768]{1,0:T(8,128)(2,1)S(1)}, bf16[128,768]{1,0:T(8,128)(2,1)S(1)}, u32[]{:S(2)}, u32[]{:S(2)}) %collective-permute-start.11) | collective-permute-done | bytes 196640 | tf_op jit(solution)/shard_map/ppermute | solution.py:66
  145.6 7.5 all-gather.7.cloned.1.call-done.refs_2_
  153.1 12.3 %attention_forward.3 = (f32[256,768]{1,0:T(8,128)}, bf16[256,768]{1,0:T(8,128)(2,1)}, bf16[256,768]{1,0:T(8,128)(2,1)}, bf16[256,768]{1,0:T(8,128)(2,1)}, bf16[2...) custom-call(f32[256,768]{1,0:T(8,128)S(1)} %maximum_convert_fusion.1.refs_0_, f32[1,768]{1,0:T(1,128)S(1)} %get-tuple-element.633.refs_1_, ...), custom_call_target="tpu_custom_call" | custom-call | tf_op jit(solution)/shard_map/attention_forward/pallas_call | solution.py:451
  166.7 8.8 %conditional.5 = ((f32[256,768]{1,0:T(8,128)}, bf16[256,768]{1,0:T(8,128)(2,1)}, f32[256,3072]{1,0:T(8,128)S(1)})) conditional(s32[]{:T(128)} %convert_element_type.473, () %tuple.161, (f32[7,768]{1,0:T(8,128)}, f32[256,768]{1,0:T(8,128)}, f32[1,768]{1,0:T(1,128)S(1)}, bf16[4,3072,768]{2,1,0:T(8,128)(2,1)}) %tuple.168), branch_computations={%region_0.1_spmd, %region_1.2_spmd} | conditional | bytes 4325418 | solution.py:738
  167.5 8.0 feed_forward.2
  182.5 7.6 collective-permute-done.13
  190.9 6.2 conditional.6
  199.2 21.3 %collective-permute-done.15 = bf16[128,768]{1,0:T(8,128)(2,1)S(1)} collective-permute-done((bf16[128,768]{1,0:T(8,128)(2,1)S(1)}, bf16[128,768]{1,0:T(8,128)(2,1)S(1)}, u32[]{:S(2)}, u32[]{:S(2)}) %collective-permute-start.15) | collective-permute-done | bytes 196640 | tf_op jit(solution)/shard_map/ppermute | solution.py:78
  222.1 42.9 %all-gather.9.cloned.1.call-done = bf16[2048,768]{1,0:T(8,128)(2,1)} async-done(((bf16[128,768]{1,0:T(8,128)(2,1)}), bf16[2048,768]{1,0:T(8,128)(2,1)}) %all-gather.9.cloned.1.call-update) | async-done | bytes 3145744 | tf_op jit(solution)/shard_map/all_gather | solution.py:772
  265.0 9.6 %fusion.116 = (f32[2048]{0:T(1024)S(1)}, f32[2048,2008]{0,1:T(8,128)S(1)}) fusion(bf16[2048,768]{1,0:T(8,128)(2,1)} %all-gather.9.cloned.1.call-done, bf16[2008,768]{1,0:T(8,128)(2,1)} %copy-done.19), kind=kOutput, calls=%fused_computation.318 | convolution fusion | flops 6320732160 | bytes 22687744 | tf_op jit(solution)/shard_map/nd,vd->nv/dot_general | solution.py:773
  274.7 5.2 select_reduce_fusion
  279.8 20.3 %all-gather.2 = f32[16,2,2048]{2,1,0:T(2,128)S(1)} all-gather(f32[1,2,2048]{2,1,0:T(2,128)S(1)} %maximum_bitcast_fusion.1), channel_id=2, replica_groups=mesh['section'=16,'dp'=2] {'section'}, dimensions={0}, use_global_device_ids=true | all-gather | bytes 278528 | tf_op jit(solution)/shard_map/all_gather | solution.py:778
  300.6 4.2 subtract_convert_fusion
  304.8 7.4 fusion.117
  318.1 8.5 %fusion.118 = f32[2008,768]{1,0:T(8,128)} fusion(bf16[2048,2008]{0,1:T(8,128)(2,1)S(1)} %subtract_convert_fusion, bf16[2048,768]{1,0:T(8,128)(2,1)S(1)} %copy-done.103), kind=kOutput, calls=%fused_computation.320 | convolution fusion | flops 6316621824 | bytes 17539072 | tf_op jit(solution)/shard_map/dot_general | solution.py:199
  326.7 9.6 %collective-permute-done.17 = bf16[512,768]{1,0:T(8,128)(2,1)S(1)} collective-permute-done((bf16[512,768]{1,0:T(8,128)(2,1)S(1)}, bf16[512,768]{1,0:T(8,128)(2,1)S(1)}, u32[]{:S(2)}, u32[]{:S(2)}) %collective-permute-start.17) | collective-permute-done | bytes 786464 | tf_op jit(solution)/shard_map/ppermute | solution.py:66
  336.6 10.6 %collective-permute-done.18 = bf16[256,768]{1,0:T(8,128)(2,1)S(1)} collective-permute-done((bf16[256,768]{1,0:T(8,128)(2,1)S(1)}, bf16[256,768]{1,0:T(8,128)(2,1)S(1)}, u32[]{:S(2)}, u32[]{:S(2)}) %collective-permute-start.18) | collective-permute-done | bytes 393248 | tf_op jit(solution)/shard_map/ppermute | solution.py:66
  348.9 9.1 %collective-permute-done.19 = bf16[128,768]{1,0:T(8,128)(2,1)S(1)} collective-permute-done((bf16[128,768]{1,0:T(8,128)(2,1)S(1)}, bf16[128,768]{1,0:T(8,128)(2,1)S(1)}, u32[]{:S(2)}, u32[]{:S(2)}) %collective-permute-start.19) | collective-permute-done | bytes 196640 | tf_op jit(solution)/shard_map/ppermute | solution.py:66
  358.1 3.4 collective-permute-start.20
  365.8 11.5 %conditional.7 = (bf16[256,768]{1,0:T(8,128)(2,1)}, f32[256,768]{1,0:T(8,128)}, bf16[1536,768]{1,0:T(8,128)(2,1)}, bf16[1536,768]{1,0:T(8,128)(2,1)}, bf16[1536,...) conditional(s32[]{:T(128)} %convert_element_type.472, ...), branch_computations={%region_12.13_spmd, %region_13.14_spmd} | conditional | flops 2309 | bytes 15344734 | solution.py:828
  379.2 9.2 %collective-permute-done.22 = bf16[2,192,768]{2,1,0:T(8,128)(2,1)} collective-permute-done((bf16[2,192,768]{2,1,0:T(8,128)(2,1)}, bf16[2,192,768]{2,1,0:T(8,128)(2,1)}, u32[]{:S(2)}, u32[]{:S(2)}) %collective-permute-start.22) | collective-permute-done | bytes 589856 | tf_op jit(solution)/shard_map/ppermute | solution.py:66
  388.4 25.7 %collective-permute-done.21 = bf16[256,768]{1,0:T(8,128)(2,1)S(1)} collective-permute-done((bf16[256,768]{1,0:T(8,128)(2,1)}, bf16[256,768]{1,0:T(8,128)(2,1)S(1)}, u32[]{:S(2)}, u32[]{:S(2)}) %collective-permute-start.21) | collective-permute-done | bytes 393248 | tf_op jit(solution)/shard_map/ppermute | solution.py:78
  416.1 15.9 %conditional.8 = (f32[256,768]{1,0:T(8,128)}, f32[2,768]{1,0:T(2,128)}, f32[12,128,128]{2,1,0:T(8,128)}, bf16[1536,768]{1,0:T(8,128)(2,1)}, bf16[1536,768]{1,0:T...) conditional(s32[]{:T(128)} %convert_element_type.473, (f32[256,768]{1,0:T(8,128)}, ...), branch_computations={%region_14.15_spmd, %region_15.16_spmd} | conditional | flops 198149 | bytes 1188976 | solution.py:866
  417.0 14.1 %feed_backward.3 = (f32[256,768]{1,0:T(8,128)}, bf16[1536,768]{1,0:T(8,128)(2,1)}, bf16[1536,768]{1,0:T(8,128)(2,1)}, bf16[1536,768]{1,0:T(8,128)(2,1)}, bf16[1536,768]{1,0:T(8,128)(2,1)}, /*index=5*/f32[2,768]{1,0:T(2,128)}) custom-call(s32[1]{0:T(128)} %bitcast.3.mine_ref, bf16[256,768]{1,0:T(8,128)(2,1)S(1)} %get-tuple-element.188.upstream_ref, ...), custom_call_target="tpu_custom_call" | custom-call | tf_op jit(solution)/shard_map/cond/branch_1_fun/feed_backward/pallas_call | solution.py:353
  435.5 3.1 add_convert_fusion.3
  441.6 21.7 %conditional.9 = (bf16[256,768]{1,0:T(8,128)(2,1)}, f32[12,128,128]{2,1,0:T(8,128)}, bf16[1536,768]{1,0:T(8,128)(2,1)}, bf16[1536,768]{1,0:T(8,128)(2,1)}, f32[5376]{0:T(1024)S(1)}) conditional(s32[]{:T(128)} %convert_element_type.473, (f32[256,768]{1,0:T(8,128)}, f32[2,768]{1,0:T(2,128)}, f32[3,768]{1,0:T(4,128)S(1)}, f32[12,128,128]{2,1,0:T(8,128)}, ...), branch_computations={%region_16.17_spmd, %region_17.18_spmd} | conditional | flops 207360 | bytes 1262720 | solution.py:882
  441.6 20.6 %attention_backward.5 = (bf16[256,768]{1,0:T(8,128)(2,1)}, bf16[1536,768]{1,0:T(8,128)(2,1)}, bf16[1536,768]{1,0:T(8,128)(2,1)}, f32[1,768]{1,0:T(1,128)S(1)}, f32[12,128,128]{2,1,0:T(8,128)}) custom-call(s32[1]{0:T(128)} %bitcast.4.mine_ref, f32[256,768]{1,0:T(8,128)} %get-tuple-element.207.refs_0_, f32[256,768]{1,0:T(8,128)S(1)} %get-tuple-element.208.refs_1_, ...), custom_call_target="tpu_custom_call" | custom-call | tf_op jit(solution)/shard_map/cond/branch_1_fun/attention_backward/pallas_call | solution.py:547
  481.9 14.5 %collective-permute-start.50 = (f32[48,128]{1,0:T(8,128)S(1)}, f32[48,128]{1,0:T(8,128)S(1)}, u32[]{:S(2)}, u32[]{:S(2)}) collective-permute-start(f32[48,128]{1,0:T(8,128)S(1)} %maximum_bitcast_fusion), channel_id=1, source_target_pairs={{0,1},{1,0},{2,3},{3,2},{4,5},{5,4},{6,7},{7,6},{8,9},{9,8},{10,11... | collective-permute-start | bytes 73736 | tf_op jit(solution)/shard_map/ppermute | solution.py:70
  498.7 8.8 %collective-permute-done.36 = bf16[768,768]{1,0:T(8,128)(2,1)} collective-permute-done((bf16[768,768]{1,0:T(8,128)(2,1)}, bf16[768,768]{1,0:T(8,128)(2,1)}, u32[]{:S(2)}, u32[]{:S(2)}) %collective-permute-start.36) | collective-permute-done | bytes 1179680 | tf_op jit(solution)/shard_map/ppermute | solution.py:66
  511.5 37.7 %collective-permute-done.41 = bf16[768,768]{1,0:T(8,128)(2,1)} collective-permute-done((bf16[768,768]{1,0:T(8,128)(2,1)}, bf16[768,768]{1,0:T(8,128)(2,1)}, u32[]{:S(2)}, u32[]{:S(2)}) %collective-permute-start.41) | collective-permute-done | bytes 1179680 | tf_op jit(solution)/shard_map/ppermute | solution.py:66
  557.6 19.2 %collective-permute-done.40 = bf16[192,768]{1,0:T(8,128)(2,1)S(1)} collective-permute-done((bf16[192,768]{1,0:T(8,128)(2,1)S(1)}, bf16[192,768]{1,0:T(8,128)(2,1)S(1)}, u32[]{:S(2)}, u32[]{:S(2)}) %collective-permute-start.40) | collective-permute-done | bytes 294944 | tf_op jit(solution)/shard_map/ppermute | solution.py:66
  584.3 8.8 %collective-permute-done.43 = bf16[192,768]{1,0:T(8,128)(2,1)S(1)} collective-permute-done((bf16[192,768]{1,0:T(8,128)(2,1)S(1)}, bf16[192,768]{1,0:T(8,128)(2,1)S(1)}, u32[]{:S(2)}, u32[]{:S(2)}) %collective-permute-start.43) | collective-permute-done | bytes 294944 | tf_op jit(solution)/shard_map/ppermute | solution.py:66
  596.1 6.9 fusion.36
  603.0 7.7 collective-permute-start.30
  610.7 5.0 fusion.42
  616.0 4.8 fusion.41
  622.7 22.7 %collective-permute-done.28 = bf16[496,768]{1,0:T(8,128)(2,1)S(1)} collective-permute-done((bf16[496,768]{1,0:T(8,128)(2,1)S(1)}, bf16[496,768]{1,0:T(8,128)(2,1)S(1)}, u32[]{:S(2)}, u32[]{:S(2)}) %collective-permute-start.28) | collective-permute-done | bytes 761888 | tf_op jit(solution)/shard_map/ppermute | solution.py:70
  647.6 5.0 fusion.40
  654.7 7.0 collective-permute-done.29
  665.7 11.4 %collective-permute-done.31 = bf16[504,768]{1,0:T(8,128)(2,1)S(1)} collective-permute-done((bf16[504,768]{1,0:T(8,128)(2,1)S(1)}, bf16[504,768]{1,0:T(8,128)(2,1)S(1)}, u32[]{:S(2)}, u32[]{:S(2)}) %collective-permute-start.31) | collective-permute-done | bytes 774176 | tf_op jit(solution)/shard_map/ppermute | solution.py:70
  680.0 3.0 multiply_reduce_fusion.5
  686.7 7.0 collective-permute-done.45
  696.3 3.5 multiply_reduce_fusion.6
  702.9 3.0 collective-permute-done.52
  706.2 3.5 collective-permute-done.53
  717.4 3.6 collective-permute-start.56
  732.0 3.2 convert_add_fusion.9
  742.1 3.5 convert_add_fusion.8
  754.3 6.0 collective-permute-start.48
  762.9 3.6 collective-permute-done.57
  783.3 13.9 %collective-permute-done.64 = bf16[4,4,48,768]{3,2,1,0:T(8,128)(2,1)} collective-permute-done((bf16[4,4,48,768]{3,2,1,0:T(8,128)(2,1)S(1)}, bf16[4,4,48,768]{3,2,1,0:T(8,128)(2,1)}, u32[]{:S(2)}, u32[]{:S(2)}) %collective-permute-start.64) | collective-permute-done | bytes 1179680 | tf_op jit(solution)/shard_map/ppermute | solution.py:70
  812.0 4.3 multiply_subtract_fusion.1
  820.2 5.1 fusion.30
  826.7 12.8 %multiply_subtract_fusion = (f32[2008,768]{1,0:T(8,128)}, f32[2008,768]{1,0:T(8,128)}, f32[2008,768]{1,0:T(8,128)}) fusion(f32[2008,768]{1,0:T(8,128)S(1)} %bitcast.407, f32[]{:T(128)S(6)} %div.101, f32[504,768]{1,0:T(8,128)S(1)} %copy-done.13, f32[512,768]{1,0:T(8,128)S(1)} %copy-done.12, f32[496,768]{1,0:T(8,128)S(1)} %copy-done.14, ...), kind=kLoop, calls=%fused_computation.25 | loop fusion | flops 29300736 | bytes 43180036 | tf_op jit(solution)/shard_map/sub | solution.py:572
  (525 shorter events, 223.8 us)
Async XLA Ops:
  7.2 145.9 %all-gather.7.cloned.1.call-start = ((), (), s32[]{:S(2)}) async-start(), calls=%async_computation | async-start | bytes 20054016 | tf_op jit(solution)/shard_map/all_gather | solution.py:704
  12.3 252.7 %all-gather.9.cloned.1.call-start = ((), (), s32[]{:S(2)}) async-start(), calls=%async_computation.1 | async-start | bytes 3342336 | tf_op jit(solution)/shard_map/all_gather | solution.py:772
  13.0 4.6 collective-permute-start
  18.8 3.7 collective-permute-start.2
  22.5 4.1 collective-permute-start.3
  26.6 6.3 collective-permute-start.4
  41.7 6.0 collective-permute-start.5
  58.2 37.4 %collective-permute-start.6 = (bf16[512,768]{1,0:T(8,128)(2,1)}, bf16[512,768]{1,0:T(8,128)(2,1)}, u32[]{:S(2)}, u32[]{:S(2)}) collective-permute-start(bf16[512,768]{1,0:T(8,128)(2,1)} %bitcast.28), channel_id=1, source_target_pairs={{0,4},{1,5},{2,6},{3,7},{4,0},{5,1},{6,2},{7,3},{8,12},{9,13},{10,... | collective-permute-start | bytes 2359304 | tf_op jit(solution)/shard_map/ppermute | solution.py:66
  63.2 37.3 %collective-permute-start.9 = (bf16[512,768]{1,0:T(8,128)(2,1)S(1)}, bf16[512,768]{1,0:T(8,128)(2,1)S(1)}, u32[]{:S(2)}, u32[]{:S(2)}) collective-permute-start(bf16[512,768]{1,0:T(8,128)(2,1)S(1)} %bitcast.484), channel_id=1, source_target_pairs={{0,8},{1,9},{2,10},{3,11},{4,12},{5,13},{6,14},{7,15},{8,0},{9,1},... | collective-permute-start | bytes 2359304 | tf_op jit(solution)/shard_map/ppermute | solution.py:66
  97.0 28.6 %collective-permute-start.7 = (bf16[256,768]{1,0:T(8,128)(2,1)S(1)}, bf16[256,768]{1,0:T(8,128)(2,1)S(1)}, u32[]{:S(2)}, u32[]{:S(2)}) collective-permute-start(bf16[256,768]{1,0:T(8,128)(2,1)S(1)} %bitcast.497), channel_id=1, source_target_pairs={{0,8},{1,9},{2,10},{3,11},{4,12},{5,13},{6,14},{7,15},{8,0},{9,1},... | collective-permute-start | bytes 1179656 | tf_op jit(solution)/shard_map/ppermute | solution.py:66
  101.5 31.7 %collective-permute-start.10 = (bf16[256,768]{1,0:T(8,128)(2,1)}, bf16[256,768]{1,0:T(8,128)(2,1)}, u32[]{:S(2)}, u32[]{:S(2)}) collective-permute-start(bf16[256,768]{1,0:T(8,128)(2,1)} %dynamic-slice_bitcast_fusion.13), channel_id=1, source_target_pairs={{0,16},{1,17},{2,18},{3,19},{4,20},{5,21},{6,22},{7,23},{8,24},{9,... | collective-permute-start | bytes 1179656 | tf_op jit(solution)/shard_map/ppermute | solution.py:66
  125.7 19.7 %collective-permute-start.8 = (bf16[128,768]{1,0:T(8,128)(2,1)S(1)}, bf16[128,768]{1,0:T(8,128)(2,1)S(1)}, u32[]{:S(2)}, u32[]{:S(2)}) collective-permute-start(bf16[128,768]{1,0:T(8,128)(2,1)S(1)} %dynamic-slice_bitcast_fusion.20), channel_id=1, source_target_pairs={{0,16},{1,17},{2,18},{3,19},{4,20},{5,21},{6,22},{7,23},{8,24},{9,... | collective-permute-start | bytes 589832 | tf_op jit(solution)/shard_map/ppermute | solution.py:66
  134.4 10.5 %collective-permute-start.11 = (bf16[128,768]{1,0:T(8,128)(2,1)S(1)}, bf16[128,768]{1,0:T(8,128)(2,1)S(1)}, u32[]{:S(2)}, u32[]{:S(2)}) collective-permute-start(bf16[128,768]{1,0:T(8,128)(2,1)S(1)} %dynamic-slice_bitcast_fusion.19), channel_id=1, source_target_pairs={{0,4},{1,5},{2,6},{3,7},{4,0},{5,1},{6,2},{7,3},{8,12},{9,13},{10,... | collective-permute-start | bytes 589832 | tf_op jit(solution)/shard_map/ppermute | solution.py:66
  166.5 9.0 %collective-permute-start.12 = (bf16[4,2,48,768]{3,2,1,0:T(8,128)(2,1)}, bf16[4,2,48,768]{3,2,1,0:T(8,128)(2,1)}, u32[]{:S(2)}, u32[]{:S(2)}) collective-permute-start(bf16[4,2,48,768]{3,2,1,0:T(8,128)(2,1)} %get-tuple-element.620), channel_id=1, source_target_pairs={{0,2},{1,3},{2,0},{3,1},{4,6},{5,7},{6,4},{7,5},{8,10},{9,11},{10,... | collective-permute-start | bytes 1769480 | tf_op jit(solution)/shard_map/ppermute | solution.py:66
  178.4 18.7 %collective-permute-start.14 = (bf16[4,2,48,768]{3,2,1,0:T(8,128)(2,1)}, bf16[4,2,48,768]{3,2,1,0:T(8,128)(2,1)}, u32[]{:S(2)}, u32[]{:S(2)}) collective-permute-start(bf16[4,2,48,768]{3,2,1,0:T(8,128)(2,1)} %get-tuple-element.618), channel_id=1, source_target_pairs={{0,4},{1,5},{2,6},{3,7},{4,0},{5,1},{6,2},{7,3},{8,12},{9,13},{10,... | collective-permute-start | bytes 1769480 | tf_op jit(solution)/shard_map/ppermute | solution.py:66
  179.7 10.4 %collective-permute-start.13 = (bf16[256,768]{1,0:T(8,128)(2,1)}, bf16[256,768]{1,0:T(8,128)(2,1)S(1)}, u32[]{:S(2)}, u32[]{:S(2)}) collective-permute-start(bf16[256,768]{1,0:T(8,128)(2,1)} %get-tuple-element.372), channel_id=1, source_target_pairs={{0,1},{2,3},{4,5},{6,7},{8,9},{10,11},{12,13},{14,15},{16,17},{18,... | collective-permute-start | bytes 1179656 | tf_op jit(solution)/shard_map/ppermute | solution.py:74
  197.1 23.4 %collective-permute-start.15 = (bf16[128,768]{1,0:T(8,128)(2,1)S(1)}, bf16[128,768]{1,0:T(8,128)(2,1)S(1)}, u32[]{:S(2)}, u32[]{:S(2)}) collective-permute-start(bf16[128,768]{1,0:T(8,128)(2,1)S(1)} %slice.167), channel_id=1, source_target_pairs={{1,0},{3,2},{5,4},{7,6},{9,8},{11,10},{13,12},{15,14},{17,16},{19,... | collective-permute-start | bytes 589832 | tf_op jit(solution)/shard_map/ppermute | solution.py:78
  221.3 374.8 %all-gather.11.cloned.1.call-start = ((), (), s32[]{:S(2)}) async-start(), calls=%async_computation.2 | async-start | bytes 6684672 | tf_op jit(solution)/shard_map/all_gather | solution.py:901
  316.4 19.9 %collective-permute-start.17 = (bf16[512,768]{1,0:T(8,128)(2,1)S(1)}, bf16[512,768]{1,0:T(8,128)(2,1)S(1)}, u32[]{:S(2)}, u32[]{:S(2)}) collective-permute-start(bf16[512,768]{1,0:T(8,128)(2,1)S(1)} %bitcast.485), channel_id=1, source_target_pairs={{0,4},{1,5},{2,6},{3,7},{4,0},{5,1},{6,2},{7,3},{8,12},{9,13},{10,... | collective-permute-start | bytes 2359304 | tf_op jit(solution)/shard_map/ppermute | solution.py:66
  336.5 10.6 %collective-permute-start.18 = (bf16[256,768]{1,0:T(8,128)(2,1)S(1)}, bf16[256,768]{1,0:T(8,128)(2,1)S(1)}, u32[]{:S(2)}, u32[]{:S(2)}) collective-permute-start(bf16[256,768]{1,0:T(8,128)(2,1)S(1)} %bitcast.498), channel_id=1, source_target_pairs={{0,8},{1,9},{2,10},{3,11},{4,12},{5,13},{6,14},{7,15},{8,0},{9,1},... | collective-permute-start | bytes 1179656 | tf_op jit(solution)/shard_map/ppermute | solution.py:66
  347.3 10.6 %collective-permute-start.19 = (bf16[128,768]{1,0:T(8,128)(2,1)S(1)}, bf16[128,768]{1,0:T(8,128)(2,1)S(1)}, u32[]{:S(2)}, u32[]{:S(2)}) collective-permute-start(bf16[128,768]{1,0:T(8,128)(2,1)S(1)} %dynamic-slice_bitcast_fusion.18), channel_id=1, source_target_pairs={{0,16},{1,17},{2,18},{3,19},{4,20},{5,21},{6,22},{7,23},{8,24},{9,... | collective-permute-start | bytes 589832 | tf_op jit(solution)/shard_map/ppermute | solution.py:66
  358.1 7.7 collective-permute-start.20
  362.8 25.6 %collective-permute-start.22 = (bf16[2,192,768]{2,1,0:T(8,128)(2,1)}, bf16[2,192,768]{2,1,0:T(8,128)(2,1)}, u32[]{:S(2)}, u32[]{:S(2)}) collective-permute-start(bf16[2,192,768]{2,1,0:T(8,128)(2,1)} %get-tuple-element.616), channel_id=1, source_target_pairs={{0,16},{1,17},{2,18},{3,19},{4,20},{5,21},{6,22},{7,23},{8,24},{9,... | collective-permute-start | bytes 1769480 | tf_op jit(solution)/shard_map/ppermute | solution.py:66
  377.9 36.2 %collective-permute-start.21 = (bf16[256,768]{1,0:T(8,128)(2,1)}, bf16[256,768]{1,0:T(8,128)(2,1)S(1)}, u32[]{:S(2)}, u32[]{:S(2)}) collective-permute-start(bf16[256,768]{1,0:T(8,128)(2,1)} %get-tuple-element.395), channel_id=1, source_target_pairs={{1,0},{3,2},{5,4},{7,6},{9,8},{11,10},{13,12},{15,14},{17,16},{19,... | collective-permute-start | bytes 1179656 | tf_op jit(solution)/shard_map/ppermute | solution.py:78
  414.1 21.4 %collective-permute-start.25 = (bf16[1536,768]{1,0:T(8,128)(2,1)}, bf16[1536,768]{1,0:T(8,128)(2,1)}, u32[]{:S(2)}, u32[]{:S(2)}) collective-permute-start(bf16[1536,768]{1,0:T(8,128)(2,1)} %get-tuple-element.423), channel_id=1, source_target_pairs={{1,3},{3,1},{5,7},{7,5},{9,11},{11,9},{13,15},{15,13},{17,19},{19,... | collective-permute-start | bytes 7077896 | tf_op jit(solution)/shard_map/ppermute | solution.py:66
  432.0 31.6 %collective-permute-start.23 = (bf16[1536,768]{1,0:T(8,128)(2,1)}, bf16[1536,768]{1,0:T(8,128)(2,1)}, u32[]{:S(2)}, u32[]{:S(2)}) collective-permute-start(bf16[1536,768]{1,0:T(8,128)(2,1)} %get-tuple-element.420), channel_id=1, source_target_pairs={{0,2},{1,3},{2,0},{3,1},{4,6},{5,7},{6,4},{7,5},{8,10},{9,11},{10,... | collective-permute-start | bytes 7077896 | tf_op jit(solution)/shard_map/ppermute | solution.py:66
  432.0 31.6 %collective-permute-start.24 = (bf16[1536,768]{1,0:T(8,128)(2,1)}, bf16[1536,768]{1,0:T(8,128)(2,1)}, u32[]{:S(2)}, u32[]{:S(2)}) collective-permute-start(bf16[1536,768]{1,0:T(8,128)(2,1)} %get-tuple-element.421), channel_id=1, source_target_pairs={{0,2},{1,3},{2,0},{3,1},{4,6},{5,7},{6,4},{7,5},{8,10},{9,11},{10,... | collective-permute-start | bytes 7077896 | tf_op jit(solution)/shard_map/ppermute | solution.py:66
  435.5 28.2 %collective-permute-start.27 = (bf16[2,2,192,768]{3,2,0,1:T(8,128)(2,1)}, bf16[2,2,192,768]{3,2,0,1:T(8,128)(2,1)}, u32[]{:S(2)}, u32[]{:S(2)}) collective-permute-start(bf16[2,2,192,768]{3,2,0,1:T(8,128)(2,1)} %maximum_select_fusion.4), channel_id=1, source_target_pairs={{0,8},{1,9},{2,10},{3,11},{4,12},{5,13},{6,14},{7,15},{8,0},{9,1},... | collective-permute-start | bytes 3538952 | tf_op jit(solution)/shard_map/ppermute | solution.py:66
  439.7 23.9 %collective-permute-start.26 = (bf16[768,768]{1,0:T(8,128)(2,1)}, bf16[768,768]{1,0:T(8,128)(2,1)}, u32[]{:S(2)}, u32[]{:S(2)}) collective-permute-start(bf16[768,768]{1,0:T(8,128)(2,1)} %dynamic-slice_bitcast_fusion.3), channel_id=1, source_target_pairs={{1,5},{3,7},{5,1},{7,3},{9,13},{11,15},{13,9},{15,11},{17,21},{19,... | collective-permute-start | bytes 3538952 | tf_op jit(solution)/shard_map/ppermute | solution.py:66
  466.0 87.8 %collective-permute-start.32 = (bf16[1536,768]{1,0:T(8,128)(2,1)}, bf16[1536,768]{1,0:T(8,128)(2,1)}, u32[]{:S(2)}, u32[]{:S(2)}) collective-permute-start(bf16[1536,768]{1,0:T(8,128)(2,1)} %get-tuple-element.432), channel_id=1, source_target_pairs={{0,2},{1,3},{2,0},{3,1},{4,6},{5,7},{6,4},{7,5},{8,10},{9,11},{10,... | collective-permute-start | bytes 7077896 | tf_op jit(solution)/shard_map/ppermute | solution.py:66
  469.1 27.4 %collective-permute-start.38 = (bf16[384,768]{1,0:T(8,128)(2,1)}, bf16[384,768]{1,0:T(8,128)(2,1)}, u32[]{:S(2)}, u32[]{:S(2)}) collective-permute-start(bf16[384,768]{1,0:T(8,128)(2,1)} %bitcast.111), channel_id=1, source_target_pairs={{1,9},{3,11},{5,13},{7,15},{9,1},{11,3},{13,5},{15,7},{17,25},{19,... | collective-permute-start | bytes 1769480 | tf_op jit(solution)/shard_map/ppermute | solution.py:66
  474.2 33.3 %collective-permute-start.36 = (bf16[768,768]{1,0:T(8,128)(2,1)}, bf16[768,768]{1,0:T(8,128)(2,1)}, u32[]{:S(2)}, u32[]{:S(2)}) collective-permute-start(bf16[768,768]{1,0:T(8,128)(2,1)} %dynamic-slice_bitcast_fusion.1), channel_id=1, source_target_pairs={{0,4},{1,5},{2,6},{3,7},{4,0},{5,1},{6,2},{7,3},{8,12},{9,13},{10,... | collective-permute-start | bytes 3538952 | tf_op jit(solution)/shard_map/ppermute | solution.py:66
  479.0 70.2 %collective-permute-start.41 = (bf16[768,768]{1,0:T(8,128)(2,1)}, bf16[768,768]{1,0:T(8,128)(2,1)}, u32[]{:S(2)}, u32[]{:S(2)}) collective-permute-start(bf16[768,768]{1,0:T(8,128)(2,1)} %dynamic-slice_bitcast_fusion), channel_id=1, source_target_pairs={{0,4},{1,5},{2,6},{3,7},{4,0},{5,1},{6,2},{7,3},{8,12},{9,13},{10,... | collective-permute-start | bytes 3538952 | tf_op jit(solution)/shard_map/ppermute | solution.py:66
  481.9 29.6 %collective-permute-start.50 = (f32[48,128]{1,0:T(8,128)S(1)}, f32[48,128]{1,0:T(8,128)S(1)}, u32[]{:S(2)}, u32[]{:S(2)}) collective-permute-start(f32[48,128]{1,0:T(8,128)S(1)} %maximum_bitcast_fusion), channel_id=1, source_target_pairs={{0,1},{1,0},{2,3},{3,2},{4,5},{5,4},{6,7},{7,6},{8,9},{9,8},{10,11... | collective-permute-start | bytes 73736 | tf_op jit(solution)/shard_map/ppermute | solution.py:70
  497.9 13.6 %collective-permute-start.39 = (bf16[192,768]{1,0:T(8,128)(2,1)S(1)}, bf16[192,768]{1,0:T(8,128)(2,1)S(1)}, u32[]{:S(2)}, u32[]{:S(2)}) collective-permute-start(bf16[192,768]{1,0:T(8,128)(2,1)S(1)} %dynamic-slice_bitcast_fusion.16), channel_id=1, source_target_pairs={{1,17},{3,19},{5,21},{7,23},{9,25},{11,27},{13,29},{15,31},{17,1},... | collective-permute-start | bytes 884744 | tf_op jit(solution)/shard_map/ppermute | solution.py:66
  509.1 43.6 %collective-permute-start.37 = (bf16[384,768]{1,0:T(8,128)(2,1)S(1)}, bf16[384,768]{1,0:T(8,128)(2,1)S(1)}, u32[]{:S(2)}, u32[]{:S(2)}) collective-permute-start(bf16[384,768]{1,0:T(8,128)(2,1)S(1)} %bitcast.491), channel_id=1, source_target_pairs={{0,8},{1,9},{2,10},{3,11},{4,12},{5,13},{6,14},{7,15},{8,0},{9,1},... | collective-permute-start | bytes 1769480 | tf_op jit(solution)/shard_map/ppermute | solution.py:66
  551.1 26.5 %collective-permute-start.42 = (bf16[384,768]{1,0:T(8,128)(2,1)S(1)}, bf16[384,768]{1,0:T(8,128)(2,1)S(1)}, u32[]{:S(2)}, u32[]{:S(2)}) collective-permute-start(bf16[384,768]{1,0:T(8,128)(2,1)S(1)} %bitcast.490), channel_id=1, source_target_pairs={{0,8},{1,9},{2,10},{3,11},{4,12},{5,13},{6,14},{7,15},{8,0},{9,1},... | collective-permute-start | bytes 1769480 | tf_op jit(solution)/shard_map/ppermute | solution.py:66
  553.0 23.9 %collective-permute-start.40 = (bf16[192,768]{1,0:T(8,128)(2,1)S(1)}, bf16[192,768]{1,0:T(8,128)(2,1)S(1)}, u32[]{:S(2)}, u32[]{:S(2)}) collective-permute-start(bf16[192,768]{1,0:T(8,128)(2,1)S(1)} %dynamic-slice_bitcast_fusion.15), channel_id=1, source_target_pairs={{0,16},{1,17},{2,18},{3,19},{4,20},{5,21},{6,22},{7,23},{8,24},{9,... | collective-permute-start | bytes 884744 | tf_op jit(solution)/shard_map/ppermute | solution.py:66
  556.8 38.1 %collective-permute-start.33 = (bf16[768,768]{1,0:T(8,128)(2,1)S(1)}, bf16[768,768]{1,0:T(8,128)(2,1)S(1)}, u32[]{:S(2)}, u32[]{:S(2)}) collective-permute-start(bf16[768,768]{1,0:T(8,128)(2,1)S(1)} %dynamic-slice_bitcast_fusion.2), channel_id=1, source_target_pairs={{0,4},{1,5},{2,6},{3,7},{4,0},{5,1},{6,2},{7,3},{8,12},{9,13},{10,... | collective-permute-start | bytes 3538952 | tf_op jit(solution)/shard_map/ppermute | solution.py:66
  557.6 24.5 %collective-permute-start.51 = (f32[48,128]{1,0:T(8,128)S(1)}, f32[48,128]{1,0:T(8,128)S(1)}, u32[]{:S(2)}, u32[]{:S(2)}) collective-permute-start(f32[48,128]{1,0:T(8,128)S(1)} %fusion.144), channel_id=1, source_target_pairs={{0,2},{1,3},{2,0},{3,1},{4,6},{5,7},{6,4},{7,5},{8,10},{9,11},{10,... | collective-permute-start | bytes 73736 | tf_op jit(solution)/shard_map/ppermute | solution.py:66
  577.8 15.3 %collective-permute-start.43 = (bf16[192,768]{1,0:T(8,128)(2,1)S(1)}, bf16[192,768]{1,0:T(8,128)(2,1)S(1)}, u32[]{:S(2)}, u32[]{:S(2)}) collective-permute-start(bf16[192,768]{1,0:T(8,128)(2,1)S(1)} %dynamic-slice_bitcast_fusion.14), channel_id=1, source_target_pairs={{0,16},{1,17},{2,18},{3,19},{4,20},{5,21},{6,22},{7,23},{8,24},{9,... | collective-permute-start | bytes 884744 | tf_op jit(solution)/shard_map/ppermute | solution.py:66
  593.8 68.0 %collective-permute-start.46 = (bf16[192,768]{1,0:T(8,128)(2,1)S(1)}, bf16[192,768]{1,0:T(8,128)(2,1)S(1)}, u32[]{:S(2)}, u32[]{:S(2)}) collective-permute-start(bf16[192,768]{1,0:T(8,128)(2,1)S(1)} %get-tuple-element.454), channel_id=1, source_target_pairs={{1,17},{3,19},{5,21},{7,23},{9,25},{11,27},{13,29},{15,31},{17,1},... | collective-permute-start | bytes 884744 | tf_op jit(solution)/shard_map/ppermute | solution.py:66
  596.1 49.3 %collective-permute-start.34 = (bf16[384,768]{1,0:T(8,128)(2,1)}, bf16[384,768]{1,0:T(8,128)(2,1)}, u32[]{:S(2)}, u32[]{:S(2)}) collective-permute-start(bf16[384,768]{1,0:T(8,128)(2,1)} %bitcast.98), channel_id=1, source_target_pairs={{0,8},{1,9},{2,10},{3,11},{4,12},{5,13},{6,14},{7,15},{8,0},{9,1},... | collective-permute-start | bytes 1769480 | tf_op jit(solution)/shard_map/ppermute | solution.py:66
  603.0 59.6 %collective-permute-start.30 = (bf16[512,768]{1,0:T(8,128)(2,1)S(1)}, bf16[512,768]{1,0:T(8,128)(2,1)S(1)}, u32[]{:S(2)}, u32[]{:S(2)}) collective-permute-start(bf16[512,768]{1,0:T(8,128)(2,1)S(1)} %fusion.36), channel_id=1, source_target_pairs={{0,1},{1,0},{2,3},{3,2},{4,5},{5,4},{6,7},{7,6},{8,9},{9,8},{10,11... | collective-permute-start | bytes 2359304 | tf_op jit(solution)/shard_map/ppermute | solution.py:70
  615.7 29.7 %collective-permute-start.28 = (bf16[496,768]{1,0:T(8,128)(2,1)S(1)}, bf16[496,768]{1,0:T(8,128)(2,1)S(1)}, u32[]{:S(2)}, u32[]{:S(2)}) collective-permute-start(bf16[496,768]{1,0:T(8,128)(2,1)S(1)} %fusion.42), channel_id=1, source_target_pairs={{0,1},{1,0},{2,3},{3,2},{4,5},{5,4},{6,7},{7,6},{8,9},{9,8},{10,11... | collective-permute-start | bytes 2285576 | tf_op jit(solution)/shard_map/ppermute | solution.py:70
  620.8 40.9 %collective-permute-start.29 = (bf16[496,768]{1,0:T(8,128)(2,1)S(1)}, bf16[496,768]{1,0:T(8,128)(2,1)S(1)}, u32[]{:S(2)}, u32[]{:S(2)}) collective-permute-start(bf16[496,768]{1,0:T(8,128)(2,1)S(1)} %fusion.41), channel_id=1, source_target_pairs={{0,1},{1,0},{2,3},{3,2},{4,5},{5,4},{6,7},{7,6},{8,9},{9,8},{10,11... | collective-permute-start | bytes 2285576 | tf_op jit(solution)/shard_map/ppermute | solution.py:70
  647.0 15.6 %collective-permute-start.35 = (bf16[192,768]{1,0:T(8,128)(2,1)S(1)}, bf16[192,768]{1,0:T(8,128)(2,1)S(1)}, u32[]{:S(2)}, u32[]{:S(2)}) collective-permute-start(bf16[192,768]{1,0:T(8,128)(2,1)S(1)} %dynamic-slice_bitcast_fusion.17), channel_id=1, source_target_pairs={{0,16},{1,17},{2,18},{3,19},{4,20},{5,21},{6,22},{7,23},{8,24},{9,... | collective-permute-start | bytes 884744 | tf_op jit(solution)/shard_map/ppermute | solution.py:66
  652.6 24.4 %collective-permute-start.31 = (bf16[504,768]{1,0:T(8,128)(2,1)S(1)}, bf16[504,768]{1,0:T(8,128)(2,1)S(1)}, u32[]{:S(2)}, u32[]{:S(2)}) collective-permute-start(bf16[504,768]{1,0:T(8,128)(2,1)S(1)} %fusion.40), channel_id=1, source_target_pairs={{0,1},{1,0},{2,3},{3,2},{4,5},{5,4},{6,7},{7,6},{8,9},{9,8},{10,11... | collective-permute-start | bytes 2322440 | tf_op jit(solution)/shard_map/ppermute | solution.py:70
  661.8 16.6 %collective-permute-start.47 = (bf16[2,192,768]{2,1,0:T(8,128)(2,1)S(1)}, bf16[2,192,768]{2,1,0:T(8,128)(2,1)S(1)}, u32[]{:S(2)}, u32[]{:S(2)}) collective-permute-start(bf16[2,192,768]{2,1,0:T(8,128)(2,1)S(1)} %fusion.62), channel_id=1, source_target_pairs={{1,9},{3,11},{5,13},{7,15},{9,1},{11,3},{13,5},{15,7},{17,25},{19,... | collective-permute-start | bytes 1769480 | tf_op jit(solution)/shard_map/ppermute | solution.py:66
  663.4 13.8 %collective-permute-start.44 = (bf16[192,768]{1,0:T(8,128)(2,1)S(1)}, bf16[192,768]{1,0:T(8,128)(2,1)S(1)}, u32[]{:S(2)}, u32[]{:S(2)}) collective-permute-start(bf16[192,768]{1,0:T(8,128)(2,1)S(1)} %get-tuple-element.450), channel_id=1, source_target_pairs={{0,16},{1,17},{2,18},{3,19},{4,20},{5,21},{6,22},{7,23},{8,24},{9,... | collective-permute-start | bytes 884744 | tf_op jit(solution)/shard_map/ppermute | solution.py:66
  678.2 15.4 %collective-permute-start.45 = (bf16[2,192,768]{2,1,0:T(8,128)(2,1)}, bf16[2,192,768]{2,1,0:T(8,128)(2,1)}, u32[]{:S(2)}, u32[]{:S(2)}) collective-permute-start(bf16[2,192,768]{2,1,0:T(8,128)(2,1)} %maximum_select_fusion.13), channel_id=1, source_target_pairs={{0,8},{1,9},{2,10},{3,11},{4,12},{5,13},{6,14},{7,15},{8,0},{9,1},... | collective-permute-start | bytes 1769480 | tf_op jit(solution)/shard_map/ppermute | solution.py:66
  685.1 35.9 %collective-permute-start.49 = (bf16[4,2,48,768]{3,2,1,0:T(8,128)(2,1)}, bf16[4,2,48,768]{3,2,1,0:T(8,128)(2,1)}, u32[]{:S(2)}, u32[]{:S(2)}) collective-permute-start(bf16[4,2,48,768]{3,2,1,0:T(8,128)(2,1)} %get-tuple-element.457), channel_id=1, source_target_pairs={{1,3},{3,1},{5,7},{7,5},{9,11},{11,9},{13,15},{15,13},{17,19},{19,... | collective-permute-start | bytes 1769480 | tf_op jit(solution)/shard_map/ppermute | solution.py:66
  702.0 19.1 %collective-permute-start.62 = (bf16[4,2,48,768]{3,2,1,0:T(8,128)(2,1)}, bf16[4,2,48,768]{3,2,1,0:T(8,128)(2,1)S(1)}, u32[]{:S(2)}, u32[]{:S(2)}) collective-permute-start(bf16[4,2,48,768]{3,2,1,0:T(8,128)(2,1)} %get-tuple-element.473), channel_id=1, source_target_pairs={{0,2},{1,3},{2,0},{3,1},{4,6},{5,7},{6,4},{7,5},{8,10},{9,11},{10,... | collective-permute-start | bytes 1769480 | tf_op jit(solution)/shard_map/ppermute | solution.py:66
  702.0 3.9 collective-permute-start.52
  705.9 3.8 collective-permute-start.53
  709.7 4.9 collective-permute-start.54
  717.4 17.8 %collective-permute-start.56 = (bf16[2,192,768]{2,1,0:T(8,128)(2,1)}, bf16[2,192,768]{2,1,0:T(8,128)(2,1)}, u32[]{:S(2)}, u32[]{:S(2)}) collective-permute-start(bf16[2,192,768]{2,1,0:T(8,128)(2,1)} %get-tuple-element.564), channel_id=1, source_target_pairs={{0,1},{1,0},{2,3},{3,2},{4,5},{5,4},{6,7},{7,6},{8,9},{9,8},{10,11... | collective-permute-start | bytes 1769480 | tf_op jit(solution)/shard_map/ppermute | solution.py:70
  725.1 10.1 %collective-permute-start.55 = (bf16[4,2,48,768]{3,2,1,0:T(8,128)(2,1)}, bf16[4,2,48,768]{3,2,1,0:T(8,128)(2,1)}, u32[]{:S(2)}, u32[]{:S(2)}) collective-permute-start(bf16[4,2,48,768]{3,2,1,0:T(8,128)(2,1)} %get-tuple-element.465), channel_id=1, source_target_pairs={{1,5},{3,7},{5,1},{7,3},{9,13},{11,15},{13,9},{15,11},{17,21},{19,... | collective-permute-start | bytes 1769480 | tf_op jit(solution)/shard_map/ppermute | solution.py:66
  737.1 29.3 %collective-permute-start.57 = (bf16[4,4,48,768]{3,2,1,0:T(8,128)(2,1)S(1)}, bf16[4,4,48,768]{3,2,1,0:T(8,128)(2,1)}, u32[]{:S(2)}, u32[]{:S(2)}) collective-permute-start(bf16[4,4,48,768]{3,2,1,0:T(8,128)(2,1)S(1)} %bitcast.437), channel_id=1, source_target_pairs={{1,0},{3,2},{5,4},{7,6},{9,8},{11,10},{13,12},{15,14},{17,16},{19,... | collective-permute-start | bytes 3538952 | tf_op jit(solution)/shard_map/ppermute | solution.py:78
  752.1 15.3 %collective-permute-start.63 = (bf16[4,2,48,768]{3,2,1,0:T(8,128)(2,1)}, bf16[4,2,48,768]{3,2,1,0:T(8,128)(2,1)S(1)}, u32[]{:S(2)}, u32[]{:S(2)}) collective-permute-start(bf16[4,2,48,768]{3,2,1,0:T(8,128)(2,1)} %get-tuple-element.474), channel_id=1, source_target_pairs={{0,4},{1,5},{2,6},{3,7},{4,0},{5,1},{6,2},{7,3},{8,12},{9,13},{10,... | collective-permute-start | bytes 1769480 | tf_op jit(solution)/shard_map/ppermute | solution.py:66
  754.3 12.1 %collective-permute-start.48 = (f32[1,128]{1,0:T(1,128)S(1)}, f32[1,128]{1,0:T(1,128)S(1)}, u32[]{:S(2)}, u32[]{:S(2)}) collective-permute-start(f32[1,128]{1,0:T(1,128)S(1)} %fusion.96), channel_id=1, source_target_pairs={{0,1},{1,0},{2,3},{3,2},{4,5},{5,4},{6,7},{7,6},{8,9},{9,8},{10,11... | collective-permute-start | bytes 1544 | tf_op jit(solution)/shard_map/ppermute | solution.py:70
  768.3 3.5 collective-permute-start.59
  769.3 28.0 %collective-permute-start.64 = (bf16[4,4,48,768]{3,2,1,0:T(8,128)(2,1)S(1)}, bf16[4,4,48,768]{3,2,1,0:T(8,128)(2,1)}, u32[]{:S(2)}, u32[]{:S(2)}) collective-permute-start(bf16[4,4,48,768]{3,2,1,0:T(8,128)(2,1)S(1)} %bitcast.428), channel_id=1, source_target_pairs={{0,1},{1,0},{2,3},{3,2},{4,5},{5,4},{6,7},{7,6},{8,9},{9,8},{10,11... | collective-permute-start | bytes 3538952 | tf_op jit(solution)/shard_map/ppermute | solution.py:70
  775.4 4.4 collective-permute-start.61
  (110 other events, 1334.1 us)
Sparse Core Ops, SparseCore 0:
  12.4 140.6 all-gather.6
  221.4 43.5 all-gather.8
  463.8 106.3 all-gather.10

commit v3 on v2

--- a/solution.py
+++ b/solution.py
@@ -83,7 +83,18 @@
 
 
 def link_cost(bit, value):
-    return 4 + value.size * (6e-6 if bit == 0 else 5.5e-5 if bit < 3 else 1.1e-4)
+    return 4 + value.size * (6e-6 if bit == 0 else 6.5e-5 if bit < 3 else 1.1e-4)
+
+
+def zero_after(value):
+    mark = value[(0,) * value.ndim]
+    return jnp.where(mark != mark, 1.0, 0.0)
+
+
+def tied(value, *others):
+    for other in others:
+        value = value + zero_after(other).astype(value.dtype)
+    return value
 
 
 def interleave(tasks, after):
@@ -92,11 +103,18 @@
 
     def advance(index, arrived):
         nonlocal last, now, count
-        try:
-            link, cost, move, value = tasks[index].send(arrived)
-        except StopIteration as stop:
-            results[index] = stop.value
-            return
+        posted = True
+        while posted:
+            try:
+                link, cost, move, value = tasks[index].send(arrived)
+            except StopIteration as stop:
+                results[index] = stop.value
+                return
+            posted = cost < 0
+            if posted:
+                value, last = lax.optimization_barrier((value, last))
+                free[link] = max(now, free.get(link, 0.0)) - cost
+                arrived = move(value)
         count += 1
         if move is None:
             heapq.heappush(pending, (now + cost, count, index, None))
@@ -116,7 +134,7 @@
         ended, unused, index, arrived = heapq.heappop(pending)
         now = max(now, ended)
         if arrived is not None:
-            now += 1.0 + 4e-6 * arrived.size
+            now += 2.0 + 6e-6 * min(arrived.size, D * D)
             arrived, last = lax.optimization_barrier((arrived, last))
             last = arrived
         advance(index, arrived)
@@ -159,8 +177,6 @@
 
 
 def summed(values):
-    arrived = yield ("dp", 5, swap_half, values)
-    values = values + arrived
     for bit in range(bit_count()):
         arrived = yield (bit, 5, over(bit), values)
         values = values + arrived
@@ -291,10 +307,8 @@
     in_ref,
     out_ref,
     grad_ref,
-    in_sent_ref,
-    in_kept_ref,
-    out_sent_ref,
-    out_kept_ref,
+    sent_ref,
+    kept_ref,
     gains_ref,
     resid_ref,
     low_ref,
@@ -323,13 +337,13 @@
 
     @pl.when(step < 2)
     def send():
-        in_sent_ref[...] = in_grad
-        out_sent_ref[...] = out_grad
+        sent_ref[0] = in_grad
+        sent_ref[1] = out_grad
 
     @pl.when(step >= 2)
     def keep():
-        in_kept_ref[...] = in_grad
-        out_kept_ref[...] = out_grad
+        kept_ref[0] = in_grad
+        kept_ref[1] = out_grad
 
     @pl.when(step == pl.num_programs(0) - 1)
     def finish():
@@ -347,9 +361,7 @@
 
     fixed = pl.BlockSpec((count, D), lambda j, mine: (0, 0))
     row = pl.BlockSpec((1, D), lambda j, mine: (0, 0))
-    sent = pl.BlockSpec((chunk, D), lambda j, mine: (jnp.minimum(j, 1), 0))
-    kept = pl.BlockSpec((chunk, D), lambda j, mine: (jnp.maximum(j - 2, 0), 0))
-    half = jax.ShapeDtypeStruct((hidden // 2, D), LOW)
+    half = jax.ShapeDtypeStruct((2, hidden // 2, D), LOW)
     return pl.pallas_call(
         functools.partial(feed_backward_kernel, last_scale),
         grid_spec=pltpu.PrefetchScalarGridSpec(
@@ -365,7 +377,12 @@
                 pl.BlockSpec((1, chunk, D), lambda j, mine: (1, place(j, mine), 0)),
                 pl.BlockSpec((1, chunk, D), lambda j, mine: (2, place(j, mine), 0)),
             ],
-            out_specs=[fixed, sent, kept, sent, kept, pl.BlockSpec((2, D), lambda j, mine: (0, 0))],
+            out_specs=[
+                fixed,
+                pl.BlockSpec((2, chunk, D), lambda j, mine: (0, jnp.minimum(j, 1), 0)),
+                pl.BlockSpec((2, chunk, D), lambda j, mine: (0, jnp.maximum(j - 2, 0), 0)),
+                pl.BlockSpec((2, D), lambda j, mine: (0, 0)),
+            ],
             scratch_shapes=[
                 pltpu.VMEM((count, D), FULL),
                 pltpu.VMEM((count, D), LOW),
@@ -373,9 +390,12 @@
                 pltpu.VMEM((count, D), FULL),
             ],
         ),
-        out_shape=[jax.ShapeDtypeStruct((count, D), FULL)]
-        + [half] * 4
-        + [jax.ShapeDtypeStruct((2, D), FULL)],
+        out_shape=[
+            jax.ShapeDtypeStruct((count, D), FULL),
+            half,
+            half,
+            jax.ShapeDtypeStruct((2, D), FULL),
+        ],
         compiler_params=params(),
         name="feed_backward",
     )(section_bit(0)[None], upstream, after, last_gain[None], rows, gain_row[None], before, weights, weights)
@@ -403,6 +423,18 @@
             yield slice(sequence * length, (sequence + 1) * length), slice(
                 pair * 2 * DK, (pair + 1) * 2 * DK
             ), pair
+
+
+def both_heads(rows):
+    left = lax.broadcasted_iota(jnp.int32, rows.shape, 1) < DK
+    none = jnp.zeros_like(rows)
+    return jnp.concatenate([jnp.where(left, rows, none), jnp.where(left, none, rows)])
+
+
+def one_pair(rows):
+    length = rows.shape[0] // 2
+    left = lax.broadcasted_iota(jnp.int32, (length, rows.shape[1]), 1) < DK
+    return jnp.where(left, rows[:length], rows[length:])
 
 
 def probabilities(queries, keys_in, bias):
@@ -428,17 +460,12 @@
     key_ref[...] = mul(source, matrix(1)).astype(LOW)
     value_ref[...] = mul(source, matrix(2)).astype(LOW)
     length = rows.shape[0] // MICRO
-    left = lax.broadcasted_iota(jnp.int32, (length, 2 * DK), 1) < DK
     for rows_at, columns, pair in head_pairs(length):
-        queries = query_ref[rows_at, columns]
-        keys_in, values_in = key_ref[rows_at, columns], value_ref[rows_at, columns]
-        mixed = []
-        for side in range(2):
-            picked = jnp.where(left == (side == 0), queries, jnp.zeros_like(queries))
-            bias = bias_ref[2 * pair + side] if biased else None
-            probs = probabilities(picked, keys_in, bias)
-            mixed.append(mul(probs.astype(LOW), values_in))
-        mixed_ref[rows_at, columns] = jnp.where(left, mixed[0], mixed[1]).astype(LOW)
+        queries = both_heads(query_ref[rows_at, columns])
+        bias = bias_ref[2 * pair : 2 * pair + 2].reshape(2 * length, length) if biased else None
+        probs = probabilities(queries, key_ref[rows_at, columns], bias)
+        mixed = mul(probs.astype(LOW), value_ref[rows_at, columns])
+        mixed_ref[rows_at, columns] = one_pair(mixed).astype(LOW)
     after_ref[...] = rows + mul(mixed_ref[...], matrix(3))
 
 
@@ -486,39 +513,24 @@
     grad_mixed_ref[...] = mul_right(grad_out, matrix(3)).astype(LOW)
     put(3, mul_left(mixed_ref[...], grad_out).astype(LOW))
     length = grad.shape[0] // MICRO
-    left = lax.broadcasted_iota(jnp.int32, (length, 2 * DK), 1) < DK
+    scale = DK ** (-0.5)
     for rows_at, columns, pair in head_pairs(length):
-        queries, keys_in = query_ref[rows_at, columns], key_ref[rows_at, columns]
-        values_in, grad_mixed = value_ref[rows_at, columns], grad_mixed_ref[rows_at, columns]
-        parts = []
-        for side in range(2):
-            half = left == (side == 0)
-            bias = bias_ref[2 * pair + side] if biased else None
-            probs = probabilities(jnp.where(half, queries, jnp.zeros_like(queries)), keys_in, bias)
-            picked = jnp.where(half, grad_mixed, jnp.zeros_like(grad_mixed))
-            grad_probs = mul_right(picked, values_in)
-            grad_scores = probs * (grad_probs - jnp.sum(probs * grad_probs, -1, keepdims=True))
-            grad_scores = grad_scores.astype(LOW)
-            if biased:
-                if rows_at.start == 0:
-                    extra_ref[2 * pair + side] = grad_scores.astype(FULL)
-                else:
-                    extra_ref[2 * pair + side] += grad_scores.astype(FULL)
-            parts.append(
-                (
-                    mul(grad_scores, keys_in),
-                    mul_left(grad_scores, queries),
-                    mul_left(probs.astype(LOW), grad_mixed),
-                )
-            )
-        scale = DK ** (-0.5)
-        grad_query_ref[rows_at, columns] = (
-            jnp.where(left, parts[0][0], parts[1][0]) * scale
-        ).astype(LOW)
-        grad_key_ref[rows_at, columns] = (
-            jnp.where(left, parts[0][1], parts[1][1]) * scale
-        ).astype(LOW)
-        grad_value_ref[rows_at, columns] = jnp.where(left, parts[0][2], parts[1][2]).astype(LOW)
+        queries, keys_in = both_heads(query_ref[rows_at, columns]), key_ref[rows_at, columns]
+        grad_mixed = both_heads(grad_mixed_ref[rows_at, columns])
+        bias = bias_ref[2 * pair : 2 * pair + 2].reshape(2 * length, length) if biased else None
+        probs = probabilities(queries, keys_in, bias)
+        grad_probs = mul_right(grad_mixed, value_ref[rows_at, columns])
+        grad_scores = probs * (grad_probs - jnp.sum(probs * grad_probs, -1, keepdims=True))
+        grad_scores = grad_scores.astype(LOW)
+        if biased:
+            score_rows = grad_scores.astype(FULL).reshape(2, length, length)
+            if rows_at.start == 0:
+                extra_ref[2 * pair : 2 * pair + 2] = score_rows
+            else:
+                extra_ref[2 * pair : 2 * pair + 2] += score_rows
+        grad_query_ref[rows_at, columns] = (one_pair(mul(grad_scores, keys_in)) * scale).astype(LOW)
+        grad_key_ref[rows_at, columns] = (mul_left(grad_scores, queries) * scale).astype(LOW)
+        grad_value_ref[rows_at, columns] = mul_left(probs.astype(LOW), grad_mixed).astype(LOW)
     normed = norm_ref[...]
     source = source_ref[...] if crossed else normed
     put(0, mul_left(normed, grad_query_ref[...]).astype(LOW))
@@ -578,14 +590,13 @@
     )
 
 
+def low_bit_order():
+    return sorted(range(lax.axis_size("section")), key=lambda section: (section & 1, section))
+
+
 def slot_places():
     order = low_bit_order()
     return [order.index(section) for section in range(len(order))]
-
-
-def low_bit_order():
-    sections = lax.axis_size("section")
-    return sorted(range(sections), key=lambda p: (p & 1, (p >> 1) & 1, p >> 2))
 
 
 def slot_layout():
@@ -705,8 +716,8 @@
         weight_shard, "section", axis=1, tiled=True, axis_index_groups=[low_bit_order()]
     )
     def natural(slot):
-        split = slot.reshape(2, 2, sections // 4, MATRICES, -1, D)
-        return jnp.transpose(split, (3, 2, 1, 0, 4, 5)).reshape(MATRICES, D, D)
+        split = slot.reshape(2, sections // 2, MATRICES, -1, D)
+        return jnp.transpose(split, (2, 1, 0, 3, 4)).reshape(MATRICES, D, D)
 
     if attention.shape[1] % 16 == 0:
         self_weights, cross_weights = (0, weights), (3, weights)
@@ -732,16 +743,31 @@
     root_rows = jnp.stack([left_roots, right_inverse_roots])
     own_roots = lax.dynamic_slice_in_dim(root_rows, half * MATRICES, MATRICES, 1)
     root_rows = jnp.stack([own_roots, root_rows[:, 8:12]]).reshape(4, 2, 2, -1, D)
-    root_rows, unused = lax.optimization_barrier((root_rows, resid))
     root_part = swap_bit(pick(root_rows, 1 - first, 1), 0)
+    root_rows, resid, root_part = lax.optimization_barrier((root_rows, resid, root_part))
+    root_rows = ordered(pick(root_rows, first, 1), root_part, first, 2)
+    root_part = swap_bit(pick(root_rows, 1 - second, 1), 1)
 
     after_enc, encoded, before_enc = lax.cond(
         is_encoder, encoder_rest, lambda: jax.tree.map(jnp.zeros_like, encoder_rest())
     )
     encoded, root_part = lax.optimization_barrier((encoded, root_part))
     arrived = to_decoder(encoded)
-    root_rows = ordered(pick(root_rows, first, 1), root_part, first, 2)
-    root_part = swap_bit(pick(root_rows, 1 - second, 1), 1)
+    root_rows = ordered(pick(root_rows, second, 1), root_part, second, 1)
+    root_rows = root_rows.reshape(2, 2, -1, D)
+    root_lefts, root_rights = root_rows[:, 0], root_rows[:, 1]
+    root_steps = list(range(bits - 1, 1, -1))
+
+    def root_step(stage):
+        return swap_bit(root_rights, root_steps[stage])
+
+    def grown(stage, part):
+        mine = section_bit(root_steps[stage])
+        return ordered(root_rights, part, mine, 1 + stage)
+
+    for stage in range(len(root_steps) - 2):
+        root_rights = grown(stage, root_step(stage))
+    root_part = root_step(len(root_steps) - 2)
 
     def decoder_rest(after, before):
         rows_feed, kept_cross = attention_forward(
@@ -761,9 +787,7 @@
     )
 
     final_low, root_part = lax.optimization_barrier((final_low, root_part))
-    root_rows = ordered(pick(root_rows, second, 1), root_part, second, 1)
-    root_rows = root_rows.reshape(2, 2, -1, D)
-    root_lefts, root_rights = root_rows[:, 0], root_rows[:, 1]
+    root_rights = grown(len(root_steps) - 2, root_part)
 
     final_split = final_low.reshape(MICRO, length, D)
     handed = to_encoder(final_split[0])
@@ -813,18 +837,8 @@
         gains = jnp.concatenate([gain_cross, gains])
         return (grad_source, grad_rows, feed_grads, cross_grads, gains)
 
-    root_steps = list(range(bits - 1, 1, -1))
-
-    def root_step(stage):
-        return swap_bit(root_rights, root_steps[stage])
-
-    def grown(stage, part):
-        mine = section_bit(root_steps[stage])
-        return ordered(root_rights, part, mine, 1 + stage)
-
-    for stage in range(len(root_steps) - 2):
-        root_rights = grown(stage, root_step(stage))
-    root_part = root_step(len(root_steps) - 2)
+    root_rights, grad_final = lax.optimization_barrier((root_rights, grad_final))
+    root_part = root_step(len(root_steps) - 1)
     grad_source, grad_dec, feed_dec, cross_grads, gains_dec = lax.cond(
         is_decoder, decoder_back, lambda: jax.tree.map(jnp.zeros_like, decoder_back())
     )
@@ -833,12 +847,14 @@
     back_source, feed_dec, cross_grads, root_part = lax.optimization_barrier(
         (back_source, feed_dec, cross_grads, root_part)
     )
-    root_rights = grown(len(root_steps) - 2, root_part)
-    root_part = root_step(len(root_steps) - 1)
-
-    late = to_low(to_full(feed_dec[1]) + to_full(swap_bit(feed_dec[0], 0, (1,))))
+    root_rights = grown(len(root_steps) - 1, root_part).reshape(2, D, D)
+
+    late = to_low(to_full(cross_grads[1]) + to_full(swap_bit(cross_grads[0], 0, (1,))))
     late_split = late.reshape(2, -1, D)
-    late_arrived = swap_bit(pick(late_split, 1 - second, 0), 1, (1,))
+    late_part, back_source, grad_dec = lax.optimization_barrier(
+        (pick(late_split, 1 - second, 0), back_source, grad_dec)
+    )
+    late_arrived = swap_bit(late_part, 1, (1,))
 
     def self_back(grad_rows):
         return attention_backward(
@@ -856,19 +872,30 @@
             weights,
             1.0,
         )
-        return (grad_rows, gains, jnp.zeros(bias_term.shape, jnp.float32), feed_grads)
+        empty = jnp.zeros((MATRICES // 2 * D, D), jnp.bfloat16)
+        score = jnp.zeros(bias_term.shape, jnp.float32)
+        return (grad_rows, gains, score, [empty, empty], feed_grads)
 
     def decoder_self():
         embed_low, *self_grads, gain_grad, score_grad = self_back(grad_dec)
         gains = jnp.concatenate([gain_grad, gain_grad])
-        return (to_full(embed_low), gains, score_grad, self_grads + cross_grads)
-
-    grad_rows, gains_middle, score_middle, grads_middle = lax.cond(
+        return (to_full(embed_low), gains, score_grad, self_grads, feed_dec)
+
+    grad_rows, gains_middle, score_middle, self_middle, feed_grads = lax.cond(
         is_encoder, encoder_feed, decoder_self
     )
-    grad_rows, grads_middle = lax.optimization_barrier((grad_rows, grads_middle))
-    sent_first = swap_bit(grads_middle[0], 0)
-    sent_second = swap_bit(grads_middle[2], 0)
+    grad_rows, self_middle, feed_grads, late_arrived = lax.optimization_barrier(
+        (grad_rows, self_middle, feed_grads, late_arrived)
+    )
+    late = to_low(to_full(pick(late_split, second, 0)) + to_full(late_arrived))
+    third = section_bit(2)
+    late_split = late.reshape(2 ** (bits - 3), 2, -1, D)
+    late_part, grad_rows = lax.optimization_barrier(
+        (pick(late_split, 1 - third, 1).reshape(-1, D), grad_rows)
+    )
+    late_arrived = swap_bit(late_part, 2, (1,))
+
+    feed_arrived = swap_bit(feed_grads[0], 0)
 
     def encoder_self():
         embed_low, *self_grads, gain_grad, score_grad = self_back(grad_rows)
@@ -877,19 +904,17 @@
 
     def decoder_skip_self():
         gains = jnp.concatenate([jnp.zeros((3, D), jnp.float32), gains_middle[:1], gains_dec])
-        return (to_low(grad_rows), gains, score_middle, feed_dec[2:])
-
-    embed_low, gain_part, score_grad, third_grads = lax.cond(
+        return (to_low(grad_rows), gains, score_middle, self_middle)
+
+    embed_low, gain_part, score_grad, self_grads = lax.cond(
         is_encoder, encoder_self, decoder_skip_self
     )
-    embed_low, third_grads, sent_first, sent_second, late_arrived, root_part = (
-        lax.optimization_barrier(
-            (embed_low, third_grads, sent_first, sent_second, late_arrived, root_part)
-        )
-    )
-    late = to_low(to_full(pick(late_split, second, 0)) + to_full(late_arrived))
-    root_rights = grown(len(root_steps) - 1, root_part).reshape(2, D, D)
-    bias_grad = jnp.einsum("hqk,qkb->bh", score_grad, onehot.astype(jnp.float32), precision=HIGH)
+    embed_low, self_grads, late_arrived, feed_arrived = lax.optimization_barrier(
+        (embed_low, self_grads, late_arrived, feed_arrived)
+    )
+    feed_half = to_low(to_full(feed_grads[1]) + to_full(feed_arrived))
+    late = pick(late_split, third, 1).reshape(-1, D)
+    late = to_low(to_full(late) + to_full(late_arrived))
 
     found = {}
     own_local = (own_ids.reshape(-1) - section_index * vocab_rows)[None, :]
@@ -901,126 +926,142 @@
         every_rows = yield ("gather", 80, lambda rows: lax.all_gather(rows, "section"), embed_low)
         found["rows"] = every_rows.reshape(-1, D)
 
-    cuts = [vocab_rows * part // 64 * 16 for part in range(4)] + [vocab_rows]
-
-    def table_task(part):
-        start, stop = cuts[part], cuts[part + 1]
+    def feed_task():
+        yield (None, 10, None, None)
+        layout = ["matrix"] + list(range(bits - 1, 0, -1))
+        own = yield from halved(feed_half.reshape(-1, D), layout, range(1, bits))
+        own = own.reshape(2, -1, D)
+        found["feed_square"] = squares(own)
+        found["feed"] = own
+        return own, (yield ("dp", -15, swap_half, own))
+
+    block_rows = -(-vocab_rows // 16) * 8
+    shared = 2 * block_rows - vocab_rows
+    starts = [0, vocab_rows - block_rows]
+
+    def table_task():
         yield from until(found, ["rows"])
-
-        def product(rows):
-            hit = own_local == jnp.arange(start, stop)[:, None]
-            return to_low(mul(hit.astype(jnp.bfloat16), rows) + head_table[start:stop])
-
-        own = yield ("core", 6, product, found["rows"])
-        other = yield ("dp", 19, swap_half, own)
-        both = to_full(own) + to_full(other)
-        found["table", part] = squares(both)
-        return both
-
-    def first_task():
-        rows = to_low(to_full(grads_middle[1]) + to_full(sent_first))
-        found["first"] = yield from halved(rows, slot_layout(), range(1, bits))
-
-    def second_task():
-        yield (None, 4, None, None)
-        rows = to_low(to_full(grads_middle[3]) + to_full(sent_second))
-        block = yield from halved(rows, slot_layout(), range(1, bits))
-        found["second"] = block
+        own_start, other_start = jnp.where(is_encoder, jnp.array(starts), jnp.array(starts[::-1]))
+
+        def product(start):
+            def rows_of(rows):
+                hit = own_local == start + jnp.arange(block_rows)[:, None]
+                head = lax.dynamic_slice_in_dim(head_table, start, block_rows, 0)
+                return to_low(mul(hit.astype(jnp.bfloat16), rows) + head)
+
+            return rows_of
+
+        sent = yield ("core", 10, product(other_start), found["rows"])
+        found["table_sent"] = sent
+        arrived = yield ("dp", -36, swap_half, sent)
+        own = yield ("core", 10, product(own_start), found["rows"])
+        yield (None, 30, None, None)
+        own = to_low(to_full(own) + to_full(arrived))
+        counted = is_encoder | (jnp.arange(block_rows) >= shared)
+        found["table_square"] = squares(jnp.where(counted[:, None], own, jnp.zeros_like(own)))
+        other = yield ("dp", -36, swap_half, own)
+        return jnp.concatenate(
+            [jnp.where(is_encoder, own, other), jnp.where(is_encoder, other, own)[shared:]]
+        )
+
+    def cross_task():
+        layout = [bit for bit in slot_layout()[1:] if bit > 2]
+        block = yield from halved(late, layout, range(3, bits), (1,))
         found["cross_square"] = squares(block)
         full = yield from doubled(block, (1,))
         terms = shampoo_terms(block, full, root_lefts[1], root_rights[1])
         found["cross_direction"] = squares(terms[1])
         terms = yield from to_rows(terms, (1,))
-        other = yield ("dp", 30, to_encoder, terms)
-        return jnp.where(is_encoder, other, terms)
-
-    def third_task():
-        found["third"] = yield from halved(tuple(third_grads), slot_layout(), range(1, bits))
-
-    def late_task():
-        found["late"] = yield from halved(late, slot_layout()[1:], range(2, bits), (1,))
+        yield from until(found, ["feed"])
+        other = yield ("dp", -30, to_encoder, tied(terms, found["feed"]))
+        return terms, other
 
     def self_task():
-        yield from until(found, ["first", "third"])
-        block = jnp.where(is_encoder, found["third"], found["first"])
+        block = yield from halved(tuple(self_grads), slot_layout(), range(1, bits))
         found["self_square"] = squares(block)
-        full = yield from doubled(block)
+        yield from until(found, ["table_sent"])
+        full = yield from doubled(tied(block, found["table_sent"]))
         terms = shampoo_terms(block, full, root_lefts[0], root_rights[0])
         found["self_direction"] = squares(terms[1])
         terms = yield from to_rows(terms)
-        other = yield ("dp", 30, swap_half, terms)
-        return ordered(terms, other, half, 1).reshape(4, 2 * MATRICES, -1, D)
-
-    def feed_task():
-        yield from until(found, ["first", "second", "third", "late"])
-        own = jnp.where(
-            is_encoder,
-            jnp.stack([found["first"], found["second"]]),
-            jnp.stack([found["late"], found["third"]]),
+        yield from until(found, ["feed"])
+        other = yield ("dp", -30, swap_half, tied(terms, found["feed"]))
+        return terms, other
+
+    def small_task():
+        yield (None, 25, None, None)
+
+        def of_buckets(values):
+            return jnp.einsum(
+                "hqk,qkb->bh", values, onehot.astype(jnp.float32), precision=HIGH
+            ).reshape(1, -1)
+
+        bias_grad = yield ("core", 6, of_buckets, score_grad)
+        rows = [jnp.where(half == layer, bias_grad, 0.0) for layer in range(2)]
+        rows = jnp.concatenate(rows, 1).reshape(-1, D)
+        found["small"] = yield from summed(jnp.concatenate([gain_part, rows]))
+
+    def norm_task():
+        yield from until(
+            found, ["self_square", "cross_square", "small", "feed_square", "table_square"]
         )
-        found["feed_square"] = squares(own)
-        other = yield ("dp", 15, swap_half, own)
-        return to_full(ordered(own, other, half, 1))
-
-    def small_task():
-        small = jnp.concatenate(
-            [gain_part.reshape(-1), jnp.where(half == 0, bias_grad, 0.0).reshape(-1)]
-            + [jnp.where(half == 1, bias_grad, 0.0).reshape(-1)]
-        )
-        small = yield from summed(small.reshape(-1, 128))
-        return small.reshape(-1)
-
-    def norm_task():
-        tables = [("table", part) for part in range(4)]
-        yield from until(
-            found,
-            tables + ["self_square", "cross_square", "feed_square"]
-            + ["self_direction", "cross_direction"],
-        )
-        cross_live = is_decoder.astype(jnp.float32)
-        square_sum = (
-            0.5 * sum(found[name] for name in tables)
-            + found["self_square"]
-            + found["feed_square"]
-            + cross_live * found["cross_square"]
-        )
+        square_sum = found["self_square"] + is_decoder.astype(jnp.float32) * found["cross_square"]
+        square_sum = square_sum + found["feed_square"] + found["table_square"]
+        sums = jnp.stack([loss_part, count_part, square_sum])
+        sums = yield from summed(jnp.pad(sums, (0, D - sums.shape[0])).reshape(1, D))
+        sums = jnp.concatenate([found["small"], sums])
+        return sums, (yield ("dp", -5, swap_half, sums))
+
+    def direction_task():
+        yield from until(found, ["self_direction", "cross_direction"])
         matrix = 2 * section_bit(0) + section_bit(1)
         names = jnp.arange(3 * MATRICES)
         own_matrix, cross_matrix = half * MATRICES + matrix, 2 * MATRICES + matrix
-        directions = jnp.where(names == own_matrix, found["self_direction"], 0.0)
-        directions = directions + jnp.where(
-            names == cross_matrix, cross_live * found["cross_direction"], 0.0
+        sums = jnp.where(names == own_matrix, found["self_direction"], 0.0)
+        sums = sums + jnp.where(
+            names == cross_matrix, is_decoder * found["cross_direction"], 0.0
         )
-        sums = jnp.concatenate([jnp.stack([loss_part, count_part, square_sum]), directions])
         sums = yield from summed(jnp.pad(sums, (0, 128 - sums.shape[0])).reshape(1, 128))
-        return sums[0, : 3 + 3 * MATRICES]
-
-    tasks = [rows_task(), first_task(), third_task(), second_task(), late_task(), self_task()]
-    tasks += [feed_task(), small_task(), norm_task()] + [table_task(part) for part in range(4)]
+        return sums, (yield ("dp", -5, swap_half, sums))
+
+    tasks = [rows_task(), self_task(), cross_task(), table_task(), feed_task()]
+    tasks += [small_task(), norm_task(), direction_task()]
     results = interleave(tasks, embed_low)
-    cross_terms, self_terms = results[3], results[5]
-    feed_both, small, sums = results[6:9]
-    table_grad = jnp.concatenate(results[9:])
-    attention_grad, direction, left_term, right_term = to_full(
-        jnp.concatenate([self_terms, cross_terms], 1)
-    )
-    inner_part = jnp.swapaxes(feed_both[0], 1, 2)
-    outer_part = feed_both[1]
-    gain_full = small[: gain_rows.size].reshape(gain_rows.shape)
-    bias_full = small[gain_rows.size :].reshape(position_bias.shape)
+    self_terms, cross_terms, table_grad, feed_both = results[1:5]
+    norm_sums, directions = results[6:]
+    norm_sums = norm_sums[0] + norm_sums[1]
+    small, sums = norm_sums[:-1], norm_sums[-1]
+    directions = (directions[0] + directions[1])[0, : 3 * MATRICES]
+    table_grad = to_full(table_grad)
+    gain_full = small[: gain_rows.shape[0]]
+    bias_full = small[gain_rows.shape[0] :].reshape(position_bias.shape)
     small_square = squares(gain_full) + squares(bias_full)
 
     grad_norm = jnp.sqrt(sums[2] + small_square)
     clip_factor = CLIP / jnp.maximum(grad_norm, CLIP)
     table_out = adamw(table, table_first, table_second, table_grad * clip_factor, RATE_TABLE)
+    feed_both = to_full(ordered(*feed_both, half, 1))
+    inner_part = jnp.swapaxes(feed_both[0], 1, 2)
+    outer_part = feed_both[1]
     inner_out = adamw(inner_weight, inner_first, inner_second, inner_part * clip_factor, RATE_INNER)
     outer_out = adamw(outer_weight, outer_first, outer_second, outer_part * clip_factor, RATE_INNER)
+    table_out, self_terms, cross_terms = lax.optimization_barrier(
+        (table_out, self_terms, cross_terms)
+    )
+    terms = jnp.concatenate(
+        [
+            ordered(*self_terms, half, 1).reshape(4, 2 * MATRICES, -1, D),
+            jnp.where(is_encoder, cross_terms[1], cross_terms[0]),
+        ],
+        1,
+    )
+    attention_grad, direction, left_term, right_term = to_full(terms)
     gain_out = adamw(gain_rows, gain_first, gain_second, gain_full * clip_factor, RATE_GAIN)
     bias_out = adamw(position_bias, bias_first, bias_second, bias_full * clip_factor, RATE_BIAS)
     clip_square = clip_factor * clip_factor
     left_new = BETA_STATS * left_stats + (1 - BETA_STATS) * clip_square * left_term
     right_new = BETA_STATS * right_stats + (1 - BETA_STATS) * clip_square * right_term
-    spread = jnp.sqrt(sums[3:] / (D * D) + EPS)[:, None, None]
+    spread = jnp.sqrt(directions / (D * D) + EPS)[:, None, None]
     attention_new = attention - RATE_ATTENTION * (direction / spread + DECAY * attention)
     return (
         sums[0],

time: 857 us -> 819 us (0.956)
  waiting for transfers between devices: 383 us -> 357 us
  Pallas kernels: 55 us -> 43.8 us
  other arithmetic: 124 us -> 114 us
    ppermute x9 -> x7, waiting for transfers between devices: 56.7 us -> 24.9 us  [swap_half(): return lax.ppermute(value, 'dp', [(0, 1), (1, 0)])]
    ppermute x51, waiting for transfers between devices: 215 us -> 237 us  [swap_bit(): return lax.ppermute(value, ('section', 'dp'), pairs)]
    ppermute x3, waiting for transfers between devices: 50.6 us -> 37.8 us  [to_encoder(): return lax.ppermute(value, 'dp', [(1, 0)])]
    ppermute x51, starting transfers between devices: 43.8 us -> 55.9 us  [swap_bit(): return lax.ppermute(value, ('section', 'dp'), pairs)]
    add x8, other arithmetic: 12.2 us -> 3.25 us  [the longest x2 1.3 us: rows_of(): hit = own_local == start + jnp.arange(block_rows)[:, None]]
    ppermute x9 -> x7, starting transfers between devices: 41.2 us -> 32.9 us  [swap_half(): return lax.ppermute(value, 'dp', [(0, 1), (1, 0)])]
    unnamed x221 -> x147, local copies, waits for them, and re-layouts: 17.8 us -> 14 us
    another operation x17 -> x18, local copies, waits for them, and re-layouts: 16.1 us -> 18.6 us
  transfers between devices with their start and end apart: 68 -> 66, of which waited for: 42 -> 33; matrix products, arithmetic and copies ran while one was open for 21% -> 25% of each run, Pallas kernels for 5% -> 5%
where the time goes in v3:
time: 819 us; the launch traced here: 810 us
  waiting for transfers between devices  357 us (44%)
  other arithmetic  114 us (14%)
  starting transfers between devices  99.7 us (12%)
  matrix products  77.5 us (9%)
  local copies, waits for them, and re-layouts  65.3 us (8%)
  Pallas kernels  43.8 us (5%)
  between operations  30.6 us (4%)
  blocking collectives  20.1 us (2%)
    ppermute x51, waiting for transfers between devices, swap_bit(): return lax.ppermute(value, ('section', 'dp'), pairs)  237 us
    ppermute x51, starting transfers between devices, swap_bit(): return lax.ppermute(value, ('section', 'dp'), pairs)  55.9 us
    all_gather x1, waiting for transfers between devices, local(): all_rows = lax.all_gather(head_low, 'section', axis=0, tiled=True)  42.8 us
    ppermute x3, waiting for transfers between devices, to_encoder(): return lax.ppermute(value, 'dp', [(1, 0)])  37.8 us
    convert_element_type x21, other arithmetic, to_low(): return values.astype(jnp.bfloat16)  32.9 us
    ppermute x7, starting transfers between devices, swap_half(): return lax.ppermute(value, 'dp', [(0, 1), (1, 0)])  32.9 us
    dot_general x5, matrix products, forward_mul(): return jnp.dot(left, right, preferred_element_type=jnp.float32)  32.7 us
    ppermute x7, waiting for transfers between devices, swap_half(): return lax.ppermute(value, 'dp', [(0, 1), (1, 0)])  24.9 us
  transfers between devices with their start and end apart: 66, of which 33 were waited for; matrix products, arithmetic and copies ran while one was open for 25% of the time, Pallas kernels for 5%

profile of v3, /device:TPU:0, one launch (start us, length us, event | category | flops | bytes accessed | tf_op | source)
XLA Modules:
  0.0 809.9 jit_solution(15652391197305233003)
XLA Ops:
  13.0 3.0 collective-permute-start
  26.6 3.1 collective-permute-start.4
  29.7 3.1 convert_element_type.429
  33.1 8.7 %fusion.14 = bf16[2048,768]{1,0:T(8,128)(2,1)} fusion(bf16[2008,768]{1,0:T(8,128)(2,1)S(1)} %convert_element_type.429, s32[2048]{0:T(1024)S(1)} %bitcast.461), kind=kOutput, calls=%fused_computation.33 | convolution fusion | flops 6322307072 | bytes 6238208 | tf_op jit(solution)/shard_map/dot_general | solution.py:192
  44.1 3.7 collective-permute-done.5
  47.8 10.2 %fusion.20 = bf16[2048,768]{1,0:T(8,128)(2,1)S(1)} fusion(bf16[2048,768]{1,0:T(8,128)(2,1)} %collective-permute-done.5, bf16[2008,768]{1,0:T(8,128)(2,1)} %copy-done.16, s32[2048]{0:T(1024)S(1)} %bitcast.460), kind=kOutput, calls=%fused_computation.51 | convolution fusion | flops 6323879936 | bytes 9383936 | tf_op jit(solution)/shard_map/dot_general | solution.py:192
  64.5 3.3 copy.119
  70.0 26.5 %collective-permute-done.6 = bf16[512,768]{1,0:T(8,128)(2,1)} collective-permute-done((bf16[512,768]{1,0:T(8,128)(2,1)}, bf16[512,768]{1,0:T(8,128)(2,1)}, u32[]{:S(2)}, u32[]{:S(2)}) %collective-permute-start.6) | collective-permute-done | bytes 786464 | tf_op jit(solution)/shard_map/ppermute | solution.py:66
  101.5 3.0 collective-permute-start.10
  105.3 21.0 %collective-permute-done.7 = bf16[256,768]{1,0:T(8,128)(2,1)} collective-permute-done((bf16[256,768]{1,0:T(8,128)(2,1)S(1)}, bf16[256,768]{1,0:T(8,128)(2,1)}, u32[]{:S(2)}, u32[]{:S(2)}) %collective-permute-start.7) | collective-permute-done | bytes 393248 | tf_op jit(solution)/shard_map/ppermute | solution.py:66
  127.5 2.6 collective-permute-start.8
  130.1 3.0 collective-permute-done.10
  134.9 9.2 %collective-permute-done.11 = bf16[128,768]{1,0:T(8,128)(2,1)S(1)} collective-permute-done((bf16[128,768]{1,0:T(8,128)(2,1)S(1)}, bf16[128,768]{1,0:T(8,128)(2,1)S(1)}, u32[]{:S(2)}, u32[]{:S(2)}) %collective-permute-start.11) | collective-permute-done | bytes 196640 | tf_op jit(solution)/shard_map/ppermute | solution.py:66
  146.8 6.3 all-gather.7.cloned.1.call-done.refs_2_
  153.1 6.1 attention_forward.3
  163.0 8.8 %conditional.5 = ((f32[256,768]{1,0:T(8,128)}, bf16[256,768]{1,0:T(8,128)(2,1)}, f32[256,3072]{1,0:T(8,128)S(1)})) conditional(s32[]{:T(128)} %convert_element_type.427, () %tuple.158, (f32[7,768]{1,0:T(8,128)}, f32[256,768]{1,0:T(8,128)}, f32[1,768]{1,0:T(1,128)S(1)}, bf16[4,3072,768]{2,1,0:T(8,128)(2,1)}) %tuple.159), branch_computations={%region_0.1_spmd, %region_1.2_spmd} | conditional | bytes 4325418 | solution.py:751
  163.8 8.0 feed_forward.2
  171.8 5.8 collective-permute-done.13
  183.9 3.4 collective-permute-start.14
  188.8 6.5 collective-permute-done.14
  196.0 6.4 conditional.6
  202.5 7.4 collective-permute-done.15
  212.0 6.9 collective-permute-done.16
  220.4 42.8 %all-gather.9.cloned.1.call-done = bf16[2048,768]{1,0:T(8,128)(2,1)} async-done(((bf16[128,768]{1,0:T(8,128)(2,1)}), bf16[2048,768]{1,0:T(8,128)(2,1)}) %all-gather.9.cloned.1.call-update) | async-done | bytes 3145744 | tf_op jit(solution)/shard_map/all_gather | solution.py:796
  263.2 9.6 %fusion.100 = (f32[2048]{0:T(1024)S(1)}, f32[2048,2008]{0,1:T(8,128)S(1)}) fusion(bf16[2048,768]{1,0:T(8,128)(2,1)} %all-gather.9.cloned.1.call-done, bf16[2008,768]{1,0:T(8,128)(2,1)} %copy-done.16), kind=kOutput, calls=%fused_computation.292 | convolution fusion | flops 6320732160 | bytes 22687744 | tf_op jit(solution)/shard_map/nd,vd->nv/dot_general | solution.py:797
  272.8 5.2 select_reduce_fusion
  278.0 20.1 %all-gather.2 = f32[16,2,2048]{2,1,0:T(2,128)S(1)} all-gather(f32[1,2,2048]{2,1,0:T(2,128)S(1)} %maximum_bitcast_fusion), channel_id=2, replica_groups=mesh['section'=16,'dp'=2] {'section'}, dimensions={0}, use_global_device_ids=true | all-gather | bytes 278528 | tf_op jit(solution)/shard_map/all_gather | solution.py:802
  298.5 4.2 subtract_convert_fusion
  302.8 7.4 fusion.101
  311.0 2.8 collective-permute-done.17
  316.1 8.6 %fusion.102 = f32[2008,768]{1,0:T(8,128)} fusion(bf16[2048,2008]{0,1:T(8,128)(2,1)S(1)} %subtract_convert_fusion, bf16[2048,768]{1,0:T(8,128)(2,1)S(1)} %copy-done.68), kind=kOutput, calls=%fused_computation.294 | convolution fusion | flops 6316621824 | bytes 17539072 | tf_op jit(solution)/shard_map/dot_general | solution.py:215
  324.6 9.5 %collective-permute-done.18 = bf16[512,768]{1,0:T(8,128)(2,1)S(1)} collective-permute-done((bf16[512,768]{1,0:T(8,128)(2,1)S(1)}, bf16[512,768]{1,0:T(8,128)(2,1)S(1)}, u32[]{:S(2)}, u32[]{:S(2)}) %collective-permute-start.18) | collective-permute-done | bytes 786464 | tf_op jit(solution)/shard_map/ppermute | solution.py:66
  334.6 10.6 %collective-permute-done.19 = bf16[256,768]{1,0:T(8,128)(2,1)S(1)} collective-permute-done((bf16[256,768]{1,0:T(8,128)(2,1)S(1)}, bf16[256,768]{1,0:T(8,128)(2,1)S(1)}, u32[]{:S(2)}, u32[]{:S(2)}) %collective-permute-start.19) | collective-permute-done | bytes 393248 | tf_op jit(solution)/shard_map/ppermute | solution.py:66
  345.4 10.5 %collective-permute-done.20 = bf16[128,768]{1,0:T(8,128)(2,1)S(1)} collective-permute-done((bf16[128,768]{1,0:T(8,128)(2,1)S(1)}, bf16[128,768]{1,0:T(8,128)(2,1)S(1)}, u32[]{:S(2)}, u32[]{:S(2)}) %collective-permute-start.20) | collective-permute-done | bytes 196640 | tf_op jit(solution)/shard_map/ppermute | solution.py:66
  356.0 3.4 collective-permute-start.21
  363.8 10.3 %conditional.7 = (bf16[256,768]{1,0:T(8,128)(2,1)}, f32[256,768]{1,0:T(8,128)}, bf16[2,1536,768]{2,1,0:T(8,128)(2,1)}, bf16[2,1536,768]{2,1,0:T(8,128)(2,1)}, bf...) conditional(s32[]{:T(128)} %convert_element_type.428, () %tuple.150, ...), branch_computations={%region_8.9_spmd, %region_9.10_spmd} | conditional | flops 2309 | bytes 15344714 | solution.py:842
  375.4 30.9 %collective-permute-done.22 = bf16[256,768]{1,0:T(8,128)(2,1)S(1)} collective-permute-done((bf16[256,768]{1,0:T(8,128)(2,1)}, bf16[256,768]{1,0:T(8,128)(2,1)S(1)}, u32[]{:S(2)}, u32[]{:S(2)}) %collective-permute-start.22) | collective-permute-done | bytes 393248 | tf_op jit(solution)/shard_map/ppermute | solution.py:78
  412.2 19.2 %conditional.8 = (f32[256,768]{1,0:T(8,128)}, f32[2,768]{1,0:T(2,128)S(1)}, f32[12,128,128]{2,1,0:T(8,128)}, bf16[1536,768]{1,0:T(8,128)(2,1)}, bf16[1536,768]{1...) conditional(s32[]{:T(128)} %convert_element_type.427, (f32[256,768]{1,0:T(8,128)}, ...), branch_computations={%region_10.11_spmd, %region_11.12_spmd} | conditional | flops 198149 | bytes 5535892 | solution.py:884
  413.1 14.2 %feed_backward.3 = (f32[256,768]{1,0:T(8,128)}, bf16[2,1536,768]{2,1,0:T(8,128)(2,1)}, bf16[2,1536,768]{2,1,0:T(8,128)(2,1)}, f32[2,768]{1,0:T(2,128)}) custom-call(s32[1]{0:T(128)} %bitcast.2.mine_ref, bf16[256,768]{1,0:T(8,128)(2,1)} %get-tuple-element.185.upstream_ref, f32[256,768]{1,0:T(8,128)} %get-tuple-element.186.after_ref, ...), custom_call_target="tpu_custom_call" | custom-call | tf_op jit(solution)/shard_map/cond/branch_1_fun/feed_backward/pallas_call | solution.py:365
  435.8 15.9 %conditional.9 = (bf16[256,768]{1,0:T(8,128)(2,1)}, f32[7,768]{1,0:T(8,128)S(1)}, f32[12,128,128]{2,1,0:T(8,128)}, bf16[1536,768]{1,0:T(8,128)(2,1)}, bf16[1536,768]{1,0:T(8,128)(2,1)}) conditional(s32[]{:T(128)} %convert_element_type.427, (f32[256,768]{1,0:T(8,128)}, f32[2,768]{1,0:T(2,128)S(1)}, f32[3,768]{1,0:T(4,128)S(1)}, ...), branch_computations={%region_12.13_spmd, %region_13.14_spmd} | conditional | flops 207360 | bytes 1219712 | solution.py:909
  435.8 15.5 %attention_backward.5 = (bf16[256,768]{1,0:T(8,128)(2,1)}, bf16[1536,768]{1,0:T(8,128)(2,1)}, bf16[1536,768]{1,0:T(8,128)(2,1)}, f32[1,768]{1,0:T(1,128)S(1)}, f32[12,128,128]{2,1,0:T(8,128)}) custom-call(s32[1]{0:T(128)} %bitcast.3.mine_ref, f32[256,768]{1,0:T(8,128)} %get-tuple-element.202.refs_0_, f32[256,768]{1,0:T(8,128)S(1)} %get-tuple-element.203.refs_1_, ...), custom_call_target="tpu_custom_call" | custom-call | tf_op jit(solution)/shard_map/cond/branch_1_fun/attention_backward/pallas_call | solution.py:559
  459.7 4.4 maximum_select_fusion
  469.0 5.2 add_convert_fusion
  484.2 3.1 multiply_reduce_fusion.2
  488.2 58.8 %collective-permute-done.41 = bf16[1536,768]{1,0:T(8,128)(2,1)} collective-permute-done((bf16[1536,768]{1,0:T(8,128)(2,1)}, bf16[1536,768]{1,0:T(8,128)(2,1)}, u32[]{:S(2)}, u32[]{:S(2)}) %collective-permute-start.41) | collective-permute-done | bytes 2359328 | tf_op jit(solution)/shard_map/ppermute | solution.py:66
  558.3 3.0 add_convert_fusion.1
  563.0 14.3 %collective-permute-done.42 = bf16[768,768]{1,0:T(8,128)(2,1)} collective-permute-done((bf16[768,768]{1,0:T(8,128)(2,1)S(1)}, bf16[768,768]{1,0:T(8,128)(2,1)}, u32[]{:S(2)}, u32[]{:S(2)}) %collective-permute-start.42) | collective-permute-done | bytes 1179680 | tf_op jit(solution)/shard_map/ppermute | solution.py:66
  577.3 11.3 %add_convert_fusion.5 = bf16[1008,768]{1,0:T(8,128)(2,1)} fusion(f32[2008,768]{1,0:T(8,128)} %fusion.102, s32[]{:T(128)S(6)} %select_n.552, bf16[4096,768]{1,0:T(8,128)(2,1)} %all-gather.11.cloned.1.call-done, s32[4096]{0:T(1024)} %bitcast.454, s32[1008]{0:T(1024)S(1)} %iota_add_fusion.1), kind=kOutput, calls=%fused_computation.41 | convolution fusion | flops 6347464704 | bytes 10956740 | tf_op jit(solution)/shard_map/dot_general | solution.py:207
  592.6 9.5 %add_convert_fusion.4 = bf16[1008,768]{1,0:T(8,128)(2,1)} fusion(f32[2008,768]{1,0:T(8,128)} %fusion.102, s32[]{:T(128)S(6)} %select_n.565, bf16[4096,768]{1,0:T(8,128)(2,1)S(1)} %copy-done.67, s32[4096]{0:T(1024)S(1)} %bitcast.455, s32[1008]{0:T(1024)S(1)} %iota_add_fusion), kind=kOutput, calls=%fused_computation.40 | convolution fusion | flops 6347464704 | bytes 10956740 | tf_op jit(solution)/shard_map/dot_general | solution.py:207
  602.1 27.4 %collective-permute-start.44 = (bf16[1008,768]{1,0:T(8,128)(2,1)}, bf16[1008,768]{1,0:T(8,128)(2,1)}, u32[]{:S(2)}, u32[]{:S(2)}) collective-permute-start(bf16[1008,768]{1,0:T(8,128)(2,1)} %add_convert_fusion.4), channel_id=1, source_target_pairs={{0,1},{1,0},{2,3},{3,2},{4,5},{5,4},{6,7},{7,6},{8,9},{9,8},{10,11... | collective-permute-start | bytes 4644872 | tf_op jit(solution)/shard_map/ppermute | solution.py:70
  640.3 26.4 %collective-permute-done.29 = f32[8,768]{1,0:T(8,128)} collective-permute-done((f32[8,768]{1,0:T(8,128)}, f32[8,768]{1,0:T(8,128)}, u32[]{:S(2)}, u32[]{:S(2)}) %collective-permute-start.29) | collective-permute-done | bytes 24608 | tf_op jit(solution)/shard_map/ppermute | solution.py:66
  675.3 3.7 multiply_reduce_fusion
  687.9 2.9 collective-permute-start.47
  690.8 3.0 fusion.41
  693.8 6.2 collective-permute-done.51
  707.7 10.7 %collective-permute-done.49 = f32[9,768]{1,0:T(8,128)S(1)} collective-permute-done((f32[9,768]{1,0:T(8,128)S(1)}, f32[9,768]{1,0:T(8,128)S(1)}, u32[]{:S(2)}, u32[]{:S(2)}) %collective-permute-start.49) | collective-permute-done | bytes 27680 | tf_op jit(solution)/shard_map/ppermute | solution.py:70
  722.3 4.5 multiply_subtract_fusion.1
  730.2 3.4 multiply_reduce_fusion.3
  738.1 3.7 multiply_subtract_fusion.2
  741.7 2.8 collective-permute-start.60
  756.7 7.8 collective-permute-done.54
  769.1 11.1 %multiply_subtract_fusion = (f32[2008,768]{1,0:T(8,128)}, f32[2008,768]{1,0:T(8,128)}, f32[2008,768]{1,0:T(8,128)}) fusion(f32[2008,768]{1,0:T(8,128)S(1)} %bitcast.358, f32[]{:T(128)S(6)} %div.101, bf16[1000,768]{1,0:T(8,128)(2,1)S(1)} %slice_select_fusion, bf16[1008,768]{1,0:T(8,128)(2,1)S(1)} %broadcast_select_fusion, f32[2008,768]{1,0:T(8,128)} %param.42, ...), kind=kLoop, calls=%fused_computation.25 | loop fusion | flops 30842880 | bytes 40095748 | tf_op jit(solution)/shard_map/sub | solution.py:584
  780.2 12.6 %collective-permute-done.55 = bf16[4,4,48,768]{3,2,1,0:T(8,128)(2,1)S(1)} collective-permute-done((bf16[4,4,48,768]{3,2,1,0:T(8,128)(2,1)S(1)}, bf16[4,4,48,768]{3,2,1,0:T(8,128)(2,1)S(1)}, u32[]{:S(2)}, u32[]{:S(2)}) %collective-permute-start.55) | collective-permute-done | bytes 1179680 | tf_op jit(solution)/shard_map/ppermute | solution.py:70
  799.3 2.7 fusion.24
  (447 shorter events, 193.8 us)
Async XLA Ops:
  7.2 145.9 %all-gather.7.cloned.1.call-start = ((), (), s32[]{:S(2)}) async-start(), calls=%async_computation | async-start | bytes 20054016 | tf_op jit(solution)/shard_map/all_gather | solution.py:715
  12.3 250.9 %all-gather.9.cloned.1.call-start = ((), (), s32[]{:S(2)}) async-start(), calls=%async_computation.1 | async-start | bytes 3342336 | tf_op jit(solution)/shard_map/all_gather | solution.py:796
  13.0 4.6 collective-permute-start
  17.6 1.2 collective-permute-start.1
  18.8 3.7 collective-permute-start.2
  22.5 4.1 collective-permute-start.3
  26.6 6.3 collective-permute-start.4
  41.8 6.0 collective-permute-start.5
  42.9 116.3 %collective-permute-start.12 = (bf16[4,2,48,768]{3,2,1,0:T(8,128)(2,1)}, bf16[4,2,48,768]{3,2,1,0:T(8,128)(2,1)}, u32[]{:S(2)}, u32[]{:S(2)}) collective-permute-start(bf16[4,2,48,768]{3,2,1,0:T(8,128)(2,1)} %dynamic-slice_bitcast_fusion.10), channel_id=1, source_target_pairs={{0,2},{1,3},{2,0},{3,1},{4,6},{5,7},{6,4},{7,5},{8,10},{9,11},{10,... | collective-permute-start | bytes 1769480 | tf_op jit(solution)/shard_map/ppermute | solution.py:66
  59.2 37.3 %collective-permute-start.6 = (bf16[512,768]{1,0:T(8,128)(2,1)}, bf16[512,768]{1,0:T(8,128)(2,1)}, u32[]{:S(2)}, u32[]{:S(2)}) collective-permute-start(bf16[512,768]{1,0:T(8,128)(2,1)} %bitcast.31), channel_id=1, source_target_pairs={{0,4},{1,5},{2,6},{3,7},{4,0},{5,1},{6,2},{7,3},{8,12},{9,13},{10,... | collective-permute-start | bytes 2359304 | tf_op jit(solution)/shard_map/ppermute | solution.py:66
  62.8 37.3 %collective-permute-start.9 = (bf16[512,768]{1,0:T(8,128)(2,1)}, bf16[512,768]{1,0:T(8,128)(2,1)}, u32[]{:S(2)}, u32[]{:S(2)}) collective-permute-start(bf16[512,768]{1,0:T(8,128)(2,1)} %bitcast.40), channel_id=1, source_target_pairs={{0,8},{1,9},{2,10},{3,11},{4,12},{5,13},{6,14},{7,15},{8,0},{9,1},... | collective-permute-start | bytes 2359304 | tf_op jit(solution)/shard_map/ppermute | solution.py:66
  97.9 28.5 %collective-permute-start.7 = (bf16[256,768]{1,0:T(8,128)(2,1)S(1)}, bf16[256,768]{1,0:T(8,128)(2,1)}, u32[]{:S(2)}, u32[]{:S(2)}) collective-permute-start(bf16[256,768]{1,0:T(8,128)(2,1)S(1)} %bitcast.440), channel_id=1, source_target_pairs={{0,8},{1,9},{2,10},{3,11},{4,12},{5,13},{6,14},{7,15},{8,0},{9,1},... | collective-permute-start | bytes 1179656 | tf_op jit(solution)/shard_map/ppermute | solution.py:66
  101.5 31.6 %collective-permute-start.10 = (bf16[256,768]{1,0:T(8,128)(2,1)S(1)}, bf16[256,768]{1,0:T(8,128)(2,1)S(1)}, u32[]{:S(2)}, u32[]{:S(2)}) collective-permute-start(bf16[256,768]{1,0:T(8,128)(2,1)S(1)} %dynamic-slice_bitcast_fusion.11), channel_id=1, source_target_pairs={{0,16},{1,17},{2,18},{3,19},{4,20},{5,21},{6,22},{7,23},{8,24},{9,... | collective-permute-start | bytes 1179656 | tf_op jit(solution)/shard_map/ppermute | solution.py:66
  127.5 19.1 %collective-permute-start.8 = (bf16[128,768]{1,0:T(8,128)(2,1)S(1)}, bf16[128,768]{1,0:T(8,128)(2,1)S(1)}, u32[]{:S(2)}, u32[]{:S(2)}) collective-permute-start(bf16[128,768]{1,0:T(8,128)(2,1)S(1)} %dynamic-slice_bitcast_fusion.16), channel_id=1, source_target_pairs={{0,16},{1,17},{2,18},{3,19},{4,20},{5,21},{6,22},{7,23},{8,24},{9,... | collective-permute-start | bytes 589832 | tf_op jit(solution)/shard_map/ppermute | solution.py:66
  133.2 10.9 %collective-permute-start.11 = (bf16[128,768]{1,0:T(8,128)(2,1)S(1)}, bf16[128,768]{1,0:T(8,128)(2,1)S(1)}, u32[]{:S(2)}, u32[]{:S(2)}) collective-permute-start(bf16[128,768]{1,0:T(8,128)(2,1)S(1)} %dynamic-slice_bitcast_fusion.15), channel_id=1, source_target_pairs={{0,4},{1,5},{2,6},{3,7},{4,0},{5,1},{6,2},{7,3},{8,12},{9,13},{10,... | collective-permute-start | bytes 589832 | tf_op jit(solution)/shard_map/ppermute | solution.py:66
  161.8 15.8 %collective-permute-start.13 = (bf16[4,2,48,768]{3,2,1,0:T(8,128)(2,1)}, bf16[4,2,48,768]{3,2,1,0:T(8,128)(2,1)}, u32[]{:S(2)}, u32[]{:S(2)}) collective-permute-start(bf16[4,2,48,768]{3,2,1,0:T(8,128)(2,1)} %get-tuple-element.609), channel_id=1, source_target_pairs={{0,4},{1,5},{2,6},{3,7},{4,0},{5,1},{6,2},{7,3},{8,12},{9,13},{10,... | collective-permute-start | bytes 1769480 | tf_op jit(solution)/shard_map/ppermute | solution.py:66
  181.5 28.4 %collective-permute-start.15 = (bf16[2,192,768]{2,1,0:T(8,128)(2,1)}, bf16[2,192,768]{2,1,0:T(8,128)(2,1)}, u32[]{:S(2)}, u32[]{:S(2)}) collective-permute-start(bf16[2,192,768]{2,1,0:T(8,128)(2,1)} %get-tuple-element.607), channel_id=1, source_target_pairs={{0,16},{1,17},{2,18},{3,19},{4,20},{5,21},{6,22},{7,23},{8,24},{9,... | collective-permute-start | bytes 1769480 | tf_op jit(solution)/shard_map/ppermute | solution.py:66
  183.9 11.4 %collective-permute-start.14 = (bf16[256,768]{1,0:T(8,128)(2,1)}, bf16[256,768]{1,0:T(8,128)(2,1)S(1)}, u32[]{:S(2)}, u32[]{:S(2)}) collective-permute-start(bf16[256,768]{1,0:T(8,128)(2,1)} %get-tuple-element.372), channel_id=1, source_target_pairs={{0,1},{2,3},{4,5},{6,7},{8,9},{10,11},{12,13},{14,15},{16,17},{18,... | collective-permute-start | bytes 1179656 | tf_op jit(solution)/shard_map/ppermute | solution.py:74
  209.9 8.9 %collective-permute-start.16 = (bf16[128,768]{1,0:T(8,128)(2,1)S(1)}, bf16[128,768]{1,0:T(8,128)(2,1)S(1)}, u32[]{:S(2)}, u32[]{:S(2)}) collective-permute-start(bf16[128,768]{1,0:T(8,128)(2,1)S(1)} %slice.162), channel_id=1, source_target_pairs={{1,0},{3,2},{5,4},{7,6},{9,8},{11,10},{13,12},{15,14},{17,16},{19,... | collective-permute-start | bytes 589832 | tf_op jit(solution)/shard_map/ppermute | solution.py:78
  219.6 357.7 %all-gather.11.cloned.1.call-start = ((), (), s32[]{:S(2)}) async-start(), calls=%async_computation.2 | async-start | bytes 6684672 | tf_op jit(solution)/shard_map/all_gather | solution.py:926
  310.3 3.5 collective-permute-start.17
  314.3 19.9 %collective-permute-start.18 = (bf16[512,768]{1,0:T(8,128)(2,1)S(1)}, bf16[512,768]{1,0:T(8,128)(2,1)S(1)}, u32[]{:S(2)}, u32[]{:S(2)}) collective-permute-start(bf16[512,768]{1,0:T(8,128)(2,1)S(1)} %bitcast.428), channel_id=1, source_target_pairs={{0,4},{1,5},{2,6},{3,7},{4,0},{5,1},{6,2},{7,3},{8,12},{9,13},{10,... | collective-permute-start | bytes 2359304 | tf_op jit(solution)/shard_map/ppermute | solution.py:66
  334.5 10.6 %collective-permute-start.19 = (bf16[256,768]{1,0:T(8,128)(2,1)S(1)}, bf16[256,768]{1,0:T(8,128)(2,1)S(1)}, u32[]{:S(2)}, u32[]{:S(2)}) collective-permute-start(bf16[256,768]{1,0:T(8,128)(2,1)S(1)} %bitcast.441), channel_id=1, source_target_pairs={{0,8},{1,9},{2,10},{3,11},{4,12},{5,13},{6,14},{7,15},{8,0},{9,1},... | collective-permute-start | bytes 1179656 | tf_op jit(solution)/shard_map/ppermute | solution.py:66
  345.3 10.6 %collective-permute-start.20 = (bf16[128,768]{1,0:T(8,128)(2,1)S(1)}, bf16[128,768]{1,0:T(8,128)(2,1)S(1)}, u32[]{:S(2)}, u32[]{:S(2)}) collective-permute-start(bf16[128,768]{1,0:T(8,128)(2,1)S(1)} %dynamic-slice_bitcast_fusion.14), channel_id=1, source_target_pairs={{0,16},{1,17},{2,18},{3,19},{4,20},{5,21},{6,22},{7,23},{8,24},{9,... | collective-permute-start | bytes 589832 | tf_op jit(solution)/shard_map/ppermute | solution.py:66
  356.0 7.7 collective-permute-start.21
  363.7 42.6 %collective-permute-start.23 = (bf16[2,2,192,768]{3,2,1,0:T(8,128)(2,1)}, bf16[2,2,192,768]{3,2,1,0:T(8,128)(2,1)}, u32[]{:S(2)}, u32[]{:S(2)}) collective-permute-start(bf16[2,2,192,768]{3,2,1,0:T(8,128)(2,1)} %maximum_select_fusion.4), channel_id=1, source_target_pairs={{0,8},{1,9},{2,10},{3,11},{4,12},{5,13},{6,14},{7,15},{8,0},{9,1},... | collective-permute-start | bytes 3538952 | tf_op jit(solution)/shard_map/ppermute | solution.py:66
  374.1 32.2 %collective-permute-start.22 = (bf16[256,768]{1,0:T(8,128)(2,1)}, bf16[256,768]{1,0:T(8,128)(2,1)S(1)}, u32[]{:S(2)}, u32[]{:S(2)}) collective-permute-start(bf16[256,768]{1,0:T(8,128)(2,1)} %get-tuple-element.390), channel_id=1, source_target_pairs={{1,0},{3,2},{5,4},{7,6},{9,8},{11,10},{13,12},{15,14},{17,16},{19,... | collective-permute-start | bytes 1179656 | tf_op jit(solution)/shard_map/ppermute | solution.py:78
  410.5 20.9 %collective-permute-start.25 = (bf16[768,768]{1,0:T(8,128)(2,1)}, bf16[768,768]{1,0:T(8,128)(2,1)}, u32[]{:S(2)}, u32[]{:S(2)}) collective-permute-start(bf16[768,768]{1,0:T(8,128)(2,1)} %dynamic-slice_bitcast_fusion.1), channel_id=1, source_target_pairs={{1,5},{3,7},{5,1},{7,3},{9,13},{11,15},{13,9},{15,11},{17,21},{19,... | collective-permute-start | bytes 3538952 | tf_op jit(solution)/shard_map/ppermute | solution.py:66
  431.4 20.4 %collective-permute-start.31 = (bf16[2,1536,768]{2,1,0:T(8,128)(2,1)}, bf16[2,1536,768]{2,1,0:T(8,128)(2,1)}, u32[]{:S(2)}, u32[]{:S(2)}) collective-permute-start(bf16[2,1536,768]{2,1,0:T(8,128)(2,1)} %get-tuple-element.433), channel_id=1, source_target_pairs={{0,2},{1,3},{2,0},{3,1},{4,6},{5,7},{6,4},{7,5},{8,10},{9,11},{10,... | collective-permute-start | bytes 14155784 | tf_op jit(solution)/shard_map/ppermute | solution.py:66
  434.3 17.5 %collective-permute-start.30 = (bf16[384,768]{1,0:T(8,128)(2,1)}, bf16[384,768]{1,0:T(8,128)(2,1)}, u32[]{:S(2)}, u32[]{:S(2)}) collective-permute-start(bf16[384,768]{1,0:T(8,128)(2,1)} %bitcast.88), channel_id=1, source_target_pairs={{1,9},{3,11},{5,13},{7,15},{9,1},{11,3},{13,5},{15,7},{17,25},{19,... | collective-permute-start | bytes 1769480 | tf_op jit(solution)/shard_map/ppermute | solution.py:66
  468.3 8.2 %collective-permute-start.35 = (bf16[192,768]{1,0:T(8,128)(2,1)S(1)}, bf16[192,768]{1,0:T(8,128)(2,1)S(1)}, u32[]{:S(2)}, u32[]{:S(2)}) collective-permute-start(bf16[192,768]{1,0:T(8,128)(2,1)S(1)} %dynamic-slice_bitcast_fusion.13), channel_id=1, source_target_pairs={{1,17},{3,19},{5,21},{7,23},{9,25},{11,27},{13,29},{15,31},{17,1},... | collective-permute-start | bytes 884744 | tf_op jit(solution)/shard_map/ppermute | solution.py:66
  475.9 71.1 %collective-permute-start.41 = (bf16[1536,768]{1,0:T(8,128)(2,1)}, bf16[1536,768]{1,0:T(8,128)(2,1)}, u32[]{:S(2)}, u32[]{:S(2)}) collective-permute-start(bf16[1536,768]{1,0:T(8,128)(2,1)} %bitcast.130), channel_id=1, source_target_pairs={{0,4},{1,5},{2,6},{3,7},{4,0},{5,1},{6,2},{7,3},{8,12},{9,13},{10,... | collective-permute-start | bytes 7077896 | tf_op jit(solution)/shard_map/ppermute | solution.py:66
  478.0 2.7 collective-permute-start.26
  478.4 4.4 collective-permute-start.37
  481.3 71.9 %collective-permute-start.27 = (f32[8,768]{1,0:T(8,128)}, f32[8,768]{1,0:T(8,128)}, u32[]{:S(2)}, u32[]{:S(2)}) collective-permute-start(f32[8,768]{1,0:T(8,128)} %fusion.125), channel_id=1, source_target_pairs={{0,4},{1,5},{2,6},{3,7},{4,0},{5,1},{6,2},{7,3},{8,12},{9,13},{10,... | collective-permute-start | bytes 73736 | tf_op jit(solution)/shard_map/ppermute | solution.py:66
  482.7 75.6 %collective-permute-start.32 = (bf16[1536,768]{1,0:T(8,128)(2,1)}, bf16[1536,768]{1,0:T(8,128)(2,1)}, u32[]{:S(2)}, u32[]{:S(2)}) collective-permute-start(bf16[1536,768]{1,0:T(8,128)(2,1)} %get-tuple-element.435), channel_id=1, source_target_pairs={{0,2},{1,3},{2,0},{3,1},{4,6},{5,7},{6,4},{7,5},{8,10},{9,11},{10,... | collective-permute-start | bytes 7077896 | tf_op jit(solution)/shard_map/ppermute | solution.py:66
  487.5 67.7 %collective-permute-start.38 = (bf16[4,2,48,768]{3,2,1,0:T(8,128)(2,1)S(1)}, bf16[4,2,48,768]{3,2,1,0:T(8,128)(2,1)S(1)}, u32[]{:S(2)}, u32[]{:S(2)}) collective-permute-start(bf16[4,2,48,768]{3,2,1,0:T(8,128)(2,1)S(1)} %get-tuple-element.444), channel_id=1, source_target_pairs={{1,3},{3,1},{5,7},{7,5},{9,11},{11,9},{13,15},{15,13},{17,19},{19,... | collective-permute-start | bytes 1769480 | tf_op jit(solution)/shard_map/ppermute | solution.py:66
  549.5 27.8 %collective-permute-start.42 = (bf16[768,768]{1,0:T(8,128)(2,1)S(1)}, bf16[768,768]{1,0:T(8,128)(2,1)}, u32[]{:S(2)}, u32[]{:S(2)}) collective-permute-start(bf16[768,768]{1,0:T(8,128)(2,1)S(1)} %bitcast.416), channel_id=1, source_target_pairs={{0,8},{1,9},{2,10},{3,11},{4,12},{5,13},{6,14},{7,15},{8,0},{9,1},... | collective-permute-start | bytes 3538952 | tf_op jit(solution)/shard_map/ppermute | solution.py:66
  554.6 78.4 %collective-permute-start.28 = (f32[8,768]{1,0:T(8,128)}, f32[8,768]{1,0:T(8,128)}, u32[]{:S(2)}, u32[]{:S(2)}) collective-permute-start(f32[8,768]{1,0:T(8,128)} %add.437), channel_id=1, source_target_pairs={{0,8},{1,9},{2,10},{3,11},{4,12},{5,13},{6,14},{7,15},{8,0},{9,1},... | collective-permute-start | bytes 73736 | tf_op jit(solution)/shard_map/ppermute | solution.py:66
  556.4 79.7 %collective-permute-start.39 = (bf16[4,2,48,768]{3,2,1,0:T(8,128)(2,1)}, bf16[4,2,48,768]{3,2,1,0:T(8,128)(2,1)}, u32[]{:S(2)}, u32[]{:S(2)}) collective-permute-start(bf16[4,2,48,768]{3,2,1,0:T(8,128)(2,1)} %get-tuple-element.445), channel_id=1, source_target_pairs={{1,5},{3,7},{5,1},{7,3},{9,13},{11,15},{13,9},{15,11},{17,21},{19,... | collective-permute-start | bytes 1769480 | tf_op jit(solution)/shard_map/ppermute | solution.py:66
  562.4 27.3 %collective-permute-start.33 = (bf16[768,768]{1,0:T(8,128)(2,1)}, bf16[768,768]{1,0:T(8,128)(2,1)}, u32[]{:S(2)}, u32[]{:S(2)}) collective-permute-start(bf16[768,768]{1,0:T(8,128)(2,1)} %dynamic-slice_bitcast_fusion), channel_id=1, source_target_pairs={{0,4},{1,5},{2,6},{3,7},{4,0},{5,1},{6,2},{7,3},{8,12},{9,13},{10,... | collective-permute-start | bytes 3538952 | tf_op jit(solution)/shard_map/ppermute | solution.py:66
  591.4 44.8 %collective-permute-start.34 = (bf16[384,768]{1,0:T(8,128)(2,1)S(1)}, bf16[384,768]{1,0:T(8,128)(2,1)S(1)}, u32[]{:S(2)}, u32[]{:S(2)}) collective-permute-start(bf16[384,768]{1,0:T(8,128)(2,1)S(1)} %bitcast.434), channel_id=1, source_target_pairs={{0,8},{1,9},{2,10},{3,11},{4,12},{5,13},{6,14},{7,15},{8,0},{9,1},... | collective-permute-start | bytes 1769480 | tf_op jit(solution)/shard_map/ppermute | solution.py:66
  602.1 73.2 %collective-permute-start.44 = (bf16[1008,768]{1,0:T(8,128)(2,1)}, bf16[1008,768]{1,0:T(8,128)(2,1)}, u32[]{:S(2)}, u32[]{:S(2)}) collective-permute-start(bf16[1008,768]{1,0:T(8,128)(2,1)} %add_convert_fusion.4), channel_id=1, source_target_pairs={{0,1},{1,0},{2,3},{3,2},{4,5},{5,4},{6,7},{7,6},{8,9},{9,8},{10,11... | collective-permute-start | bytes 4644872 | tf_op jit(solution)/shard_map/ppermute | solution.py:70
  631.1 38.3 %collective-permute-start.43 = (bf16[384,768]{1,0:T(8,128)(2,1)S(1)}, bf16[384,768]{1,0:T(8,128)(2,1)S(1)}, u32[]{:S(2)}, u32[]{:S(2)}) collective-permute-start(bf16[384,768]{1,0:T(8,128)(2,1)S(1)} %bitcast.433), channel_id=1, source_target_pairs={{0,16},{1,17},{2,18},{3,19},{4,20},{5,21},{6,22},{7,23},{8,24},{9,... | collective-permute-start | bytes 1769480 | tf_op jit(solution)/shard_map/ppermute | solution.py:66
  634.4 32.3 %collective-permute-start.29 = (f32[8,768]{1,0:T(8,128)}, f32[8,768]{1,0:T(8,128)}, u32[]{:S(2)}, u32[]{:S(2)}) collective-permute-start(f32[8,768]{1,0:T(8,128)} %add.438), channel_id=1, source_target_pairs={{0,16},{1,17},{2,18},{3,19},{4,20},{5,21},{6,22},{7,23},{8,24},{9,... | collective-permute-start | bytes 73736 | tf_op jit(solution)/shard_map/ppermute | solution.py:66
  636.4 36.7 %collective-permute-start.40 = (bf16[192,768]{1,0:T(8,128)(2,1)S(1)}, bf16[192,768]{1,0:T(8,128)(2,1)S(1)}, u32[]{:S(2)}, u32[]{:S(2)}) collective-permute-start(bf16[192,768]{1,0:T(8,128)(2,1)S(1)} %dynamic-slice_bitcast_fusion.12), channel_id=1, source_target_pairs={{0,16},{1,17},{2,18},{3,19},{4,20},{5,21},{6,22},{7,23},{8,24},{9,... | collective-permute-start | bytes 884744 | tf_op jit(solution)/shard_map/ppermute | solution.py:66
  670.3 20.5 %collective-permute-start.57 = (bf16[2,192,768]{2,1,0:T(8,128)(2,1)S(1)}, bf16[2,192,768]{2,1,0:T(8,128)(2,1)}, u32[]{:S(2)}, u32[]{:S(2)}) collective-permute-start(bf16[2,192,768]{2,1,0:T(8,128)(2,1)S(1)} %bitcast.403), channel_id=1, source_target_pairs={{0,1},{1,0},{2,3},{3,2},{4,5},{5,4},{6,7},{7,6},{8,9},{9,8},{10,11... | collective-permute-start | bytes 1769480 | tf_op jit(solution)/shard_map/ppermute | solution.py:70
  680.4 3.4 collective-permute-start.45
  683.8 16.2 %collective-permute-start.51 = (bf16[192,768]{1,0:T(8,128)(2,1)S(1)}, bf16[192,768]{1,0:T(8,128)(2,1)S(1)}, u32[]{:S(2)}, u32[]{:S(2)}) collective-permute-start(bf16[192,768]{1,0:T(8,128)(2,1)S(1)} %get-tuple-element.459), channel_id=1, source_target_pairs={{0,16},{1,17},{2,18},{3,19},{4,20},{5,21},{6,22},{7,23},{8,24},{9,... | collective-permute-start | bytes 884744 | tf_op jit(solution)/shard_map/ppermute | solution.py:66
  683.9 4.0 collective-permute-start.46
  686.4 93.8 %collective-permute-start.56 = (bf16[4,4,48,768]{3,2,1,0:T(8,128)(2,1)}, bf16[4,4,48,768]{3,2,1,0:T(8,128)(2,1)}, u32[]{:S(2)}, u32[]{:S(2)}) collective-permute-start(bf16[4,4,48,768]{3,2,1,0:T(8,128)(2,1)} %broadcast_add_fusion), channel_id=1, source_target_pairs={{1,0},{3,2},{5,4},{7,6},{9,8},{11,10},{13,12},{15,14},{17,16},{19,... | collective-permute-start | bytes 3538952 | tf_op jit(solution)/shard_map/ppermute | solution.py:78
  687.9 12.0 %collective-permute-start.47 = (f32[1,768]{1,0:T(1,128)S(1)}, f32[1,768]{1,0:T(1,128)S(1)}, u32[]{:S(2)}, u32[]{:S(2)}) collective-permute-start(f32[1,768]{1,0:T(1,128)S(1)} %add.465), channel_id=1, source_target_pairs={{0,8},{1,9},{2,10},{3,11},{4,12},{5,13},{6,14},{7,15},{8,0},{9,1},... | collective-permute-start | bytes 9224 | tf_op jit(solution)/shard_map/ppermute | solution.py:66
  700.0 4.7 collective-permute-start.48
  701.0 25.8 %collective-permute-start.52 = (bf16[2,192,768]{2,1,0:T(8,128)(2,1)}, bf16[2,192,768]{2,1,0:T(8,128)(2,1)}, u32[]{:S(2)}, u32[]{:S(2)}) collective-permute-start(bf16[2,192,768]{2,1,0:T(8,128)(2,1)} %maximum_select_fusion.14), channel_id=1, source_target_pairs={{0,8},{1,9},{2,10},{3,11},{4,12},{5,13},{6,14},{7,15},{8,0},{9,1},... | collective-permute-start | bytes 1769480 | tf_op jit(solution)/shard_map/ppermute | solution.py:66
  704.7 13.7 %collective-permute-start.49 = (f32[9,768]{1,0:T(8,128)S(1)}, f32[9,768]{1,0:T(8,128)S(1)}, u32[]{:S(2)}, u32[]{:S(2)}) collective-permute-start(f32[9,768]{1,0:T(8,128)S(1)} %pad_maximum_fusion.10), channel_id=1, source_target_pairs={{0,1},{1,0},{2,3},{3,2},{4,5},{5,4},{6,7},{7,6},{8,9},{9,8},{10,11... | collective-permute-start | bytes 82952 | tf_op jit(solution)/shard_map/ppermute | solution.py:70
  706.6 59.9 %collective-permute-start.50 = (bf16[1008,768]{1,0:T(8,128)(2,1)S(1)}, bf16[1008,768]{1,0:T(8,128)(2,1)}, u32[]{:S(2)}, u32[]{:S(2)}) collective-permute-start(bf16[1008,768]{1,0:T(8,128)(2,1)S(1)} %get-tuple-element.562), channel_id=1, source_target_pairs={{0,1},{1,0},{2,3},{3,2},{4,5},{5,4},{6,7},{7,6},{8,9},{9,8},{10,11... | collective-permute-start | bytes 4644872 | tf_op jit(solution)/shard_map/ppermute | solution.py:70
  734.3 3.0 collective-permute-start.58
  736.9 11.3 %collective-permute-start.53 = (bf16[4,2,48,768]{3,2,1,0:T(8,128)(2,1)}, bf16[4,2,48,768]{3,2,1,0:T(8,128)(2,1)S(1)}, u32[]{:S(2)}, u32[]{:S(2)}) collective-permute-start(bf16[4,2,48,768]{3,2,1,0:T(8,128)(2,1)} %get-tuple-element.461), channel_id=1, source_target_pairs={{0,2},{1,3},{2,0},{3,1},{4,6},{5,7},{6,4},{7,5},{8,10},{9,11},{10,... | collective-permute-start | bytes 1769480 | tf_op jit(solution)/shard_map/ppermute | solution.py:66
  737.4 4.4 collective-permute-start.59
  741.7 4.3 collective-permute-start.60
  746.0 5.6 collective-permute-start.61
  749.5 14.9 %collective-permute-start.54 = (bf16[4,2,48,768]{3,2,1,0:T(8,128)(2,1)}, bf16[4,2,48,768]{3,2,1,0:T(8,128)(2,1)}, u32[]{:S(2)}, u32[]{:S(2)}) collective-permute-start(bf16[4,2,48,768]{3,2,1,0:T(8,128)(2,1)} %get-tuple-element.462), channel_id=1, source_target_pairs={{0,4},{1,5},{2,6},{3,7},{4,0},{5,1},{6,2},{7,3},{8,12},{9,13},{10,... | collective-permute-start | bytes 1769480 | tf_op jit(solution)/shard_map/ppermute | solution.py:66
  751.6 5.1 collective-permute-start.62
  766.4 26.4 %collective-permute-start.55 = (bf16[4,4,48,768]{3,2,1,0:T(8,128)(2,1)S(1)}, bf16[4,4,48,768]{3,2,1,0:T(8,128)(2,1)S(1)}, u32[]{:S(2)}, u32[]{:S(2)}) collective-permute-start(bf16[4,4,48,768]{3,2,1,0:T(8,128)(2,1)S(1)} %broadcast_add_fusion.1), channel_id=1, source_target_pairs={{0,1},{1,0},{2,3},{3,2},{4,5},{5,4},{6,7},{7,6},{8,9},{9,8},{10,11... | collective-permute-start | bytes 3538952 | tf_op jit(solution)/shard_map/ppermute | solution.py:70
  (72 other events, 722.3 us)
Sparse Core Ops, SparseCore 0:
  12.4 140.6 all-gather.6
  219.8 43.3 all-gather.8
  451.9 99.3 all-gather.10

commit v4 on v3

--- a/solution.py
+++ b/solution.py
@@ -799,11 +799,13 @@
     row_peak = jnp.max(logits, -1)
     row_total = jnp.sum(jnp.exp(logits - row_peak[:, None]), -1)
     goal_logit = jnp.sum(jnp.where(goal_hit, logits, 0.0), -1)
-    every_stat = lax.all_gather(jnp.stack([row_peak, row_total]), "section")
-    top_peak = jnp.max(every_stat[:, 0], 0)
-    log_total = top_peak + jnp.log(
-        jnp.sum(every_stat[:, 1] * jnp.exp(every_stat[:, 0] - top_peak), 0)
-    )
+    for bit in range(bits):
+        other_peak, other_total = swap_bit(jnp.stack([row_peak, row_total]), bit)
+        top_peak = jnp.maximum(row_peak, other_peak)
+        row_total = row_total * jnp.exp(row_peak - top_peak)
+        row_total = row_total + other_total * jnp.exp(other_peak - top_peak)
+        row_peak = top_peak
+    log_total = row_peak + jnp.log(row_total)
     grad_logits = to_low(jnp.exp(logits - log_total[:, None]) - goal_hit.astype(jnp.float32))
     grad_all = forward_mul(grad_logits, shard_low)
     def head_table_task():
@@ -929,7 +931,9 @@
     def feed_task():
         yield (None, 10, None, None)
         layout = ["matrix"] + list(range(bits - 1, 0, -1))
-        own = yield from halved(feed_half.reshape(-1, D), layout, range(1, bits))
+        own = yield from halved(feed_half.reshape(-1, D), layout, range(1, 3))
+        found["feed_two"] = own
+        own = yield from halved(own, layout[:-2], range(3, bits))
         own = own.reshape(2, -1, D)
         found["feed_square"] = squares(own)
         found["feed"] = own
@@ -940,7 +944,7 @@
     starts = [0, vocab_rows - block_rows]
 
     def table_task():
-        yield from until(found, ["rows"])
+        yield from until(found, ["rows", "feed_two"])
         own_start, other_start = jnp.where(is_encoder, jnp.array(starts), jnp.array(starts[::-1]))
 
         def product(start):
@@ -988,28 +992,18 @@
         other = yield ("dp", -30, swap_half, tied(terms, found["feed"]))
         return terms, other
 
-    def small_task():
-        yield (None, 25, None, None)
-
-        def of_buckets(values):
-            return jnp.einsum(
-                "hqk,qkb->bh", values, onehot.astype(jnp.float32), precision=HIGH
-            ).reshape(1, -1)
-
-        bias_grad = yield ("core", 6, of_buckets, score_grad)
-        rows = [jnp.where(half == layer, bias_grad, 0.0) for layer in range(2)]
-        rows = jnp.concatenate(rows, 1).reshape(-1, D)
-        found["small"] = yield from summed(jnp.concatenate([gain_part, rows]))
-
     def norm_task():
-        yield from until(
-            found, ["self_square", "cross_square", "small", "feed_square", "table_square"]
-        )
+        yield from until(found, ["self_square", "cross_square", "feed_square", "table_square"])
+        bias_grad = jnp.einsum(
+            "hqk,qkb->bh", score_grad, onehot.astype(jnp.float32), precision=HIGH
+        ).reshape(1, -1)
+        bias_rows = [jnp.where(half == layer, bias_grad, 0.0) for layer in range(2)]
         square_sum = found["self_square"] + is_decoder.astype(jnp.float32) * found["cross_square"]
         square_sum = square_sum + found["feed_square"] + found["table_square"]
         sums = jnp.stack([loss_part, count_part, square_sum])
-        sums = yield from summed(jnp.pad(sums, (0, D - sums.shape[0])).reshape(1, D))
-        sums = jnp.concatenate([found["small"], sums])
+        sums = jnp.pad(sums, (0, D - sums.shape[0])).reshape(1, D)
+        bias_rows = jnp.concatenate(bias_rows, 1).reshape(-1, D)
+        sums = yield from summed(jnp.concatenate([gain_part, bias_rows, sums]))
         return sums, (yield ("dp", -5, swap_half, sums))
 
     def direction_task():
@@ -1025,14 +1019,13 @@
         return sums, (yield ("dp", -5, swap_half, sums))
 
     tasks = [rows_task(), self_task(), cross_task(), table_task(), feed_task()]
-    tasks += [small_task(), norm_task(), direction_task()]
+    tasks += [norm_task(), direction_task()]
     results = interleave(tasks, embed_low)
     self_terms, cross_terms, table_grad, feed_both = results[1:5]
-    norm_sums, directions = results[6:]
+    norm_sums, directions = results[5:]
     norm_sums = norm_sums[0] + norm_sums[1]
     small, sums = norm_sums[:-1], norm_sums[-1]
     directions = (directions[0] + directions[1])[0, : 3 * MATRICES]
-    table_grad = to_full(table_grad)
     gain_full = small[: gain_rows.shape[0]]
     bias_full = small[gain_rows.shape[0] :].reshape(position_bias.shape)
     small_square = squares(gain_full) + squares(bias_full)

time: 819 us -> 785 us (0.958)
  waiting for transfers between devices: 357 us -> 322 us
  blocking collectives: 20.1 us -> 0 us
  matrix products: 77.5 us -> 87.8 us
  local copies, waits for them, and re-layouts: 65.3 us -> 74.2 us
    ppermute x51, waiting for transfers between devices: 237 us -> 201 us  [swap_bit(): return lax.ppermute(value, ('section', 'dp'), pairs)]
    all_gather x1 -> x0, blocking collectives: 20.1 us -> none  [local(): every_stat = lax.all_gather(jnp.stack([row_peak, row_total]), 'section')]
    dot_general x5, matrix products: 32.7 us -> 42.4 us  [forward_mul(): return jnp.dot(left, right, preferred_element_type=jnp.float32)]
    another operation x17 -> x18, local copies, waits for them, and re-layouts: 18 us -> 18 us
  transfers between devices with their start and end apart: 66 -> 66, of which waited for: 33 -> 36; matrix products, arithmetic and copies ran while one was open for 25% -> 28% of each run, Pallas kernels for 5% -> 6%
where the time goes in v4:
time: 785 us; the launch traced here: 776 us
  waiting for transfers between devices  322 us (41%)
  other arithmetic  112 us (14%)
  starting transfers between devices  104 us (13%)
  matrix products  87.8 us (11%)
  local copies, waits for them, and re-layouts  74.2 us (9%)
  Pallas kernels  43.9 us (6%)
  between operations  30.7 us (4%)
    ppermute x51, waiting for transfers between devices, swap_bit(): return lax.ppermute(value, ('section', 'dp'), pairs)  201 us
    ppermute x51, starting transfers between devices, swap_bit(): return lax.ppermute(value, ('section', 'dp'), pairs)  59.7 us
    all_gather x1, waiting for transfers between devices, local(): all_rows = lax.all_gather(head_low, 'section', axis=0, tiled=True)  42.8 us
    dot_general x5, matrix products, forward_mul(): return jnp.dot(left, right, preferred_element_type=jnp.float32)  42.4 us
    ppermute x3, waiting for transfers between devices, to_encoder(): return lax.ppermute(value, 'dp', [(1, 0)])  36.2 us
    ppermute x7, starting transfers between devices, swap_half(): return lax.ppermute(value, 'dp', [(0, 1), (1, 0)])  33.2 us
    convert_element_type x21, other arithmetic, to_low(): return values.astype(jnp.bfloat16)  32.7 us
    ppermute x7, waiting for transfers between devices, swap_half(): return lax.ppermute(value, 'dp', [(0, 1), (1, 0)])  30.9 us
  transfers between devices with their start and end apart: 66, of which 36 were waited for; matrix products, arithmetic and copies ran while one was open for 28% of the time, Pallas kernels for 6%

profile of v4, /device:TPU:0, one launch (start us, length us, event | category | flops | bytes accessed | tf_op | source)
XLA Modules:
  0.0 775.5 jit_solution(17456931940442702641)
XLA Ops:
  13.0 3.0 collective-permute-start
  26.6 3.1 collective-permute-start.4
  29.7 3.1 convert_element_type.429
  33.1 8.7 %fusion.14 = bf16[2048,768]{1,0:T(8,128)(2,1)} fusion(bf16[2008,768]{1,0:T(8,128)(2,1)S(1)} %convert_element_type.429, s32[2048]{0:T(1024)S(1)} %bitcast.460), kind=kOutput, calls=%fused_computation.33 | convolution fusion | flops 6322307072 | bytes 6238208 | tf_op jit(solution)/shard_map/dot_general | solution.py:192
  44.1 3.7 collective-permute-done.5
  47.8 20.2 %fusion.20 = bf16[2048,768]{1,0:T(8,128)(2,1)S(1)} fusion(bf16[2048,768]{1,0:T(8,128)(2,1)} %collective-permute-done.5, bf16[2008,768]{1,0:T(8,128)(2,1)} %copy-done.18, s32[2048]{0:T(1024)S(1)} %bitcast.459), kind=kOutput, calls=%fused_computation.51 | convolution fusion | flops 6323879936 | bytes 9383936 | tf_op jit(solution)/shard_map/dot_general | solution.py:192
  74.5 3.3 copy.89
  80.0 26.5 %collective-permute-done.6 = bf16[512,768]{1,0:T(8,128)(2,1)} collective-permute-done((bf16[512,768]{1,0:T(8,128)(2,1)}, bf16[512,768]{1,0:T(8,128)(2,1)}, u32[]{:S(2)}, u32[]{:S(2)}) %collective-permute-start.6) | collective-permute-done | bytes 786464 | tf_op jit(solution)/shard_map/ppermute | solution.py:66
  111.5 3.0 collective-permute-start.10
  115.3 21.0 %collective-permute-done.7 = bf16[256,768]{1,0:T(8,128)(2,1)} collective-permute-done((bf16[256,768]{1,0:T(8,128)(2,1)S(1)}, bf16[256,768]{1,0:T(8,128)(2,1)}, u32[]{:S(2)}, u32[]{:S(2)}) %collective-permute-start.7) | collective-permute-done | bytes 393248 | tf_op jit(solution)/shard_map/ppermute | solution.py:66
  140.1 3.0 collective-permute-done.10
  144.9 4.1 collective-permute-done.11
  149.2 3.9 all-gather.5.cloned.1.call-done.refs_2_
  153.1 6.1 attention_forward.3
  163.1 8.8 %conditional.5 = ((f32[256,768]{1,0:T(8,128)}, bf16[256,768]{1,0:T(8,128)(2,1)}, f32[256,3072]{1,0:T(8,128)S(1)})) conditional(s32[]{:T(128)} %convert_element_type.427, () %tuple.148, (f32[7,768]{1,0:T(8,128)}, f32[256,768]{1,0:T(8,128)}, f32[1,768]{1,0:T(1,128)S(1)}, bf16[4,3072,768]{2,1,0:T(8,128)(2,1)}) %tuple.149), branch_computations={%region_0.1_spmd, %region_1.2_spmd} | conditional | bytes 4325418 | solution.py:751
  163.8 8.0 %feed_forward.2 = (f32[256,768]{1,0:T(8,128)}, bf16[256,768]{1,0:T(8,128)(2,1)}, f32[256,3072]{1,0:T(8,128)S(1)}) custom-call(f32[256,768]{1,0:T(8,128)} %get-tuple-element.124.rows_ref, f32[1,768]{1,0:T(1,128)S(1)} %get-tuple-element.125.gain_ref, f32[1,768]{1,0:T(1,128)S(1)} %slice.108.last_ref, bf16[4,3072,768]{2,1,0:T(8,128)(2,1)} %get-tuple-element.127.in_ref.out_ref, ...), custom_call_target="tpu_custom_call" | custom-call | tf_op jit(solution)/shard_map/cond/branch_1_fun/feed_forward/pallas_call | solution.py:276
  171.8 5.8 collective-permute-done.13
  181.9 3.5 collective-permute-start.14
  187.0 6.5 collective-permute-done.14
  194.2 6.3 conditional.6
  200.5 9.3 %collective-permute-done.15 = bf16[2,192,768]{2,1,0:T(8,128)(2,1)} collective-permute-done((bf16[2,192,768]{2,1,0:T(8,128)(2,1)}, bf16[2,192,768]{2,1,0:T(8,128)(2,1)}, u32[]{:S(2)}, u32[]{:S(2)}) %collective-permute-start.15) | collective-permute-done | bytes 589856 | tf_op jit(solution)/shard_map/ppermute | solution.py:66
  211.8 6.7 collective-permute-done.16
  220.1 42.8 %all-gather.7.cloned.1.call-done = bf16[2048,768]{1,0:T(8,128)(2,1)} async-done(((bf16[128,768]{1,0:T(8,128)(2,1)}), bf16[2048,768]{1,0:T(8,128)(2,1)}) %all-gather.7.cloned.1.call-update) | async-done | bytes 3145744 | tf_op jit(solution)/shard_map/all_gather | solution.py:796
  262.8 9.6 %fusion.105 = (f32[2048]{0:T(1024)S(1)}, f32[2048,2008]{0,1:T(8,128)S(1)}) fusion(bf16[2048,768]{1,0:T(8,128)(2,1)} %all-gather.7.cloned.1.call-done, bf16[2008,768]{1,0:T(8,128)(2,1)} %copy-done.18), kind=kOutput, calls=%fused_computation.306 | convolution fusion | flops 6320732160 | bytes 22687744 | tf_op jit(solution)/shard_map/nd,vd->nv/dot_general | solution.py:797
  272.5 5.6 select_reduce_fusion
  280.0 3.2 collective-permute-done.18
  291.9 4.2 subtract_convert_fusion
  296.2 7.4 fusion.106
  304.1 3.1 collective-permute-done.21
  309.5 8.5 %fusion.107 = f32[2008,768]{1,0:T(8,128)} fusion(bf16[2048,2008]{0,1:T(8,128)(2,1)S(1)} %subtract_convert_fusion, bf16[2048,768]{1,0:T(8,128)(2,1)S(1)} %copy-done.74), kind=kOutput, calls=%fused_computation.308 | convolution fusion | flops 6316621824 | bytes 17539072 | tf_op jit(solution)/shard_map/dot_general | solution.py:215
  318.0 9.3 %collective-permute-done.22 = bf16[512,768]{1,0:T(8,128)(2,1)S(1)} collective-permute-done((bf16[512,768]{1,0:T(8,128)(2,1)S(1)}, bf16[512,768]{1,0:T(8,128)(2,1)S(1)}, u32[]{:S(2)}, u32[]{:S(2)}) %collective-permute-start.22) | collective-permute-done | bytes 786464 | tf_op jit(solution)/shard_map/ppermute | solution.py:66
  329.7 8.6 %collective-permute-done.23 = bf16[256,768]{1,0:T(8,128)(2,1)S(1)} collective-permute-done((bf16[256,768]{1,0:T(8,128)(2,1)S(1)}, bf16[256,768]{1,0:T(8,128)(2,1)S(1)}, u32[]{:S(2)}, u32[]{:S(2)}) %collective-permute-start.23) | collective-permute-done | bytes 393248 | tf_op jit(solution)/shard_map/ppermute | solution.py:66
  340.5 8.5 %collective-permute-done.24 = bf16[128,768]{1,0:T(8,128)(2,1)S(1)} collective-permute-done((bf16[128,768]{1,0:T(8,128)(2,1)S(1)}, bf16[128,768]{1,0:T(8,128)(2,1)S(1)}, u32[]{:S(2)}, u32[]{:S(2)}) %collective-permute-start.24) | collective-permute-done | bytes 196640 | tf_op jit(solution)/shard_map/ppermute | solution.py:66
  349.0 3.4 collective-permute-start.25
  355.8 10.3 %conditional.7 = (bf16[256,768]{1,0:T(8,128)(2,1)}, f32[256,768]{1,0:T(8,128)}, bf16[2,1536,768]{2,1,0:T(8,128)(2,1)}, bf16[2,1536,768]{2,1,0:T(8,128)(2,1)}, bf...) conditional(s32[]{:T(128)} %convert_element_type.428, () %tuple.140, ...), branch_computations={%region_6.7_spmd, %region_7.8_spmd} | conditional | flops 2309 | bytes 15344714 | solution.py:844
  367.4 29.5 %collective-permute-done.26 = bf16[256,768]{1,0:T(8,128)(2,1)S(1)} collective-permute-done((bf16[256,768]{1,0:T(8,128)(2,1)}, bf16[256,768]{1,0:T(8,128)(2,1)S(1)}, u32[]{:S(2)}, u32[]{:S(2)}) %collective-permute-start.26) | collective-permute-done | bytes 393248 | tf_op jit(solution)/shard_map/ppermute | solution.py:78
  402.8 19.2 %conditional.8 = (f32[256,768]{1,0:T(8,128)}, f32[2,768]{1,0:T(2,128)S(1)}, f32[12,128,128]{2,1,0:T(8,128)}, bf16[1536,768]{1,0:T(8,128)(2,1)}, bf16[1536,768]{1...) conditional(s32[]{:T(128)} %convert_element_type.427, (f32[256,768]{1,0:T(8,128)}, ...), branch_computations={%region_8.9_spmd, %region_9.10_spmd} | conditional | flops 198149 | bytes 5535892 | solution.py:886
  403.7 14.2 %feed_backward.3 = (f32[256,768]{1,0:T(8,128)}, bf16[2,1536,768]{2,1,0:T(8,128)(2,1)}, bf16[2,1536,768]{2,1,0:T(8,128)(2,1)}, f32[2,768]{1,0:T(2,128)}) custom-call(s32[1]{0:T(128)} %bitcast.2.mine_ref, bf16[256,768]{1,0:T(8,128)(2,1)} %get-tuple-element.185.upstream_ref, f32[256,768]{1,0:T(8,128)} %get-tuple-element.186.after_ref, ...), custom_call_target="tpu_custom_call" | custom-call | tf_op jit(solution)/shard_map/cond/branch_1_fun/feed_backward/pallas_call | solution.py:365
  426.5 15.9 %conditional.9 = (bf16[256,768]{1,0:T(8,128)(2,1)}, f32[7,768]{1,0:T(8,128)S(1)}, f32[12,128,128]{2,1,0:T(8,128)}, bf16[1536,768]{1,0:T(8,128)(2,1)}, bf16[1536,768]{1,0:T(8,128)(2,1)}) conditional(s32[]{:T(128)} %convert_element_type.427, (f32[256,768]{1,0:T(8,128)}, f32[2,768]{1,0:T(2,128)S(1)}, f32[3,768]{1,0:T(4,128)S(1)}, ...), branch_computations={%region_10.11_spmd, %region_11.12_spmd} | conditional | flops 207360 | bytes 1219712 | solution.py:911
  426.5 15.6 %attention_backward.5 = (bf16[256,768]{1,0:T(8,128)(2,1)}, bf16[1536,768]{1,0:T(8,128)(2,1)}, bf16[1536,768]{1,0:T(8,128)(2,1)}, f32[1,768]{1,0:T(1,128)S(1)}, f32[12,128,128]{2,1,0:T(8,128)}) custom-call(s32[1]{0:T(128)} %bitcast.3.mine_ref, f32[256,768]{1,0:T(8,128)} %get-tuple-element.202.refs_0_, f32[256,768]{1,0:T(8,128)S(1)} %get-tuple-element.203.refs_1_, ...), custom_call_target="tpu_custom_call" | custom-call | tf_op jit(solution)/shard_map/cond/branch_1_fun/attention_backward/pallas_call | solution.py:559
  457.3 4.9 add_convert_fusion
  468.6 3.1 maximum_select_fusion
  477.4 3.1 broadcast_select_fusion.3
  485.7 3.0 add_convert_fusion.1
  491.3 47.0 %collective-permute-done.41 = bf16[1536,768]{1,0:T(8,128)(2,1)} collective-permute-done((bf16[1536,768]{1,0:T(8,128)(2,1)}, bf16[1536,768]{1,0:T(8,128)(2,1)}, u32[]{:S(2)}, u32[]{:S(2)}) %collective-permute-start.41) | collective-permute-done | bytes 2359328 | tf_op jit(solution)/shard_map/ppermute | solution.py:66
  549.6 13.7 %collective-permute-done.33 = bf16[768,768]{1,0:T(8,128)(2,1)} collective-permute-done((bf16[768,768]{1,0:T(8,128)(2,1)}, bf16[768,768]{1,0:T(8,128)(2,1)}, u32[]{:S(2)}, u32[]{:S(2)}) %collective-permute-start.33) | collective-permute-done | bytes 1179680 | tf_op jit(solution)/shard_map/ppermute | solution.py:66
  567.3 3.9 collective-permute-done.42
  577.3 11.5 %add_convert_fusion.4 = bf16[1008,768]{1,0:T(8,128)(2,1)} fusion(f32[2008,768]{1,0:T(8,128)} %fusion.107, s32[]{:T(128)S(6)} %select_n.589, bf16[4096,768]{1,0:T(8,128)(2,1)} %all-gather.9.cloned.1.call-done, s32[4096]{0:T(1024)S(1)} %bitcast.453, s32[1008]{0:T(1024)S(1)} %copy-done.68), kind=kOutput, calls=%fused_computation.40 | convolution fusion | flops 6347464704 | bytes 10956740 | tf_op jit(solution)/shard_map/dot_general | solution.py:207
  588.9 18.5 %collective-permute-start.44 = (bf16[1008,768]{1,0:T(8,128)(2,1)}, bf16[1008,768]{1,0:T(8,128)(2,1)}, u32[]{:S(2)}, u32[]{:S(2)}) collective-permute-start(bf16[1008,768]{1,0:T(8,128)(2,1)} %add_convert_fusion.4), channel_id=1, source_target_pairs={{0,1},{1,0},{2,3},{3,2},{4,5},{5,4},{6,7},{7,6},{8,9},{9,8},{10,11... | collective-permute-start | bytes 4644872 | tf_op jit(solution)/shard_map/ppermute | solution.py:70
  611.5 8.1 %add_convert_fusion.5 = bf16[1008,768]{1,0:T(8,128)(2,1)} fusion(f32[2008,768]{1,0:T(8,128)S(1)} %bitcast.468, s32[]{:T(128)S(6)} %select_n.588, bf16[4096,768]{1,0:T(8,128)(2,1)S(1)} %bitcast.466, s32[4096]{0:T(1024)S(1)} %bitcast.454, s32[1008]{0:T(1024)S(1)} %copy-done.67), kind=kOutput, calls=%fused_computation.41 | convolution fusion | flops 6347464704 | bytes 10956740 | tf_op jit(solution)/shard_map/dot_general | solution.py:207
  627.2 8.6 %collective-permute-start.57 = (bf16[2,192,768]{2,1,0:T(8,128)(2,1)}, bf16[2,192,768]{2,1,0:T(8,128)(2,1)}, u32[]{:S(2)}, u32[]{:S(2)}) collective-permute-start(bf16[2,192,768]{2,1,0:T(8,128)(2,1)} %bitcast.167), channel_id=1, source_target_pairs={{0,1},{1,0},{2,3},{3,2},{4,5},{5,4},{6,7},{7,6},{8,9},{9,8},{10,11... | collective-permute-start | bytes 1769480 | tf_op jit(solution)/shard_map/ppermute | solution.py:70
  638.0 4.5 collective-permute-done.44
  642.5 3.7 multiply_reduce_fusion
  647.8 3.0 collective-permute-start.51
  655.8 3.2 fusion.41
  659.0 5.9 collective-permute-done.51
  673.9 12.1 %collective-permute-done.49 = f32[9,768]{1,0:T(8,128)S(1)} collective-permute-done((f32[9,768]{1,0:T(8,128)S(1)}, f32[9,768]{1,0:T(8,128)S(1)}, u32[]{:S(2)}, u32[]{:S(2)}) %collective-permute-start.49) | collective-permute-done | bytes 27680 | tf_op jit(solution)/shard_map/ppermute | solution.py:70
  689.9 4.5 multiply_subtract_fusion.1
  697.8 3.4 multiply_reduce_fusion.3
  705.5 3.7 multiply_subtract_fusion.2
  709.6 3.2 collective-permute-done.60
  722.3 7.7 collective-permute-done.54
  734.7 11.1 %multiply_subtract_fusion = (f32[2008,768]{1,0:T(8,128)}, f32[2008,768]{1,0:T(8,128)}, f32[2008,768]{1,0:T(8,128)}) fusion(f32[2008,768]{1,0:T(8,128)S(1)} %bitcast.352, f32[]{:T(128)S(6)} %div.101, bf16[1000,768]{1,0:T(8,128)(2,1)S(1)} %slice_select_fusion, bf16[1008,768]{1,0:T(8,128)(2,1)S(1)} %broadcast_select_fusion, f32[2008,768]{1,0:T(8,128)} %param.42, ...), kind=kLoop, calls=%fused_computation.25 | loop fusion | flops 30842880 | bytes 40095748 | tf_op jit(solution)/shard_map/sub | solution.py:584
  745.8 12.7 %collective-permute-done.55 = bf16[4,4,48,768]{3,2,1,0:T(8,128)(2,1)S(1)} collective-permute-done((bf16[4,4,48,768]{3,2,1,0:T(8,128)(2,1)S(1)}, bf16[4,4,48,768]{3,2,1,0:T(8,128)(2,1)S(1)}, u32[]{:S(2)}, u32[]{:S(2)}) %collective-permute-start.55) | collective-permute-done | bytes 1179680 | tf_op jit(solution)/shard_map/ppermute | solution.py:70
  (470 shorter events, 214.1 us)
Async XLA Ops:
  7.2 145.9 %all-gather.5.cloned.1.call-start = ((), (), s32[]{:S(2)}) async-start(), calls=%async_computation | async-start | bytes 20054016 | tf_op jit(solution)/shard_map/all_gather | solution.py:715
  12.3 250.5 %all-gather.7.cloned.1.call-start = ((), (), s32[]{:S(2)}) async-start(), calls=%async_computation.1 | async-start | bytes 3342336 | tf_op jit(solution)/shard_map/all_gather | solution.py:796
  13.0 4.6 collective-permute-start
  18.8 3.7 collective-permute-start.2
  22.5 4.1 collective-permute-start.3
  26.6 6.3 collective-permute-start.4
  41.8 6.0 collective-permute-start.5
  42.9 116.3 %collective-permute-start.12 = (bf16[4,2,48,768]{3,2,1,0:T(8,128)(2,1)}, bf16[4,2,48,768]{3,2,1,0:T(8,128)(2,1)}, u32[]{:S(2)}, u32[]{:S(2)}) collective-permute-start(bf16[4,2,48,768]{3,2,1,0:T(8,128)(2,1)} %dynamic-slice_bitcast_fusion.10), channel_id=1, source_target_pairs={{0,2},{1,3},{2,0},{3,1},{4,6},{5,7},{6,4},{7,5},{8,10},{9,11},{10,... | collective-permute-start | bytes 1769480 | tf_op jit(solution)/shard_map/ppermute | solution.py:66
  69.2 37.3 %collective-permute-start.6 = (bf16[512,768]{1,0:T(8,128)(2,1)}, bf16[512,768]{1,0:T(8,128)(2,1)}, u32[]{:S(2)}, u32[]{:S(2)}) collective-permute-start(bf16[512,768]{1,0:T(8,128)(2,1)} %bitcast.31), channel_id=1, source_target_pairs={{0,4},{1,5},{2,6},{3,7},{4,0},{5,1},{6,2},{7,3},{8,12},{9,13},{10,... | collective-permute-start | bytes 2359304 | tf_op jit(solution)/shard_map/ppermute | solution.py:66
  72.9 37.3 %collective-permute-start.9 = (bf16[512,768]{1,0:T(8,128)(2,1)}, bf16[512,768]{1,0:T(8,128)(2,1)}, u32[]{:S(2)}, u32[]{:S(2)}) collective-permute-start(bf16[512,768]{1,0:T(8,128)(2,1)} %bitcast.40), channel_id=1, source_target_pairs={{0,8},{1,9},{2,10},{3,11},{4,12},{5,13},{6,14},{7,15},{8,0},{9,1},... | collective-permute-start | bytes 2359304 | tf_op jit(solution)/shard_map/ppermute | solution.py:66
  107.9 28.5 %collective-permute-start.7 = (bf16[256,768]{1,0:T(8,128)(2,1)S(1)}, bf16[256,768]{1,0:T(8,128)(2,1)}, u32[]{:S(2)}, u32[]{:S(2)}) collective-permute-start(bf16[256,768]{1,0:T(8,128)(2,1)S(1)} %bitcast.429), channel_id=1, source_target_pairs={{0,8},{1,9},{2,10},{3,11},{4,12},{5,13},{6,14},{7,15},{8,0},{9,1},... | collective-permute-start | bytes 1179656 | tf_op jit(solution)/shard_map/ppermute | solution.py:66
  111.5 31.6 %collective-permute-start.10 = (bf16[256,768]{1,0:T(8,128)(2,1)S(1)}, bf16[256,768]{1,0:T(8,128)(2,1)S(1)}, u32[]{:S(2)}, u32[]{:S(2)}) collective-permute-start(bf16[256,768]{1,0:T(8,128)(2,1)S(1)} %dynamic-slice_bitcast_fusion.11), channel_id=1, source_target_pairs={{0,16},{1,17},{2,18},{3,19},{4,20},{5,21},{6,22},{7,23},{8,24},{9,... | collective-permute-start | bytes 1179656 | tf_op jit(solution)/shard_map/ppermute | solution.py:66
  137.5 11.5 %collective-permute-start.8 = (bf16[128,768]{1,0:T(8,128)(2,1)S(1)}, bf16[128,768]{1,0:T(8,128)(2,1)S(1)}, u32[]{:S(2)}, u32[]{:S(2)}) collective-permute-start(bf16[128,768]{1,0:T(8,128)(2,1)S(1)} %dynamic-slice_bitcast_fusion.16), channel_id=1, source_target_pairs={{0,16},{1,17},{2,18},{3,19},{4,20},{5,21},{6,22},{7,23},{8,24},{9,... | collective-permute-start | bytes 589832 | tf_op jit(solution)/shard_map/ppermute | solution.py:66
  143.2 5.7 collective-permute-start.11
  161.8 15.8 %collective-permute-start.13 = (bf16[4,2,48,768]{3,2,1,0:T(8,128)(2,1)}, bf16[4,2,48,768]{3,2,1,0:T(8,128)(2,1)}, u32[]{:S(2)}, u32[]{:S(2)}) collective-permute-start(bf16[4,2,48,768]{3,2,1,0:T(8,128)(2,1)} %get-tuple-element.581), channel_id=1, source_target_pairs={{0,4},{1,5},{2,6},{3,7},{4,0},{5,1},{6,2},{7,3},{8,12},{9,13},{10,... | collective-permute-start | bytes 1769480 | tf_op jit(solution)/shard_map/ppermute | solution.py:66
  181.5 28.2 %collective-permute-start.15 = (bf16[2,192,768]{2,1,0:T(8,128)(2,1)}, bf16[2,192,768]{2,1,0:T(8,128)(2,1)}, u32[]{:S(2)}, u32[]{:S(2)}) collective-permute-start(bf16[2,192,768]{2,1,0:T(8,128)(2,1)} %get-tuple-element.579), channel_id=1, source_target_pairs={{0,16},{1,17},{2,18},{3,19},{4,20},{5,21},{6,22},{7,23},{8,24},{9,... | collective-permute-start | bytes 1769480 | tf_op jit(solution)/shard_map/ppermute | solution.py:66
  181.9 11.5 %collective-permute-start.14 = (bf16[256,768]{1,0:T(8,128)(2,1)}, bf16[256,768]{1,0:T(8,128)(2,1)S(1)}, u32[]{:S(2)}, u32[]{:S(2)}) collective-permute-start(bf16[256,768]{1,0:T(8,128)(2,1)} %get-tuple-element.367), channel_id=1, source_target_pairs={{0,1},{2,3},{4,5},{6,7},{8,9},{10,11},{12,13},{14,15},{16,17},{18,... | collective-permute-start | bytes 1179656 | tf_op jit(solution)/shard_map/ppermute | solution.py:74
  209.8 8.7 %collective-permute-start.16 = (bf16[128,768]{1,0:T(8,128)(2,1)S(1)}, bf16[128,768]{1,0:T(8,128)(2,1)S(1)}, u32[]{:S(2)}, u32[]{:S(2)}) collective-permute-start(bf16[128,768]{1,0:T(8,128)(2,1)S(1)} %slice.155), channel_id=1, source_target_pairs={{1,0},{3,2},{5,4},{7,6},{9,8},{11,10},{13,12},{15,14},{17,16},{19,... | collective-permute-start | bytes 589832 | tf_op jit(solution)/shard_map/ppermute | solution.py:78
  219.3 356.6 %all-gather.9.cloned.1.call-start = ((), (), s32[]{:S(2)}) async-start(), calls=%async_computation.2 | async-start | bytes 6684672 | tf_op jit(solution)/shard_map/all_gather | solution.py:928
  278.1 1.2 collective-permute-start.17
  279.4 3.8 collective-permute-start.18
  283.3 3.8 collective-permute-start.19
  287.2 4.7 collective-permute-start.20
  303.7 3.5 collective-permute-start.21
  307.7 19.6 %collective-permute-start.22 = (bf16[512,768]{1,0:T(8,128)(2,1)S(1)}, bf16[512,768]{1,0:T(8,128)(2,1)S(1)}, u32[]{:S(2)}, u32[]{:S(2)}) collective-permute-start(bf16[512,768]{1,0:T(8,128)(2,1)S(1)} %bitcast.418), channel_id=1, source_target_pairs={{0,4},{1,5},{2,6},{3,7},{4,0},{5,1},{6,2},{7,3},{8,12},{9,13},{10,... | collective-permute-start | bytes 2359304 | tf_op jit(solution)/shard_map/ppermute | solution.py:66
  327.7 10.5 %collective-permute-start.23 = (bf16[256,768]{1,0:T(8,128)(2,1)S(1)}, bf16[256,768]{1,0:T(8,128)(2,1)S(1)}, u32[]{:S(2)}, u32[]{:S(2)}) collective-permute-start(bf16[256,768]{1,0:T(8,128)(2,1)S(1)} %bitcast.430), channel_id=1, source_target_pairs={{0,8},{1,9},{2,10},{3,11},{4,12},{5,13},{6,14},{7,15},{8,0},{9,1},... | collective-permute-start | bytes 1179656 | tf_op jit(solution)/shard_map/ppermute | solution.py:66
  338.4 10.5 %collective-permute-start.24 = (bf16[128,768]{1,0:T(8,128)(2,1)S(1)}, bf16[128,768]{1,0:T(8,128)(2,1)S(1)}, u32[]{:S(2)}, u32[]{:S(2)}) collective-permute-start(bf16[128,768]{1,0:T(8,128)(2,1)S(1)} %dynamic-slice_bitcast_fusion.14), channel_id=1, source_target_pairs={{0,16},{1,17},{2,18},{3,19},{4,20},{5,21},{6,22},{7,23},{8,24},{9,... | collective-permute-start | bytes 589832 | tf_op jit(solution)/shard_map/ppermute | solution.py:66
  349.0 6.6 collective-permute-start.25
  355.7 41.2 %collective-permute-start.27 = (bf16[2,2,192,768]{3,2,1,0:T(8,128)(2,1)}, bf16[2,2,192,768]{3,2,1,0:T(8,128)(2,1)}, u32[]{:S(2)}, u32[]{:S(2)}) collective-permute-start(bf16[2,2,192,768]{3,2,1,0:T(8,128)(2,1)} %maximum_select_fusion.4), channel_id=1, source_target_pairs={{0,8},{1,9},{2,10},{3,11},{4,12},{5,13},{6,14},{7,15},{8,0},{9,1},... | collective-permute-start | bytes 3538952 | tf_op jit(solution)/shard_map/ppermute | solution.py:66
  366.1 30.8 %collective-permute-start.26 = (bf16[256,768]{1,0:T(8,128)(2,1)}, bf16[256,768]{1,0:T(8,128)(2,1)S(1)}, u32[]{:S(2)}, u32[]{:S(2)}) collective-permute-start(bf16[256,768]{1,0:T(8,128)(2,1)} %get-tuple-element.385), channel_id=1, source_target_pairs={{1,0},{3,2},{5,4},{7,6},{9,8},{11,10},{13,12},{15,14},{17,16},{19,... | collective-permute-start | bytes 1179656 | tf_op jit(solution)/shard_map/ppermute | solution.py:78
  401.1 20.9 %collective-permute-start.29 = (bf16[768,768]{1,0:T(8,128)(2,1)}, bf16[768,768]{1,0:T(8,128)(2,1)}, u32[]{:S(2)}, u32[]{:S(2)}) collective-permute-start(bf16[768,768]{1,0:T(8,128)(2,1)} %dynamic-slice_bitcast_fusion.1), channel_id=1, source_target_pairs={{1,5},{3,7},{5,1},{7,3},{9,13},{11,15},{13,9},{15,11},{17,21},{19,... | collective-permute-start | bytes 3538952 | tf_op jit(solution)/shard_map/ppermute | solution.py:66
  422.0 20.5 %collective-permute-start.31 = (bf16[2,1536,768]{2,1,0:T(8,128)(2,1)}, bf16[2,1536,768]{2,1,0:T(8,128)(2,1)}, u32[]{:S(2)}, u32[]{:S(2)}) collective-permute-start(bf16[2,1536,768]{2,1,0:T(8,128)(2,1)} %get-tuple-element.424), channel_id=1, source_target_pairs={{0,2},{1,3},{2,0},{3,1},{4,6},{5,7},{6,4},{7,5},{8,10},{9,11},{10,... | collective-permute-start | bytes 14155784 | tf_op jit(solution)/shard_map/ppermute | solution.py:66
  424.9 17.6 %collective-permute-start.30 = (bf16[384,768]{1,0:T(8,128)(2,1)}, bf16[384,768]{1,0:T(8,128)(2,1)}, u32[]{:S(2)}, u32[]{:S(2)}) collective-permute-start(bf16[384,768]{1,0:T(8,128)(2,1)} %bitcast.94), channel_id=1, source_target_pairs={{1,9},{3,11},{5,13},{7,15},{9,1},{11,3},{13,5},{15,7},{17,25},{19,... | collective-permute-start | bytes 1769480 | tf_op jit(solution)/shard_map/ppermute | solution.py:66
  456.1 8.4 %collective-permute-start.35 = (bf16[192,768]{1,0:T(8,128)(2,1)S(1)}, bf16[192,768]{1,0:T(8,128)(2,1)S(1)}, u32[]{:S(2)}, u32[]{:S(2)}) collective-permute-start(bf16[192,768]{1,0:T(8,128)(2,1)S(1)} %dynamic-slice_bitcast_fusion.13), channel_id=1, source_target_pairs={{1,17},{3,19},{5,21},{7,23},{9,25},{11,27},{13,29},{15,31},{17,1},... | collective-permute-start | bytes 884744 | tf_op jit(solution)/shard_map/ppermute | solution.py:66
  456.8 28.9 %collective-permute-start.32 = (bf16[1536,768]{1,0:T(8,128)(2,1)}, bf16[1536,768]{1,0:T(8,128)(2,1)}, u32[]{:S(2)}, u32[]{:S(2)}) collective-permute-start(bf16[1536,768]{1,0:T(8,128)(2,1)} %get-tuple-element.426), channel_id=1, source_target_pairs={{0,2},{1,3},{2,0},{3,1},{4,6},{5,7},{6,4},{7,5},{8,10},{9,11},{10,... | collective-permute-start | bytes 7077896 | tf_op jit(solution)/shard_map/ppermute | solution.py:66
  464.0 74.4 %collective-permute-start.41 = (bf16[1536,768]{1,0:T(8,128)(2,1)}, bf16[1536,768]{1,0:T(8,128)(2,1)}, u32[]{:S(2)}, u32[]{:S(2)}) collective-permute-start(bf16[1536,768]{1,0:T(8,128)(2,1)} %bitcast.134), channel_id=1, source_target_pairs={{0,4},{1,5},{2,6},{3,7},{4,0},{5,1},{6,2},{7,3},{8,12},{9,13},{10,... | collective-permute-start | bytes 7077896 | tf_op jit(solution)/shard_map/ppermute | solution.py:66
  465.3 6.4 collective-permute-start.36
  472.7 12.3 %collective-permute-start.37 = (bf16[2,192,768]{2,1,0:T(8,128)(2,1)}, bf16[2,192,768]{2,1,0:T(8,128)(2,1)S(1)}, u32[]{:S(2)}, u32[]{:S(2)}) collective-permute-start(bf16[2,192,768]{2,1,0:T(8,128)(2,1)} %maximum_select_fusion.12), channel_id=1, source_target_pairs={{1,9},{3,11},{5,13},{7,15},{9,1},{11,3},{13,5},{15,7},{17,25},{19,... | collective-permute-start | bytes 1769480 | tf_op jit(solution)/shard_map/ppermute | solution.py:66
  489.9 73.4 %collective-permute-start.33 = (bf16[768,768]{1,0:T(8,128)(2,1)}, bf16[768,768]{1,0:T(8,128)(2,1)}, u32[]{:S(2)}, u32[]{:S(2)}) collective-permute-start(bf16[768,768]{1,0:T(8,128)(2,1)} %dynamic-slice_bitcast_fusion), channel_id=1, source_target_pairs={{0,4},{1,5},{2,6},{3,7},{4,0},{5,1},{6,2},{7,3},{8,12},{9,13},{10,... | collective-permute-start | bytes 3538952 | tf_op jit(solution)/shard_map/ppermute | solution.py:66
  542.3 28.9 %collective-permute-start.42 = (bf16[768,768]{1,0:T(8,128)(2,1)}, bf16[768,768]{1,0:T(8,128)(2,1)}, u32[]{:S(2)}, u32[]{:S(2)}) collective-permute-start(bf16[768,768]{1,0:T(8,128)(2,1)} %bitcast.137), channel_id=1, source_target_pairs={{0,8},{1,9},{2,10},{3,11},{4,12},{5,13},{6,14},{7,15},{8,0},{9,1},... | collective-permute-start | bytes 3538952 | tf_op jit(solution)/shard_map/ppermute | solution.py:66
  548.1 27.8 %collective-permute-start.38 = (bf16[4,2,48,768]{3,2,1,0:T(8,128)(2,1)}, bf16[4,2,48,768]{3,2,1,0:T(8,128)(2,1)S(1)}, u32[]{:S(2)}, u32[]{:S(2)}) collective-permute-start(bf16[4,2,48,768]{3,2,1,0:T(8,128)(2,1)} %get-tuple-element.433), channel_id=1, source_target_pairs={{1,3},{3,1},{5,7},{7,5},{9,11},{11,9},{13,15},{15,13},{17,19},{19,... | collective-permute-start | bytes 1769480 | tf_op jit(solution)/shard_map/ppermute | solution.py:66
  565.8 41.6 %collective-permute-start.34 = (bf16[384,768]{1,0:T(8,128)(2,1)}, bf16[384,768]{1,0:T(8,128)(2,1)S(1)}, u32[]{:S(2)}, u32[]{:S(2)}) collective-permute-start(bf16[384,768]{1,0:T(8,128)(2,1)} %bitcast.104), channel_id=1, source_target_pairs={{0,8},{1,9},{2,10},{3,11},{4,12},{5,13},{6,14},{7,15},{8,0},{9,1},... | collective-permute-start | bytes 1769480 | tf_op jit(solution)/shard_map/ppermute | solution.py:66
  573.6 47.1 %collective-permute-start.43 = (bf16[384,768]{1,0:T(8,128)(2,1)}, bf16[384,768]{1,0:T(8,128)(2,1)}, u32[]{:S(2)}, u32[]{:S(2)}) collective-permute-start(bf16[384,768]{1,0:T(8,128)(2,1)} %bitcast.140), channel_id=1, source_target_pairs={{0,16},{1,17},{2,18},{3,19},{4,20},{5,21},{6,22},{7,23},{8,24},{9,... | collective-permute-start | bytes 1769480 | tf_op jit(solution)/shard_map/ppermute | solution.py:66
  576.2 31.3 %collective-permute-start.39 = (bf16[4,2,48,768]{3,2,1,0:T(8,128)(2,1)S(1)}, bf16[4,2,48,768]{3,2,1,0:T(8,128)(2,1)S(1)}, u32[]{:S(2)}, u32[]{:S(2)}) collective-permute-start(bf16[4,2,48,768]{3,2,1,0:T(8,128)(2,1)S(1)} %get-tuple-element.436), channel_id=1, source_target_pairs={{1,5},{3,7},{5,1},{7,3},{9,13},{11,15},{13,9},{15,11},{17,21},{19,... | collective-permute-start | bytes 1769480 | tf_op jit(solution)/shard_map/ppermute | solution.py:66
  588.9 53.6 %collective-permute-start.44 = (bf16[1008,768]{1,0:T(8,128)(2,1)}, bf16[1008,768]{1,0:T(8,128)(2,1)}, u32[]{:S(2)}, u32[]{:S(2)}) collective-permute-start(bf16[1008,768]{1,0:T(8,128)(2,1)} %add_convert_fusion.4), channel_id=1, source_target_pairs={{0,1},{1,0},{2,3},{3,2},{4,5},{5,4},{6,7},{7,6},{8,9},{9,8},{10,11... | collective-permute-start | bytes 4644872 | tf_op jit(solution)/shard_map/ppermute | solution.py:70
  608.5 27.3 %collective-permute-start.40 = (bf16[192,768]{1,0:T(8,128)(2,1)S(1)}, bf16[192,768]{1,0:T(8,128)(2,1)S(1)}, u32[]{:S(2)}, u32[]{:S(2)}) collective-permute-start(bf16[192,768]{1,0:T(8,128)(2,1)S(1)} %dynamic-slice_bitcast_fusion.12), channel_id=1, source_target_pairs={{0,16},{1,17},{2,18},{3,19},{4,20},{5,21},{6,22},{7,23},{8,24},{9,... | collective-permute-start | bytes 884744 | tf_op jit(solution)/shard_map/ppermute | solution.py:66
  627.2 28.6 %collective-permute-start.57 = (bf16[2,192,768]{2,1,0:T(8,128)(2,1)}, bf16[2,192,768]{2,1,0:T(8,128)(2,1)}, u32[]{:S(2)}, u32[]{:S(2)}) collective-permute-start(bf16[2,192,768]{2,1,0:T(8,128)(2,1)} %bitcast.167), channel_id=1, source_target_pairs={{0,1},{1,0},{2,3},{3,2},{4,5},{5,4},{6,7},{7,6},{8,9},{9,8},{10,11... | collective-permute-start | bytes 1769480 | tf_op jit(solution)/shard_map/ppermute | solution.py:70
  647.6 3.2 collective-permute-start.45
  647.8 17.0 %collective-permute-start.51 = (bf16[192,768]{1,0:T(8,128)(2,1)S(1)}, bf16[192,768]{1,0:T(8,128)(2,1)S(1)}, u32[]{:S(2)}, u32[]{:S(2)}) collective-permute-start(bf16[192,768]{1,0:T(8,128)(2,1)S(1)} %get-tuple-element.449), channel_id=1, source_target_pairs={{0,16},{1,17},{2,18},{3,19},{4,20},{5,21},{6,22},{7,23},{8,24},{9,... | collective-permute-start | bytes 884744 | tf_op jit(solution)/shard_map/ppermute | solution.py:66
  650.8 4.6 collective-permute-start.46
  654.0 91.8 %collective-permute-start.56 = (bf16[4,4,48,768]{3,2,1,0:T(8,128)(2,1)}, bf16[4,4,48,768]{3,2,1,0:T(8,128)(2,1)}, u32[]{:S(2)}, u32[]{:S(2)}) collective-permute-start(bf16[4,4,48,768]{3,2,1,0:T(8,128)(2,1)} %broadcast_add_fusion), channel_id=1, source_target_pairs={{1,0},{3,2},{5,4},{7,6},{9,8},{11,10},{13,12},{15,14},{17,16},{19,... | collective-permute-start | bytes 3538952 | tf_op jit(solution)/shard_map/ppermute | solution.py:78
  655.5 9.4 %collective-permute-start.47 = (f32[9,768]{1,0:T(8,128)S(1)}, f32[9,768]{1,0:T(8,128)S(1)}, u32[]{:S(2)}, u32[]{:S(2)}) collective-permute-start(f32[9,768]{1,0:T(8,128)S(1)} %add.496), channel_id=1, source_target_pairs={{0,8},{1,9},{2,10},{3,11},{4,12},{5,13},{6,14},{7,15},{8,0},{9,1},... | collective-permute-start | bytes 82952 | tf_op jit(solution)/shard_map/ppermute | solution.py:66
  664.9 5.2 collective-permute-start.48
  665.9 28.4 %collective-permute-start.52 = (bf16[2,192,768]{2,1,0:T(8,128)(2,1)}, bf16[2,192,768]{2,1,0:T(8,128)(2,1)}, u32[]{:S(2)}, u32[]{:S(2)}) collective-permute-start(bf16[2,192,768]{2,1,0:T(8,128)(2,1)} %maximum_select_fusion.14), channel_id=1, source_target_pairs={{0,8},{1,9},{2,10},{3,11},{4,12},{5,13},{6,14},{7,15},{8,0},{9,1},... | collective-permute-start | bytes 1769480 | tf_op jit(solution)/shard_map/ppermute | solution.py:66
  670.1 15.9 %collective-permute-start.49 = (f32[9,768]{1,0:T(8,128)S(1)}, f32[9,768]{1,0:T(8,128)S(1)}, u32[]{:S(2)}, u32[]{:S(2)}) collective-permute-start(f32[9,768]{1,0:T(8,128)S(1)} %add.498), channel_id=1, source_target_pairs={{0,1},{1,0},{2,3},{3,2},{4,5},{5,4},{6,7},{7,6},{8,9},{9,8},{10,11... | collective-permute-start | bytes 82952 | tf_op jit(solution)/shard_map/ppermute | solution.py:70
  673.9 58.2 %collective-permute-start.50 = (bf16[1008,768]{1,0:T(8,128)(2,1)S(1)}, bf16[1008,768]{1,0:T(8,128)(2,1)}, u32[]{:S(2)}, u32[]{:S(2)}) collective-permute-start(bf16[1008,768]{1,0:T(8,128)(2,1)S(1)} %get-tuple-element.530), channel_id=1, source_target_pairs={{0,1},{1,0},{2,3},{3,2},{4,5},{5,4},{6,7},{7,6},{8,9},{9,8},{10,11... | collective-permute-start | bytes 4644872 | tf_op jit(solution)/shard_map/ppermute | solution.py:70
  701.9 3.0 collective-permute-start.58
  704.5 9.3 %collective-permute-start.53 = (bf16[4,2,48,768]{3,2,1,0:T(8,128)(2,1)}, bf16[4,2,48,768]{3,2,1,0:T(8,128)(2,1)S(1)}, u32[]{:S(2)}, u32[]{:S(2)}) collective-permute-start(bf16[4,2,48,768]{3,2,1,0:T(8,128)(2,1)} %get-tuple-element.451), channel_id=1, source_target_pairs={{0,2},{1,3},{2,0},{3,1},{4,6},{5,7},{6,4},{7,5},{8,10},{9,11},{10,... | collective-permute-start | bytes 1769480 | tf_op jit(solution)/shard_map/ppermute | solution.py:66
  704.9 4.3 collective-permute-start.59
  709.2 3.5 collective-permute-start.60
  712.8 4.5 collective-permute-start.61
  715.1 15.0 %collective-permute-start.54 = (bf16[4,2,48,768]{3,2,1,0:T(8,128)(2,1)}, bf16[4,2,48,768]{3,2,1,0:T(8,128)(2,1)}, u32[]{:S(2)}, u32[]{:S(2)}) collective-permute-start(bf16[4,2,48,768]{3,2,1,0:T(8,128)(2,1)} %get-tuple-element.452), channel_id=1, source_target_pairs={{0,4},{1,5},{2,6},{3,7},{4,0},{5,1},{6,2},{7,3},{8,12},{9,13},{10,... | collective-permute-start | bytes 1769480 | tf_op jit(solution)/shard_map/ppermute | solution.py:66
  717.3 5.1 collective-permute-start.62
  732.0 26.5 %collective-permute-start.55 = (bf16[4,4,48,768]{3,2,1,0:T(8,128)(2,1)S(1)}, bf16[4,4,48,768]{3,2,1,0:T(8,128)(2,1)S(1)}, u32[]{:S(2)}, u32[]{:S(2)}) collective-permute-start(bf16[4,4,48,768]{3,2,1,0:T(8,128)(2,1)S(1)} %broadcast_add_fusion.1), channel_id=1, source_target_pairs={{0,1},{1,0},{2,3},{3,2},{4,5},{5,4},{6,7},{7,6},{8,9},{9,8},{10,11... | collective-permute-start | bytes 3538952 | tf_op jit(solution)/shard_map/ppermute | solution.py:70
  (82 other events, 1098.2 us)
Sparse Core Ops, SparseCore 0:
  12.4 140.6 all-gather.4
  219.4 43.3 all-gather.6
  442.6 101.2 all-gather.8

commit v5 on v4

--- a/solution.py
+++ b/solution.py
@@ -976,8 +976,7 @@
         terms = shampoo_terms(block, full, root_lefts[1], root_rights[1])
         found["cross_direction"] = squares(terms[1])
         terms = yield from to_rows(terms, (1,))
-        yield from until(found, ["feed"])
-        other = yield ("dp", -30, to_encoder, tied(terms, found["feed"]))
+        other = yield ("dp", -30, to_encoder, terms)
         return terms, other
 
     def self_task():
@@ -988,8 +987,7 @@
         terms = shampoo_terms(block, full, root_lefts[0], root_rights[0])
         found["self_direction"] = squares(terms[1])
         terms = yield from to_rows(terms)
-        yield from until(found, ["feed"])
-        other = yield ("dp", -30, swap_half, tied(terms, found["feed"]))
+        other = yield ("dp", -30, swap_half, terms)
         return terms, other
 
     def norm_task():

time: 785 us -> 856 us (1.090)
  waiting for transfers between devices: 322 us -> 412 us
    ppermute x51, waiting for transfers between devices: 201 us -> 261 us  [swap_bit(): return lax.ppermute(value, ('section', 'dp'), pairs)]
    ppermute x7, waiting for transfers between devices: 30.9 us -> 44.8 us  [swap_half(): return lax.ppermute(value, 'dp', [(0, 1), (1, 0)])]
    ppermute x3, waiting for transfers between devices: 36.2 us -> 49.9 us  [to_encoder(): return lax.ppermute(value, 'dp', [(1, 0)])]
    dot_general x5, matrix products: 42.4 us -> 32.7 us  [forward_mul(): return jnp.dot(left, right, preferred_element_type=jnp.float32)]
    select_n x21 -> x20, other arithmetic: 15.9 us -> 20.7 us  [ordered(): jnp.where(mine == 0, jnp.stack([own, other], axis), jnp.stack([other, own...]
    convert_element_type x21 -> x22, other arithmetic: 32.7 us -> 33.1 us  [to_low(): return values.astype(jnp.bfloat16)]
  transfers between devices with their start and end apart: 66 -> 66, of which waited for: 36 -> 45; matrix products, arithmetic and copies ran while one was open for 28% -> 24% of each run, Pallas kernels for 6% -> 5%
where the time goes in v5:
time: 856 us; the launch traced here: 847 us
  waiting for transfers between devices  412 us (48%)
  other arithmetic  111 us (13%)
  starting transfers between devices  101 us (12%)
  matrix products  79.4 us (9%)
  local copies, waits for them, and re-layouts  69.6 us (8%)
  Pallas kernels  43.9 us (5%)
  between operations  29.2 us (3%)
    ppermute x51, waiting for transfers between devices, swap_bit(): return lax.ppermute(value, ('section', 'dp'), pairs)  261 us
    ppermute x51, starting transfers between devices, swap_bit(): return lax.ppermute(value, ('section', 'dp'), pairs)  59 us
    ppermute x3, waiting for transfers between devices, to_encoder(): return lax.ppermute(value, 'dp', [(1, 0)])  49.9 us
    ppermute x7, waiting for transfers between devices, swap_half(): return lax.ppermute(value, 'dp', [(0, 1), (1, 0)])  44.8 us
    all_gather x1, waiting for transfers between devices, local(): all_rows = lax.all_gather(head_low, 'section', axis=0, tiled=True)  43 us
    convert_element_type x22, other arithmetic, to_low(): return values.astype(jnp.bfloat16)  33.1 us
    dot_general x5, matrix products, forward_mul(): return jnp.dot(left, right, preferred_element_type=jnp.float32)  32.7 us
    ppermute x7, starting transfers between devices, swap_half(): return lax.ppermute(value, 'dp', [(0, 1), (1, 0)])  31.1 us
  transfers between devices with their start and end apart: 66, of which 45 were waited for; matrix products, arithmetic and copies ran while one was open for 24% of the time, Pallas kernels for 5%

profile of v5, /device:TPU:0, one launch (start us, length us, event | category | flops | bytes accessed | tf_op | source)
XLA Modules:
  0.0 847.1 jit_solution(13763638037921724546)
XLA Ops:
  13.0 3.0 collective-permute-start
  26.6 3.1 collective-permute-start.4
  29.7 3.1 convert_element_type.422
  33.1 8.7 %fusion.14 = bf16[2048,768]{1,0:T(8,128)(2,1)} fusion(bf16[2008,768]{1,0:T(8,128)(2,1)S(1)} %convert_element_type.422, s32[2048]{0:T(1024)S(1)} %bitcast.458), kind=kOutput, calls=%fused_computation.33 | convolution fusion | flops 6322307072 | bytes 6238208 | tf_op jit(solution)/shard_map/dot_general | solution.py:192
  44.1 3.7 collective-permute-done.5
  47.8 10.1 %fusion.20 = bf16[2048,768]{1,0:T(8,128)(2,1)S(1)} fusion(bf16[2048,768]{1,0:T(8,128)(2,1)} %collective-permute-done.5, bf16[2008,768]{1,0:T(8,128)(2,1)} %copy-done.13, s32[2048]{0:T(1024)S(1)} %bitcast.457), kind=kOutput, calls=%fused_computation.51 | convolution fusion | flops 6323879936 | bytes 9383936 | tf_op jit(solution)/shard_map/dot_general | solution.py:192
  64.4 3.3 copy.88
  70.0 26.5 %collective-permute-done.6 = bf16[512,768]{1,0:T(8,128)(2,1)} collective-permute-done((bf16[512,768]{1,0:T(8,128)(2,1)}, bf16[512,768]{1,0:T(8,128)(2,1)}, u32[]{:S(2)}, u32[]{:S(2)}) %collective-permute-start.6) | collective-permute-done | bytes 786464 | tf_op jit(solution)/shard_map/ppermute | solution.py:66
  101.5 3.0 collective-permute-start.10
  105.3 21.0 %collective-permute-done.7 = bf16[256,768]{1,0:T(8,128)(2,1)} collective-permute-done((bf16[256,768]{1,0:T(8,128)(2,1)S(1)}, bf16[256,768]{1,0:T(8,128)(2,1)}, u32[]{:S(2)}, u32[]{:S(2)}) %collective-permute-start.7) | collective-permute-done | bytes 393248 | tf_op jit(solution)/shard_map/ppermute | solution.py:66
  130.1 3.0 collective-permute-done.10
  134.8 9.3 %collective-permute-done.11 = bf16[128,768]{1,0:T(8,128)(2,1)S(1)} collective-permute-done((bf16[128,768]{1,0:T(8,128)(2,1)S(1)}, bf16[128,768]{1,0:T(8,128)(2,1)S(1)}, u32[]{:S(2)}, u32[]{:S(2)}) %collective-permute-start.11) | collective-permute-done | bytes 196640 | tf_op jit(solution)/shard_map/ppermute | solution.py:66
  146.8 6.3 all-gather.5.cloned.1.call-done.refs_2_
  153.1 6.1 attention_forward.3
  163.0 8.8 %conditional.5 = ((f32[256,768]{1,0:T(8,128)}, bf16[256,768]{1,0:T(8,128)(2,1)}, f32[256,3072]{1,0:T(8,128)S(1)})) conditional(s32[]{:T(128)} %convert_element_type.420, () %tuple.148, (f32[7,768]{1,0:T(8,128)}, f32[256,768]{1,0:T(8,128)}, f32[1,768]{1,0:T(1,128)S(1)}, bf16[4,3072,768]{2,1,0:T(8,128)(2,1)}) %tuple.149), branch_computations={%region_0.1_spmd, %region_1.2_spmd} | conditional | bytes 4325418 | solution.py:751
  163.8 8.0 feed_forward.2
  171.8 5.8 collective-permute-done.13
  183.9 3.4 collective-permute-start.14
  188.8 6.5 collective-permute-done.14
  196.1 6.3 conditional.6
  202.4 7.5 collective-permute-done.15
  212.0 6.7 collective-permute-done.16
  220.2 43.0 %all-gather.7.cloned.1.call-done = bf16[2048,768]{1,0:T(8,128)(2,1)} async-done(((bf16[128,768]{1,0:T(8,128)(2,1)}), bf16[2048,768]{1,0:T(8,128)(2,1)}) %all-gather.7.cloned.1.call-update) | async-done | bytes 3145744 | tf_op jit(solution)/shard_map/all_gather | solution.py:796
  263.2 9.6 %fusion.105 = (f32[2048]{0:T(1024)S(1)}, f32[2048,2008]{0,1:T(8,128)S(1)}) fusion(bf16[2048,768]{1,0:T(8,128)(2,1)} %all-gather.7.cloned.1.call-done, bf16[2008,768]{1,0:T(8,128)(2,1)} %copy-done.13), kind=kOutput, calls=%fused_computation.304 | convolution fusion | flops 6320732160 | bytes 22687744 | tf_op jit(solution)/shard_map/nd,vd->nv/dot_general | solution.py:797
  272.8 5.6 select_reduce_fusion
  280.4 3.2 collective-permute-done.18
  292.3 4.2 subtract_convert_fusion
  296.5 7.4 fusion.106
  304.5 3.1 collective-permute-done.21
  309.8 8.5 %fusion.107 = f32[2008,768]{1,0:T(8,128)} fusion(bf16[2048,2008]{0,1:T(8,128)(2,1)S(1)} %subtract_convert_fusion, bf16[2048,768]{1,0:T(8,128)(2,1)S(1)} %copy-done.68), kind=kOutput, calls=%fused_computation.306 | convolution fusion | flops 6316621824 | bytes 17539072 | tf_op jit(solution)/shard_map/dot_general | solution.py:215
  318.4 9.3 %collective-permute-done.22 = bf16[512,768]{1,0:T(8,128)(2,1)S(1)} collective-permute-done((bf16[512,768]{1,0:T(8,128)(2,1)S(1)}, bf16[512,768]{1,0:T(8,128)(2,1)S(1)}, u32[]{:S(2)}, u32[]{:S(2)}) %collective-permute-start.22) | collective-permute-done | bytes 786464 | tf_op jit(solution)/shard_map/ppermute | solution.py:66
  330.0 8.6 %collective-permute-done.23 = bf16[256,768]{1,0:T(8,128)(2,1)S(1)} collective-permute-done((bf16[256,768]{1,0:T(8,128)(2,1)S(1)}, bf16[256,768]{1,0:T(8,128)(2,1)S(1)}, u32[]{:S(2)}, u32[]{:S(2)}) %collective-permute-start.23) | collective-permute-done | bytes 393248 | tf_op jit(solution)/shard_map/ppermute | solution.py:66
  340.8 8.5 %collective-permute-done.24 = bf16[128,768]{1,0:T(8,128)(2,1)S(1)} collective-permute-done((bf16[128,768]{1,0:T(8,128)(2,1)S(1)}, bf16[128,768]{1,0:T(8,128)(2,1)S(1)}, u32[]{:S(2)}, u32[]{:S(2)}) %collective-permute-start.24) | collective-permute-done | bytes 196640 | tf_op jit(solution)/shard_map/ppermute | solution.py:66
  349.4 3.4 collective-permute-start.25
  356.1 10.3 %conditional.7 = (bf16[256,768]{1,0:T(8,128)(2,1)}, f32[256,768]{1,0:T(8,128)}, bf16[2,1536,768]{2,1,0:T(8,128)(2,1)}, bf16[2,1536,768]{2,1,0:T(8,128)(2,1)}, bf...) conditional(s32[]{:T(128)} %convert_element_type.421, () %tuple.140, ...), branch_computations={%region_6.7_spmd, %region_7.8_spmd} | conditional | flops 2309 | bytes 15344714 | solution.py:844
  367.7 29.5 %collective-permute-done.26 = bf16[256,768]{1,0:T(8,128)(2,1)S(1)} collective-permute-done((bf16[256,768]{1,0:T(8,128)(2,1)}, bf16[256,768]{1,0:T(8,128)(2,1)S(1)}, u32[]{:S(2)}, u32[]{:S(2)}) %collective-permute-start.26) | collective-permute-done | bytes 393248 | tf_op jit(solution)/shard_map/ppermute | solution.py:78
  403.1 19.2 %conditional.8 = (f32[256,768]{1,0:T(8,128)}, f32[2,768]{1,0:T(2,128)S(1)}, f32[12,128,128]{2,1,0:T(8,128)}, bf16[1536,768]{1,0:T(8,128)(2,1)}, bf16[1536,768]{1...) conditional(s32[]{:T(128)} %convert_element_type.420, (f32[256,768]{1,0:T(8,128)}, ...), branch_computations={%region_8.9_spmd, %region_9.10_spmd} | conditional | flops 198149 | bytes 5535892 | solution.py:886
  404.0 14.2 %feed_backward.3 = (f32[256,768]{1,0:T(8,128)}, bf16[2,1536,768]{2,1,0:T(8,128)(2,1)}, bf16[2,1536,768]{2,1,0:T(8,128)(2,1)}, f32[2,768]{1,0:T(2,128)}) custom-call(s32[1]{0:T(128)} %bitcast.2.mine_ref, bf16[256,768]{1,0:T(8,128)(2,1)} %get-tuple-element.185.upstream_ref, f32[256,768]{1,0:T(8,128)} %get-tuple-element.186.after_ref, ...), custom_call_target="tpu_custom_call" | custom-call | tf_op jit(solution)/shard_map/cond/branch_1_fun/feed_backward/pallas_call | solution.py:365
  426.7 15.9 %conditional.9 = (bf16[256,768]{1,0:T(8,128)(2,1)}, f32[7,768]{1,0:T(8,128)S(1)}, f32[12,128,128]{2,1,0:T(8,128)}, bf16[1536,768]{1,0:T(8,128)(2,1)}, bf16[1536,768]{1,0:T(8,128)(2,1)}) conditional(s32[]{:T(128)} %convert_element_type.420, (f32[256,768]{1,0:T(8,128)}, f32[2,768]{1,0:T(2,128)S(1)}, f32[3,768]{1,0:T(4,128)S(1)}, ...), branch_computations={%region_10.11_spmd, %region_11.12_spmd} | conditional | flops 207360 | bytes 1219712 | solution.py:911
  426.8 15.6 %attention_backward.5 = (bf16[256,768]{1,0:T(8,128)(2,1)}, bf16[1536,768]{1,0:T(8,128)(2,1)}, bf16[1536,768]{1,0:T(8,128)(2,1)}, f32[1,768]{1,0:T(1,128)S(1)}, f32[12,128,128]{2,1,0:T(8,128)}) custom-call(s32[1]{0:T(128)} %bitcast.3.mine_ref, f32[256,768]{1,0:T(8,128)} %get-tuple-element.202.refs_0_, f32[256,768]{1,0:T(8,128)S(1)} %get-tuple-element.203.refs_1_, ...), custom_call_target="tpu_custom_call" | custom-call | tf_op jit(solution)/shard_map/cond/branch_1_fun/attention_backward/pallas_call | solution.py:559
  457.4 4.9 add_convert_fusion
  468.7 3.0 maximum_select_fusion
  471.7 3.0 add_convert_fusion.1
  483.0 3.0 broadcast_select_fusion.3
  491.9 3.8 multiply_reduce_fusion.2
  495.6 43.0 %collective-permute-done.37 = bf16[1536,768]{1,0:T(8,128)(2,1)} collective-permute-done((bf16[1536,768]{1,0:T(8,128)(2,1)}, bf16[1536,768]{1,0:T(8,128)(2,1)}, u32[]{:S(2)}, u32[]{:S(2)}) %collective-permute-start.37) | collective-permute-done | bytes 2359328 | tf_op jit(solution)/shard_map/ppermute | solution.py:66
  538.6 25.0 %collective-permute-done.33 = bf16[768,768]{1,0:T(8,128)(2,1)} collective-permute-done((bf16[768,768]{1,0:T(8,128)(2,1)}, bf16[768,768]{1,0:T(8,128)(2,1)}, u32[]{:S(2)}, u32[]{:S(2)}) %collective-permute-start.33) | collective-permute-done | bytes 1179680 | tf_op jit(solution)/shard_map/ppermute | solution.py:66
  571.7 10.2 %collective-permute-done.34 = bf16[384,768]{1,0:T(8,128)(2,1)S(1)} collective-permute-done((bf16[384,768]{1,0:T(8,128)(2,1)S(1)}, bf16[384,768]{1,0:T(8,128)(2,1)S(1)}, u32[]{:S(2)}, u32[]{:S(2)}) %collective-permute-start.34) | collective-permute-done | bytes 589856 | tf_op jit(solution)/shard_map/ppermute | solution.py:66
  591.2 21.3 %collective-permute-done.38 = bf16[768,768]{1,0:T(8,128)(2,1)} collective-permute-done((bf16[768,768]{1,0:T(8,128)(2,1)}, bf16[768,768]{1,0:T(8,128)(2,1)}, u32[]{:S(2)}, u32[]{:S(2)}) %collective-permute-start.38) | collective-permute-done | bytes 1179680 | tf_op jit(solution)/shard_map/ppermute | solution.py:66
  612.5 11.2 %add_convert_fusion.4 = bf16[1008,768]{1,0:T(8,128)(2,1)} fusion(f32[2008,768]{1,0:T(8,128)} %fusion.107, s32[]{:T(128)S(6)} %select_n.572, bf16[4096,768]{1,0:T(8,128)(2,1)} %all-gather.9.cloned.1.call-done, s32[4096]{0:T(1024)} %bitcast.451, s32[1008]{0:T(1024)S(1)} %copy-done.61), kind=kOutput, calls=%fused_computation.40 | convolution fusion | flops 6347464704 | bytes 10956740 | tf_op jit(solution)/shard_map/dot_general | solution.py:207
  632.2 24.8 %collective-permute-done.47 = bf16[192,768]{1,0:T(8,128)(2,1)S(1)} collective-permute-done((bf16[192,768]{1,0:T(8,128)(2,1)S(1)}, bf16[192,768]{1,0:T(8,128)(2,1)S(1)}, u32[]{:S(2)}, u32[]{:S(2)}) %collective-permute-start.47) | collective-permute-done | bytes 294944 | tf_op jit(solution)/shard_map/ppermute | solution.py:66
  658.6 9.6 %add_convert_fusion.5 = bf16[1008,768]{1,0:T(8,128)(2,1)} fusion(f32[2008,768]{1,0:T(8,128)} %fusion.107, s32[]{:T(128)S(6)} %select_n.571, bf16[4096,768]{1,0:T(8,128)(2,1)S(1)} %copy-done.67, s32[4096]{0:T(1024)S(1)} %bitcast.452, s32[1008]{0:T(1024)S(1)} %copy-done.60), kind=kOutput, calls=%fused_computation.41 | convolution fusion | flops 6347464704 | bytes 10956740 | tf_op jit(solution)/shard_map/dot_general | solution.py:207
  668.3 11.9 %collective-permute-start.40 = (bf16[1008,768]{1,0:T(8,128)(2,1)}, bf16[1008,768]{1,0:T(8,128)(2,1)}, u32[]{:S(2)}, u32[]{:S(2)}) collective-permute-start(bf16[1008,768]{1,0:T(8,128)(2,1)} %add_convert_fusion.4), channel_id=1, source_target_pairs={{0,1},{1,0},{2,3},{3,2},{4,5},{5,4},{6,7},{7,6},{8,9},{9,8},{10,11... | collective-permute-start | bytes 4644872 | tf_op jit(solution)/shard_map/ppermute | solution.py:70
  703.1 9.4 %collective-permute-start.62 = (f32[1,128]{1,0:T(1,128)S(1)}, f32[1,128]{1,0:T(1,128)S(1)}, u32[]{:S(2)}, u32[]{:S(2)}) collective-permute-start(f32[1,128]{1,0:T(1,128)S(1)} %add.528), channel_id=1, source_target_pairs={{0,1},{1,0},{2,3},{3,2},{4,5},{5,4},{6,7},{7,6},{8,9},{9,8},{10,11... | collective-permute-start | bytes 1544 | tf_op jit(solution)/shard_map/ppermute | solution.py:70
  715.2 3.3 multiply_reduce_fusion
  719.9 7.2 collective-permute-done.57
  727.1 3.0 fusion.41
  730.8 3.5 collective-permute-done.42
  754.4 4.9 multiply_subtract_fusion.1
  767.9 3.7 collective-permute-start.51
  771.6 12.8 %collective-permute-done.46 = bf16[1008,768]{1,0:T(8,128)(2,1)S(1)} collective-permute-done((bf16[1008,768]{1,0:T(8,128)(2,1)S(1)}, bf16[1008,768]{1,0:T(8,128)(2,1)S(1)}, u32[]{:S(2)}, u32[]{:S(2)}) %collective-permute-start.46) | collective-permute-done | bytes 1548320 | tf_op jit(solution)/shard_map/ppermute | solution.py:70
  784.9 11.2 %multiply_subtract_fusion = (f32[2008,768]{1,0:T(8,128)}, f32[2008,768]{1,0:T(8,128)}, f32[2008,768]{1,0:T(8,128)}) fusion(f32[2008,768]{1,0:T(8,128)S(1)} %bitcast.351, f32[]{:T(128)S(6)} %div.98, bf16[1000,768]{1,0:T(8,128)(2,1)S(1)} %slice_select_fusion, bf16[1008,768]{1,0:T(8,128)(2,1)S(1)} %broadcast_select_fusion, f32[2008,768]{1,0:T(8,128)} %param.42, ...), kind=kLoop, calls=%fused_computation.25 | loop fusion | flops 30842880 | bytes 40095748 | tf_op jit(solution)/shard_map/sub | solution.py:584
  796.1 13.8 %collective-permute-done.56 = bf16[4,4,48,768]{3,2,1,0:T(8,128)(2,1)} collective-permute-done((bf16[4,4,48,768]{3,2,1,0:T(8,128)(2,1)}, bf16[4,4,48,768]{3,2,1,0:T(8,128)(2,1)}, u32[]{:S(2)}, u32[]{:S(2)}) %collective-permute-start.56) | collective-permute-done | bytes 1179680 | tf_op jit(solution)/shard_map/ppermute | solution.py:78
  809.9 19.9 %collective-permute-done.51 = bf16[4,4,48,768]{3,2,1,0:T(8,128)(2,1)} collective-permute-done((bf16[4,4,48,768]{3,2,1,0:T(8,128)(2,1)S(1)}, bf16[4,4,48,768]{3,2,1,0:T(8,128)(2,1)}, u32[]{:S(2)}, u32[]{:S(2)}) %collective-permute-start.51) | collective-permute-done | bytes 1179680 | tf_op jit(solution)/shard_map/ppermute | solution.py:70
  (444 shorter events, 227.9 us)
Async XLA Ops:
  7.2 145.9 %all-gather.5.cloned.1.call-start = ((), (), s32[]{:S(2)}) async-start(), calls=%async_computation | async-start | bytes 20054016 | tf_op jit(solution)/shard_map/all_gather | solution.py:715
  12.3 250.9 %all-gather.7.cloned.1.call-start = ((), (), s32[]{:S(2)}) async-start(), calls=%async_computation.1 | async-start | bytes 3342336 | tf_op jit(solution)/shard_map/all_gather | solution.py:796
  13.0 4.6 collective-permute-start
  18.8 3.7 collective-permute-start.2
  22.5 4.1 collective-permute-start.3
  26.6 6.3 collective-permute-start.4
  41.8 6.0 collective-permute-start.5
  42.9 116.3 %collective-permute-start.12 = (bf16[4,2,48,768]{3,2,1,0:T(8,128)(2,1)}, bf16[4,2,48,768]{3,2,1,0:T(8,128)(2,1)}, u32[]{:S(2)}, u32[]{:S(2)}) collective-permute-start(bf16[4,2,48,768]{3,2,1,0:T(8,128)(2,1)} %dynamic-slice_bitcast_fusion.10), channel_id=1, source_target_pairs={{0,2},{1,3},{2,0},{3,1},{4,6},{5,7},{6,4},{7,5},{8,10},{9,11},{10,... | collective-permute-start | bytes 1769480 | tf_op jit(solution)/shard_map/ppermute | solution.py:66
  59.1 37.3 %collective-permute-start.6 = (bf16[512,768]{1,0:T(8,128)(2,1)}, bf16[512,768]{1,0:T(8,128)(2,1)}, u32[]{:S(2)}, u32[]{:S(2)}) collective-permute-start(bf16[512,768]{1,0:T(8,128)(2,1)} %bitcast.31), channel_id=1, source_target_pairs={{0,4},{1,5},{2,6},{3,7},{4,0},{5,1},{6,2},{7,3},{8,12},{9,13},{10,... | collective-permute-start | bytes 2359304 | tf_op jit(solution)/shard_map/ppermute | solution.py:66
  62.8 37.3 %collective-permute-start.9 = (bf16[512,768]{1,0:T(8,128)(2,1)}, bf16[512,768]{1,0:T(8,128)(2,1)}, u32[]{:S(2)}, u32[]{:S(2)}) collective-permute-start(bf16[512,768]{1,0:T(8,128)(2,1)} %bitcast.40), channel_id=1, source_target_pairs={{0,8},{1,9},{2,10},{3,11},{4,12},{5,13},{6,14},{7,15},{8,0},{9,1},... | collective-permute-start | bytes 2359304 | tf_op jit(solution)/shard_map/ppermute | solution.py:66
  97.8 28.5 %collective-permute-start.7 = (bf16[256,768]{1,0:T(8,128)(2,1)S(1)}, bf16[256,768]{1,0:T(8,128)(2,1)}, u32[]{:S(2)}, u32[]{:S(2)}) collective-permute-start(bf16[256,768]{1,0:T(8,128)(2,1)S(1)} %bitcast.427), channel_id=1, source_target_pairs={{0,8},{1,9},{2,10},{3,11},{4,12},{5,13},{6,14},{7,15},{8,0},{9,1},... | collective-permute-start | bytes 1179656 | tf_op jit(solution)/shard_map/ppermute | solution.py:66
  101.5 31.6 %collective-permute-start.10 = (bf16[256,768]{1,0:T(8,128)(2,1)S(1)}, bf16[256,768]{1,0:T(8,128)(2,1)S(1)}, u32[]{:S(2)}, u32[]{:S(2)}) collective-permute-start(bf16[256,768]{1,0:T(8,128)(2,1)S(1)} %dynamic-slice_bitcast_fusion.11), channel_id=1, source_target_pairs={{0,16},{1,17},{2,18},{3,19},{4,20},{5,21},{6,22},{7,23},{8,24},{9,... | collective-permute-start | bytes 1179656 | tf_op jit(solution)/shard_map/ppermute | solution.py:66
  127.5 19.1 %collective-permute-start.8 = (bf16[128,768]{1,0:T(8,128)(2,1)S(1)}, bf16[128,768]{1,0:T(8,128)(2,1)S(1)}, u32[]{:S(2)}, u32[]{:S(2)}) collective-permute-start(bf16[128,768]{1,0:T(8,128)(2,1)S(1)} %dynamic-slice_bitcast_fusion.16), channel_id=1, source_target_pairs={{0,16},{1,17},{2,18},{3,19},{4,20},{5,21},{6,22},{7,23},{8,24},{9,... | collective-permute-start | bytes 589832 | tf_op jit(solution)/shard_map/ppermute | solution.py:66
  133.2 10.9 %collective-permute-start.11 = (bf16[128,768]{1,0:T(8,128)(2,1)S(1)}, bf16[128,768]{1,0:T(8,128)(2,1)S(1)}, u32[]{:S(2)}, u32[]{:S(2)}) collective-permute-start(bf16[128,768]{1,0:T(8,128)(2,1)S(1)} %dynamic-slice_bitcast_fusion.15), channel_id=1, source_target_pairs={{0,4},{1,5},{2,6},{3,7},{4,0},{5,1},{6,2},{7,3},{8,12},{9,13},{10,... | collective-permute-start | bytes 589832 | tf_op jit(solution)/shard_map/ppermute | solution.py:66
  161.8 15.8 %collective-permute-start.13 = (bf16[4,2,48,768]{3,2,1,0:T(8,128)(2,1)}, bf16[4,2,48,768]{3,2,1,0:T(8,128)(2,1)}, u32[]{:S(2)}, u32[]{:S(2)}) collective-permute-start(bf16[4,2,48,768]{3,2,1,0:T(8,128)(2,1)} %get-tuple-element.581), channel_id=1, source_target_pairs={{0,4},{1,5},{2,6},{3,7},{4,0},{5,1},{6,2},{7,3},{8,12},{9,13},{10,... | collective-permute-start | bytes 1769480 | tf_op jit(solution)/shard_map/ppermute | solution.py:66
  181.5 28.4 %collective-permute-start.15 = (bf16[2,192,768]{2,1,0:T(8,128)(2,1)}, bf16[2,192,768]{2,1,0:T(8,128)(2,1)}, u32[]{:S(2)}, u32[]{:S(2)}) collective-permute-start(bf16[2,192,768]{2,1,0:T(8,128)(2,1)} %get-tuple-element.579), channel_id=1, source_target_pairs={{0,16},{1,17},{2,18},{3,19},{4,20},{5,21},{6,22},{7,23},{8,24},{9,... | collective-permute-start | bytes 1769480 | tf_op jit(solution)/shard_map/ppermute | solution.py:66
  183.9 11.4 %collective-permute-start.14 = (bf16[256,768]{1,0:T(8,128)(2,1)}, bf16[256,768]{1,0:T(8,128)(2,1)S(1)}, u32[]{:S(2)}, u32[]{:S(2)}) collective-permute-start(bf16[256,768]{1,0:T(8,128)(2,1)} %get-tuple-element.367), channel_id=1, source_target_pairs={{0,1},{2,3},{4,5},{6,7},{8,9},{10,11},{12,13},{14,15},{16,17},{18,... | collective-permute-start | bytes 1179656 | tf_op jit(solution)/shard_map/ppermute | solution.py:74
  209.9 8.7 %collective-permute-start.16 = (bf16[128,768]{1,0:T(8,128)(2,1)S(1)}, bf16[128,768]{1,0:T(8,128)(2,1)S(1)}, u32[]{:S(2)}, u32[]{:S(2)}) collective-permute-start(bf16[128,768]{1,0:T(8,128)(2,1)S(1)} %slice.151), channel_id=1, source_target_pairs={{1,0},{3,2},{5,4},{7,6},{9,8},{11,10},{13,12},{15,14},{17,16},{19,... | collective-permute-start | bytes 589832 | tf_op jit(solution)/shard_map/ppermute | solution.py:78
  219.4 393.1 %all-gather.9.cloned.1.call-start = ((), (), s32[]{:S(2)}) async-start(), calls=%async_computation.2 | async-start | bytes 6684672 | tf_op jit(solution)/shard_map/all_gather | solution.py:928
  278.4 1.2 collective-permute-start.17
  279.8 3.8 collective-permute-start.18
  283.6 3.8 collective-permute-start.19
  287.5 4.7 collective-permute-start.20
  304.1 3.5 collective-permute-start.21
  308.1 19.6 %collective-permute-start.22 = (bf16[512,768]{1,0:T(8,128)(2,1)S(1)}, bf16[512,768]{1,0:T(8,128)(2,1)S(1)}, u32[]{:S(2)}, u32[]{:S(2)}) collective-permute-start(bf16[512,768]{1,0:T(8,128)(2,1)S(1)} %bitcast.416), channel_id=1, source_target_pairs={{0,4},{1,5},{2,6},{3,7},{4,0},{5,1},{6,2},{7,3},{8,12},{9,13},{10,... | collective-permute-start | bytes 2359304 | tf_op jit(solution)/shard_map/ppermute | solution.py:66
  328.1 10.5 %collective-permute-start.23 = (bf16[256,768]{1,0:T(8,128)(2,1)S(1)}, bf16[256,768]{1,0:T(8,128)(2,1)S(1)}, u32[]{:S(2)}, u32[]{:S(2)}) collective-permute-start(bf16[256,768]{1,0:T(8,128)(2,1)S(1)} %bitcast.428), channel_id=1, source_target_pairs={{0,8},{1,9},{2,10},{3,11},{4,12},{5,13},{6,14},{7,15},{8,0},{9,1},... | collective-permute-start | bytes 1179656 | tf_op jit(solution)/shard_map/ppermute | solution.py:66
  338.8 10.5 %collective-permute-start.24 = (bf16[128,768]{1,0:T(8,128)(2,1)S(1)}, bf16[128,768]{1,0:T(8,128)(2,1)S(1)}, u32[]{:S(2)}, u32[]{:S(2)}) collective-permute-start(bf16[128,768]{1,0:T(8,128)(2,1)S(1)} %dynamic-slice_bitcast_fusion.14), channel_id=1, source_target_pairs={{0,16},{1,17},{2,18},{3,19},{4,20},{5,21},{6,22},{7,23},{8,24},{9,... | collective-permute-start | bytes 589832 | tf_op jit(solution)/shard_map/ppermute | solution.py:66
  349.4 6.6 collective-permute-start.25
  356.0 41.1 %collective-permute-start.27 = (bf16[2,2,192,768]{3,2,1,0:T(8,128)(2,1)}, bf16[2,2,192,768]{3,2,1,0:T(8,128)(2,1)}, u32[]{:S(2)}, u32[]{:S(2)}) collective-permute-start(bf16[2,2,192,768]{3,2,1,0:T(8,128)(2,1)} %maximum_select_fusion.4), channel_id=1, source_target_pairs={{0,8},{1,9},{2,10},{3,11},{4,12},{5,13},{6,14},{7,15},{8,0},{9,1},... | collective-permute-start | bytes 3538952 | tf_op jit(solution)/shard_map/ppermute | solution.py:66
  366.4 30.8 %collective-permute-start.26 = (bf16[256,768]{1,0:T(8,128)(2,1)}, bf16[256,768]{1,0:T(8,128)(2,1)S(1)}, u32[]{:S(2)}, u32[]{:S(2)}) collective-permute-start(bf16[256,768]{1,0:T(8,128)(2,1)} %get-tuple-element.385), channel_id=1, source_target_pairs={{1,0},{3,2},{5,4},{7,6},{9,8},{11,10},{13,12},{15,14},{17,16},{19,... | collective-permute-start | bytes 1179656 | tf_op jit(solution)/shard_map/ppermute | solution.py:78
  401.4 20.9 %collective-permute-start.29 = (bf16[768,768]{1,0:T(8,128)(2,1)}, bf16[768,768]{1,0:T(8,128)(2,1)}, u32[]{:S(2)}, u32[]{:S(2)}) collective-permute-start(bf16[768,768]{1,0:T(8,128)(2,1)} %dynamic-slice_bitcast_fusion.1), channel_id=1, source_target_pairs={{1,5},{3,7},{5,1},{7,3},{9,13},{11,15},{13,9},{15,11},{17,21},{19,... | collective-permute-start | bytes 3538952 | tf_op jit(solution)/shard_map/ppermute | solution.py:66
  422.3 20.4 %collective-permute-start.31 = (bf16[2,1536,768]{2,1,0:T(8,128)(2,1)}, bf16[2,1536,768]{2,1,0:T(8,128)(2,1)}, u32[]{:S(2)}, u32[]{:S(2)}) collective-permute-start(bf16[2,1536,768]{2,1,0:T(8,128)(2,1)} %get-tuple-element.424), channel_id=1, source_target_pairs={{0,2},{1,3},{2,0},{3,1},{4,6},{5,7},{6,4},{7,5},{8,10},{9,11},{10,... | collective-permute-start | bytes 14155784 | tf_op jit(solution)/shard_map/ppermute | solution.py:66
  425.2 17.5 %collective-permute-start.30 = (bf16[384,768]{1,0:T(8,128)(2,1)}, bf16[384,768]{1,0:T(8,128)(2,1)}, u32[]{:S(2)}, u32[]{:S(2)}) collective-permute-start(bf16[384,768]{1,0:T(8,128)(2,1)} %bitcast.94), channel_id=1, source_target_pairs={{1,9},{3,11},{5,13},{7,15},{9,1},{11,3},{13,5},{15,7},{17,25},{19,... | collective-permute-start | bytes 1769480 | tf_op jit(solution)/shard_map/ppermute | solution.py:66
  452.4 19.3 %collective-permute-start.32 = (bf16[1536,768]{1,0:T(8,128)(2,1)}, bf16[1536,768]{1,0:T(8,128)(2,1)}, u32[]{:S(2)}, u32[]{:S(2)}) collective-permute-start(bf16[1536,768]{1,0:T(8,128)(2,1)} %get-tuple-element.426), channel_id=1, source_target_pairs={{0,2},{1,3},{2,0},{3,1},{4,6},{5,7},{6,4},{7,5},{8,10},{9,11},{10,... | collective-permute-start | bytes 7077896 | tf_op jit(solution)/shard_map/ppermute | solution.py:66
  456.7 7.9 collective-permute-start.36
  464.1 74.6 %collective-permute-start.37 = (bf16[1536,768]{1,0:T(8,128)(2,1)}, bf16[1536,768]{1,0:T(8,128)(2,1)}, u32[]{:S(2)}, u32[]{:S(2)}) collective-permute-start(bf16[1536,768]{1,0:T(8,128)(2,1)} %bitcast.114), channel_id=1, source_target_pairs={{0,4},{1,5},{2,6},{3,7},{4,0},{5,1},{6,2},{7,3},{8,12},{9,13},{10,... | collective-permute-start | bytes 7077896 | tf_op jit(solution)/shard_map/ppermute | solution.py:66
  465.4 6.3 collective-permute-start.52
  475.9 87.7 %collective-permute-start.33 = (bf16[768,768]{1,0:T(8,128)(2,1)}, bf16[768,768]{1,0:T(8,128)(2,1)}, u32[]{:S(2)}, u32[]{:S(2)}) collective-permute-start(bf16[768,768]{1,0:T(8,128)(2,1)} %dynamic-slice_bitcast_fusion), channel_id=1, source_target_pairs={{0,4},{1,5},{2,6},{3,7},{4,0},{5,1},{6,2},{7,3},{8,12},{9,13},{10,... | collective-permute-start | bytes 3538952 | tf_op jit(solution)/shard_map/ppermute | solution.py:66
  478.3 12.3 %collective-permute-start.53 = (bf16[2,192,768]{2,1,0:T(8,128)(2,1)}, bf16[2,192,768]{2,1,0:T(8,128)(2,1)S(1)}, u32[]{:S(2)}, u32[]{:S(2)}) collective-permute-start(bf16[2,192,768]{2,1,0:T(8,128)(2,1)} %maximum_select_fusion.14), channel_id=1, source_target_pairs={{1,9},{3,11},{5,13},{7,15},{9,1},{11,3},{13,5},{15,7},{17,25},{19,... | collective-permute-start | bytes 1769480 | tf_op jit(solution)/shard_map/ppermute | solution.py:66
  565.6 16.3 %collective-permute-start.34 = (bf16[384,768]{1,0:T(8,128)(2,1)S(1)}, bf16[384,768]{1,0:T(8,128)(2,1)S(1)}, u32[]{:S(2)}, u32[]{:S(2)}) collective-permute-start(bf16[384,768]{1,0:T(8,128)(2,1)S(1)} %bitcast.421), channel_id=1, source_target_pairs={{0,8},{1,9},{2,10},{3,11},{4,12},{5,13},{6,14},{7,15},{8,0},{9,1},... | collective-permute-start | bytes 1769480 | tf_op jit(solution)/shard_map/ppermute | solution.py:66
  570.6 41.9 %collective-permute-start.38 = (bf16[768,768]{1,0:T(8,128)(2,1)}, bf16[768,768]{1,0:T(8,128)(2,1)}, u32[]{:S(2)}, u32[]{:S(2)}) collective-permute-start(bf16[768,768]{1,0:T(8,128)(2,1)} %bitcast.117), channel_id=1, source_target_pairs={{0,8},{1,9},{2,10},{3,11},{4,12},{5,13},{6,14},{7,15},{8,0},{9,1},... | collective-permute-start | bytes 3538952 | tf_op jit(solution)/shard_map/ppermute | solution.py:66
  582.9 29.6 %collective-permute-start.35 = (bf16[192,768]{1,0:T(8,128)(2,1)}, bf16[192,768]{1,0:T(8,128)(2,1)}, u32[]{:S(2)}, u32[]{:S(2)}) collective-permute-start(bf16[192,768]{1,0:T(8,128)(2,1)} %dynamic-slice_bitcast_fusion.13), channel_id=1, source_target_pairs={{0,16},{1,17},{2,18},{3,19},{4,20},{5,21},{6,22},{7,23},{8,24},{9,... | collective-permute-start | bytes 884744 | tf_op jit(solution)/shard_map/ppermute | solution.py:66
  589.3 79.0 %collective-permute-start.54 = (bf16[4,2,48,768]{3,2,1,0:T(8,128)(2,1)}, bf16[4,2,48,768]{3,2,1,0:T(8,128)(2,1)}, u32[]{:S(2)}, u32[]{:S(2)}) collective-permute-start(bf16[4,2,48,768]{3,2,1,0:T(8,128)(2,1)} %get-tuple-element.450), channel_id=1, source_target_pairs={{1,3},{3,1},{5,7},{7,5},{9,11},{11,9},{13,15},{15,13},{17,19},{19,... | collective-permute-start | bytes 1769480 | tf_op jit(solution)/shard_map/ppermute | solution.py:66
  627.3 29.7 %collective-permute-start.47 = (bf16[192,768]{1,0:T(8,128)(2,1)S(1)}, bf16[192,768]{1,0:T(8,128)(2,1)S(1)}, u32[]{:S(2)}, u32[]{:S(2)}) collective-permute-start(bf16[192,768]{1,0:T(8,128)(2,1)S(1)} %get-tuple-element.442), channel_id=1, source_target_pairs={{0,16},{1,17},{2,18},{3,19},{4,20},{5,21},{6,22},{7,23},{8,24},{9,... | collective-permute-start | bytes 884744 | tf_op jit(solution)/shard_map/ppermute | solution.py:66
  631.5 48.7 %collective-permute-start.39 = (bf16[384,768]{1,0:T(8,128)(2,1)S(1)}, bf16[384,768]{1,0:T(8,128)(2,1)S(1)}, u32[]{:S(2)}, u32[]{:S(2)}) collective-permute-start(bf16[384,768]{1,0:T(8,128)(2,1)S(1)} %bitcast.420), channel_id=1, source_target_pairs={{0,16},{1,17},{2,18},{3,19},{4,20},{5,21},{6,22},{7,23},{8,24},{9,... | collective-permute-start | bytes 1769480 | tf_op jit(solution)/shard_map/ppermute | solution.py:66
  658.6 26.0 %collective-permute-start.48 = (bf16[2,192,768]{2,1,0:T(8,128)(2,1)}, bf16[2,192,768]{2,1,0:T(8,128)(2,1)S(1)}, u32[]{:S(2)}, u32[]{:S(2)}) collective-permute-start(bf16[2,192,768]{2,1,0:T(8,128)(2,1)} %maximum_select_fusion.12), channel_id=1, source_target_pairs={{0,8},{1,9},{2,10},{3,11},{4,12},{5,13},{6,14},{7,15},{8,0},{9,1},... | collective-permute-start | bytes 1769480 | tf_op jit(solution)/shard_map/ppermute | solution.py:66
  668.3 46.9 %collective-permute-start.40 = (bf16[1008,768]{1,0:T(8,128)(2,1)}, bf16[1008,768]{1,0:T(8,128)(2,1)}, u32[]{:S(2)}, u32[]{:S(2)}) collective-permute-start(bf16[1008,768]{1,0:T(8,128)(2,1)} %add_convert_fusion.4), channel_id=1, source_target_pairs={{0,1},{1,0},{2,3},{3,2},{4,5},{5,4},{6,7},{7,6},{8,9},{9,8},{10,11... | collective-permute-start | bytes 4644872 | tf_op jit(solution)/shard_map/ppermute | solution.py:70
  681.2 46.0 %collective-permute-start.57 = (bf16[2,192,768]{2,1,0:T(8,128)(2,1)S(1)}, bf16[2,192,768]{2,1,0:T(8,128)(2,1)}, u32[]{:S(2)}, u32[]{:S(2)}) collective-permute-start(bf16[2,192,768]{2,1,0:T(8,128)(2,1)S(1)} %bitcast.394), channel_id=1, source_target_pairs={{0,1},{1,0},{2,3},{3,2},{4,5},{5,4},{6,7},{7,6},{8,9},{9,8},{10,11... | collective-permute-start | bytes 1769480 | tf_op jit(solution)/shard_map/ppermute | solution.py:70
  690.3 1.2 collective-permute-start.58
  691.5 3.5 collective-permute-start.59
  695.1 3.5 collective-permute-start.60
  698.6 4.4 collective-permute-start.61
  701.3 29.5 %collective-permute-start.49 = (bf16[4,2,48,768]{3,2,1,0:T(8,128)(2,1)}, bf16[4,2,48,768]{3,2,1,0:T(8,128)(2,1)}, u32[]{:S(2)}, u32[]{:S(2)}) collective-permute-start(bf16[4,2,48,768]{3,2,1,0:T(8,128)(2,1)} %get-tuple-element.445), channel_id=1, source_target_pairs={{0,2},{1,3},{2,0},{3,1},{4,6},{5,7},{6,4},{7,5},{8,10},{9,11},{10,... | collective-permute-start | bytes 1769480 | tf_op jit(solution)/shard_map/ppermute | solution.py:66
  703.1 27.0 %collective-permute-start.62 = (f32[1,128]{1,0:T(1,128)S(1)}, f32[1,128]{1,0:T(1,128)S(1)}, u32[]{:S(2)}, u32[]{:S(2)}) collective-permute-start(f32[1,128]{1,0:T(1,128)S(1)} %add.528), channel_id=1, source_target_pairs={{0,1},{1,0},{2,3},{3,2},{4,5},{5,4},{6,7},{7,6},{8,9},{9,8},{10,11... | collective-permute-start | bytes 1544 | tf_op jit(solution)/shard_map/ppermute | solution.py:70
  719.8 10.3 %collective-permute-start.41 = (f32[9,768]{1,0:T(8,128)S(1)}, f32[9,768]{1,0:T(8,128)S(1)}, u32[]{:S(2)}, u32[]{:S(2)}) collective-permute-start(f32[9,768]{1,0:T(8,128)S(1)} %pad_maximum_fusion.10), channel_id=1, source_target_pairs={{0,2},{1,3},{2,0},{3,1},{4,6},{5,7},{6,4},{7,5},{8,10},{9,11},{10,... | collective-permute-start | bytes 82952 | tf_op jit(solution)/shard_map/ppermute | solution.py:66
  730.1 4.2 collective-permute-start.42
  734.3 4.2 collective-permute-start.43
  738.4 5.0 collective-permute-start.44
  740.7 21.7 %collective-permute-start.55 = (bf16[4,2,48,768]{3,2,1,0:T(8,128)(2,1)}, bf16[4,2,48,768]{3,2,1,0:T(8,128)(2,1)}, u32[]{:S(2)}, u32[]{:S(2)}) collective-permute-start(bf16[4,2,48,768]{3,2,1,0:T(8,128)(2,1)} %get-tuple-element.452), channel_id=1, source_target_pairs={{1,5},{3,7},{5,1},{7,3},{9,13},{11,15},{13,9},{15,11},{17,21},{19,... | collective-permute-start | bytes 1769480 | tf_op jit(solution)/shard_map/ppermute | solution.py:66
  743.5 4.7 collective-permute-start.45
  746.4 20.0 %collective-permute-start.50 = (bf16[4,2,48,768]{3,2,1,0:T(8,128)(2,1)}, bf16[4,2,48,768]{3,2,1,0:T(8,128)(2,1)}, u32[]{:S(2)}, u32[]{:S(2)}) collective-permute-start(bf16[4,2,48,768]{3,2,1,0:T(8,128)(2,1)} %get-tuple-element.446), channel_id=1, source_target_pairs={{0,4},{1,5},{2,6},{3,7},{4,0},{5,1},{6,2},{7,3},{8,12},{9,13},{10,... | collective-permute-start | bytes 1769480 | tf_op jit(solution)/shard_map/ppermute | solution.py:66
  747.7 36.8 %collective-permute-start.46 = (bf16[1008,768]{1,0:T(8,128)(2,1)S(1)}, bf16[1008,768]{1,0:T(8,128)(2,1)S(1)}, u32[]{:S(2)}, u32[]{:S(2)}) collective-permute-start(bf16[1008,768]{1,0:T(8,128)(2,1)S(1)} %get-tuple-element.530), channel_id=1, source_target_pairs={{0,1},{1,0},{2,3},{3,2},{4,5},{5,4},{6,7},{7,6},{8,9},{9,8},{10,11... | collective-permute-start | bytes 4644872 | tf_op jit(solution)/shard_map/ppermute | solution.py:70
  765.1 44.8 %collective-permute-start.56 = (bf16[4,4,48,768]{3,2,1,0:T(8,128)(2,1)}, bf16[4,4,48,768]{3,2,1,0:T(8,128)(2,1)}, u32[]{:S(2)}, u32[]{:S(2)}) collective-permute-start(bf16[4,4,48,768]{3,2,1,0:T(8,128)(2,1)} %bitcast.168), channel_id=1, source_target_pairs={{1,0},{3,2},{5,4},{7,6},{9,8},{11,10},{13,12},{15,14},{17,16},{19,... | collective-permute-start | bytes 3538952 | tf_op jit(solution)/shard_map/ppermute | solution.py:78
  767.9 61.8 %collective-permute-start.51 = (bf16[4,4,48,768]{3,2,1,0:T(8,128)(2,1)S(1)}, bf16[4,4,48,768]{3,2,1,0:T(8,128)(2,1)}, u32[]{:S(2)}, u32[]{:S(2)}) collective-permute-start(bf16[4,4,48,768]{3,2,1,0:T(8,128)(2,1)S(1)} %bitcast.365), channel_id=1, source_target_pairs={{0,1},{1,0},{2,3},{3,2},{4,5},{5,4},{6,7},{7,6},{8,9},{9,8},{10,11... | collective-permute-start | bytes 3538952 | tf_op jit(solution)/shard_map/ppermute | solution.py:70
  (72 other events, 936.1 us)
Sparse Core Ops, SparseCore 0:
  12.4 140.6 all-gather.4
  219.6 43.5 all-gather.6
  442.8 101.0 all-gather.8
